TPU v7x, 32 devices: a whole 2x2x4 slice. The times are simulated.
32 devices in a mesh: dp: 8 (over y, x, core), fsdp: 4 (over z).
Axes of the slice: x: 2, y: 2, z: 4, core: 2. Of those that a mesh axis runs over, the one named last changes fastest.
Arguments:
- tokens: bfloat16 [28672, 1408], P(('dp', 'fsdp')), may hold values from -8 to 8
- qkv_weight: bfloat16 [1408, 4224], P('fsdp'), may hold values from -1 to 1
- image_lengths: int32 [8, 4, 2, 2], P(None, 'fsdp'), may hold values from 1 to 320, 448 in all within a row
- balance: int32 [8, 4, 2], P(None, 'fsdp'), may hold values from 0 to 1, each once within a row
Outputs:
- attended: bfloat16 [28672, 1408], P(('dp', 'fsdp'))
Inputs may be any that keep to these rules, and one draw needn't show every extreme that they name: `image_lengths`: the 2 lengths of a bundle sum to 448, and none exceeds 320. For each device, balance lists each of its bundles once over the routes.
All inputs are finite; a program needn't handle non-finite values.
Results may differ from a plain program's by a relative error of at most 0.0069.
Values may be sent and summed in bfloat16 or wider, within the bound.
No kernel may reach another device: no remote copies, remote signals or barrier semaphores. Data moves between devices by JAX's collectives and lax.ppermute only.
A program may use at most 128 MiB of HBM per device.

v0:
```python
import math

import jax
import jax.numpy as jnp
from jax import lax
from jax.sharding import PartitionSpec as P

HEADS = 16


def passed_along(x, axis, by):
    length = lax.axis_size(axis)
    return lax.ppermute(x, axis, [(i, (i + by) % length) for i in range(length)])


def attend_bundle(projected, image_tag, model_width):
    row_count = projected.shape[0]
    head_dim = model_width // HEADS
    score_scale = 1.0 / math.sqrt(head_dim)
    shaped = projected.reshape(row_count, 3, HEADS, head_dim)
    queries = shaped[:, 0]
    key_rows = shaped[:, 1]
    values = shaped[:, 2]
    scores = (
        jnp.einsum("qhd,khd->hqk", queries, key_rows, preferred_element_type=jnp.float32)
        * score_scale
    )
    allowed = (image_tag[:, None] == image_tag[None, :])[None]
    masked = jnp.where(allowed, scores, -1e30)
    row_max = jnp.max(masked, axis=-1, keepdims=True)
    raised = jnp.where(allowed, jnp.exp(masked - row_max), 0.0)
    weights = (raised / jnp.sum(raised, axis=-1, keepdims=True)).astype(jnp.bfloat16)
    attended = jnp.einsum("hqk,khd->qhd", weights, values, preferred_element_type=jnp.float32)
    return attended.reshape(row_count, model_width).astype(jnp.bfloat16)


def on_device(tokens, qkv_weight, image_lengths, balance):
    peer_count = lax.axis_size("dp")
    half_count = peer_count // 2
    own_rank = lax.axis_index("dp")
    row_count, model_width = tokens.shape
    bundle_rows = row_count // 2
    routes_column = balance[:, 0]
    lengths_column = image_lengths[:, 0]
    own_routes = lax.dynamic_index_in_dim(routes_column, own_rank, 0, keepdims=False)
    positions = jnp.arange(bundle_rows, dtype=jnp.int32)

    def arrival_tag(source, route):
        chosen = lax.dynamic_index_in_dim(routes_column, source, 0, keepdims=False)[route]
        per_source = lax.dynamic_index_in_dim(lengths_column, source, 0, keepdims=False)
        first_end = jnp.where(chosen == 0, per_source[0, 0], per_source[1, 0])
        return (positions >= first_end).astype(jnp.int32) + 4 * route

    near_tag = arrival_tag((own_rank - 1) % peer_count, 0)
    far_tag = arrival_tag((own_rank - half_count) % peer_count, 1)
    summed = jnp.dot(
        tokens,
        lax.all_gather(qkv_weight, "fsdp", axis=0, tiled=True),
        preferred_element_type=jnp.float32,
    )
    source_rows = summed.astype(jnp.bfloat16)
    bundled = source_rows.reshape(2, bundle_rows, source_rows.shape[1])
    first_near = own_routes[0] == 0
    near_rows = jnp.where(first_near, bundled[0], bundled[1])
    far_rows = jnp.where(first_near, bundled[1], bundled[0])
    near_rows, far_rows = (near_rows, far_rows)
    near_proj = passed_along(near_rows, "dp", 1)
    far_proj = passed_along(far_rows, "dp", half_count)
    near_out = attend_bundle(near_proj, near_tag, model_width)
    far_out = attend_bundle(far_proj, far_tag, model_width)
    return jnp.concatenate([near_out, far_out], axis=0)


def solution(mesh):
    in_specs = (
        P(("dp", "fsdp"), None),
        P("fsdp", None),
        P(None, "fsdp", None, None),
        P(None, "fsdp", None),
    )
    out_specs = P(("dp", "fsdp"), None)
    return jax.shard_map(
        on_device, mesh=mesh, in_specs=in_specs, out_specs=out_specs, check_vma=False
    )
```

profile of v0, /device:TPU:0, one launch (start us, length us, event | category | flops | bytes accessed | tf_op | source)
XLA Modules:
  0.0 415.5 jit_solution(17542876429373692237)
XLA Ops:
  6.5 0.0 copy-start
  6.5 0.0 all-gather.2.cloned.1.call-start
  6.5 0.7 all-gather.2.cloned.1.call-update
  7.3 0.9 constant_dynamic-slice_fusion.1
  8.2 0.5 slice.52
  9.3 209.3 %all-gather.2.cloned.1.call-done = bf16[1408,4224]{1,0:T(8,128)(2,1)} async-done(((bf16[352,4224]{1,0:T(8,128)(2,1)}), bf16[1408,4224]{1,0:T(8,128)(2,1)}) %all-gather.2.cloned.1.call-update) | async-done | bytes 11894800 | tf_op jit(solution)/shard_map/all_gather | solution.py:58
  218.6 0.0 copy-done
  218.6 15.2 %convolution_convert_fusion = bf16[896,4224]{1,0:T(8,128)(2,1)S(1)} fusion(bf16[896,1408]{1,0:T(8,128)(2,1)S(1)} %copy-done, bf16[1408,4224]{1,0:T(8,128)(2,1)} %all-gather.2.cloned.1.call-done), kind=kOutput, calls=%fused_computation.10 | convolution fusion | flops 10661511168 | bytes 21987328 | tf_op jit(solution)/shard_map/dot_general | solution.py:56
  233.9 0.0 copy-start.2
  233.9 3.4 broadcast_select_fusion.1
  237.3 0.1 collective-permute-start
  237.3 0.5 slice.56
  238.5 0.5 slice.62
  239.7 0.0 copy-done.2
  239.7 0.2 dynamic-slice_reduce_fusion.1
  239.9 0.6 fusion.21
  243.1 0.2 broadcast_compare_fusion.1
  243.3 0.2 broadcast_compare_fusion
  243.5 1.5 collective-permute-start.1
  245.0 37.2 %collective-permute-done = bf16[448,4224]{1,0:T(8,128)(2,1)} collective-permute-done((bf16[448,4224]{1,0:T(8,128)(2,1)}, bf16[448,4224]{1,0:T(8,128)(2,1)}, u32[]{:S(2)}, u32[]{:S(2)}) %collective-permute-start) | collective-permute-done | bytes 3784736 | tf_op jit(solution)/shard_map/ppermute | solution.py:13
  282.2 6.5 %copy.15 = bf16[448,4224]{0,1:T(8,128)(2,1)} copy(bf16[448,4224]{1,0:T(8,128)(2,1)} %collective-permute-done) | data formatting | bytes 7569408 | tf_op jit(solution)/shard_map/ppermute | solution.py:13
  288.6 9.1 %fusion.15 = f32[16,448,448]{1,2,0:T(8,128)} fusion(bf16[448,3,16,88]{0,3,2,1:T(8,128)(2,1)} %bitcast.35), kind=kOutput, calls=%fused_computation.29 | convolution fusion | flops 565182464 | bytes 15728640 | tf_op jit(solution)/shard_map/qhd,khd->hqk/dot_general | solution.py:25
  297.7 16.0 %fusion.24 = (f32[16,448]{1,0:T(8,128)S(1)}, f32[16,448,448]{1,2,0:T(8,128)}) fusion(f32[16,448,448]{1,2,0:T(8,128)} %fusion.15, pred[448,448]{0,1:T(8,128)(4,1)S(1)} %broadcast_compare_fusion.1), kind=kOutput, calls=%fused_computation.50 | output fusion | flops 22479296 | bytes 25919488 | tf_op jit(solution)/shard_map/sub | solution.py:31
  313.7 7.0 %fusion.13 = bf16[16,88,448]{2,1,0:T(8,128)(2,1)S(1)} fusion(f32[16,448,448]{1,2,0:T(8,128)} %get-tuple-element.19, f32[16,448]{1,0:T(8,128)S(1)} %get-tuple-element.18, bf16[448,3,16,88]{0,3,2,1:T(8,128)(2,1)} %bitcast.36), kind=kOutput, calls=%fused_computation.23 | convolution fusion | flops 572235776 | bytes 17412096 | tf_op jit(solution)/shard_map/hqk,khd->qhd/dot_general | solution.py:33
  320.7 1.6 copy.19
  322.3 40.8 %collective-permute-done.1 = bf16[448,4224]{1,0:T(8,128)(2,1)} collective-permute-done((bf16[448,4224]{1,0:T(8,128)(2,1)}, bf16[448,4224]{1,0:T(8,128)(2,1)}, u32[]{:S(2)}, u32[]{:S(2)}) %collective-permute-start.1) | collective-permute-done | bytes 3784736 | tf_op jit(solution)/shard_map/ppermute | solution.py:13
  363.1 6.5 %copy.17 = bf16[448,4224]{0,1:T(8,128)(2,1)} copy(bf16[448,4224]{1,0:T(8,128)(2,1)} %collective-permute-done.1) | data formatting | bytes 7569408 | tf_op jit(solution)/shard_map/ppermute | solution.py:13
  369.6 9.1 %fusion.14 = f32[16,448,448]{1,2,0:T(8,128)} fusion(bf16[448,3,16,88]{0,3,2,1:T(8,128)(2,1)} %bitcast.37), kind=kOutput, calls=%fused_computation.25 | convolution fusion | flops 565182464 | bytes 15728640 | tf_op jit(solution)/shard_map/qhd,khd->hqk/dot_general | solution.py:25
  378.7 16.0 %fusion.23 = (f32[16,448]{1,0:T(8,128)S(1)}, f32[16,448,448]{1,2,0:T(8,128)}) fusion(f32[16,448,448]{1,2,0:T(8,128)} %fusion.14, pred[448,448]{0,1:T(8,128)(4,1)S(1)} %broadcast_compare_fusion), kind=kOutput, calls=%fused_computation.49 | output fusion | flops 22479296 | bytes 25919488 | tf_op jit(solution)/shard_map/sub | solution.py:31
  394.7 0.0 copy-start.1
  394.7 8.2 %fusion.12 = bf16[16,88,448]{2,1,0:T(8,128)(2,1)} fusion(f32[16,448,448]{1,2,0:T(8,128)} %get-tuple-element.17, f32[16,448]{1,0:T(8,128)S(1)} %get-tuple-element.16, bf16[448,3,16,88]{0,3,2,1:T(8,128)(2,1)} %bitcast.38), kind=kOutput, calls=%fused_computation.22 | convolution fusion | flops 572235776 | bytes 17412096 | tf_op jit(solution)/shard_map/hqk,khd->qhd/dot_general | solution.py:33
  402.9 2.5 copy.20
  405.3 3.3 pad_maximum_fusion
  408.6 0.0 copy-done.1
  (2 shorter events, 0.0 us)
Async XLA Ops:
  6.5 212.1 %copy-start = (bf16[896,1408]{1,0:T(8,128)(2,1)S(1)}, bf16[896,1408]{1,0:T(8,128)(2,1)}, u32[]{:S(2)}) copy-start(bf16[896,1408]{1,0:T(8,128)(2,1)} %param.4) | copy-start | bytes 7569412
  6.5 212.1 %all-gather.2.cloned.1.call-start = ((), (), s32[]{:S(2)}) async-start(), calls=%async_computation | async-start | bytes 14868480 | tf_op jit(solution)/shard_map/all_gather | solution.py:58
  233.9 5.8 %copy-start.2 = (s32[8,1,2,2]{0,3,2,1:T(2,128)S(1)}, s32[8,1,2,2]{0,3,2,1:T(2,128)}, u32[]{:S(2)}) copy-start(s32[8,1,2,2]{0,3,2,1:T(2,128)} %param.6) | copy-start | bytes 388
  237.3 44.9 %collective-permute-start = (bf16[448,4224]{1,0:T(8,128)(2,1)}, bf16[448,4224]{1,0:T(8,128)(2,1)}, u32[]{:S(2)}, u32[]{:S(2)}) collective-permute-start(bf16[448,4224]{1,0:T(8,128)(2,1)} %get-tuple-element.7), channel_id=1, source_target_pairs={{0,4},{4,8},{8,12},{12,16},{16,20},{20,24},{24,28},{28,0},{1,5},{5... | collective-permute-start | bytes 11354120 | tf_op jit(solution)/shard_map/ppermute | solution.py:13
  243.5 119.6 %collective-permute-start.1 = (bf16[448,4224]{1,0:T(8,128)(2,1)}, bf16[448,4224]{1,0:T(8,128)(2,1)}, u32[]{:S(2)}, u32[]{:S(2)}) collective-permute-start(bf16[448,4224]{1,0:T(8,128)(2,1)} %get-tuple-element.8), channel_id=1, source_target_pairs={{0,16},{4,20},{8,24},{12,28},{16,0},{20,4},{24,8},{28,12},{1,17},{... | collective-permute-start | bytes 11354120 | tf_op jit(solution)/shard_map/ppermute | solution.py:13
  394.7 14.0 %copy-start.1 = (bf16[896,1408]{1,0:T(8,128)(2,1)S(1)}, bf16[896,1408]{1,0:T(8,128)(2,1)}, u32[]{:S(2)}) copy-start(bf16[896,1408]{1,0:T(8,128)(2,1)} %param.4) | copy-start | bytes 7569412
Sparse Core Ops, SparseCore 0:
  8.9 209.6 all-gather.1
where the time goes:
time: 416 us; the launch traced here: 415 us
  waiting for transfers between devices  288 us (69%)
  matrix products  48.6 us (12%)
  other arithmetic  39.2 us (9%)
  local copies, waits for them, and re-layouts  20.2 us (5%)
  between operations  18 us (4%)
    all_gather x1, waiting for transfers between devices, on_device(): lax.all_gather(qkv_weight, 'fsdp', axis=0, tiled=True)  209 us
    ppermute x2, waiting for transfers between devices, passed_along(): lax.ppermute(x, axis, [(i, (i + by) % length) for i in range(length)])  78 us
    sub x2, other arithmetic, attend_bundle(): raised = jnp.where(allowed, jnp.exp(masked - row_max), 0.0)  32 us
    dot_general x2, matrix products, attend_bundle(): jnp.einsum('qhd,khd->hqk', queries, key_rows, preferred_element_type=jnp....  18.2 us
    dot_general x1, matrix products, on_device(): jnp.dot(tokens, lax.all_gather(qkv_weight, 'fsdp', axis=0, tiled=True), p...  15.2 us
    dot_general x2, matrix products, attend_bundle(): jnp.einsum('hqk,khd->qhd', weights, values, preferred_element_type=jnp.fl...  15.1 us
    ppermute x2, local copies, waits for them, and re-layouts, passed_along(): lax.ppermute(x, axis, [(i, (i + by) % length) for i in range(length)])  12.9 us
  transfers between devices with their start and end apart: 3, of which 3 were waited for; matrix products, arithmetic and copies ran while one was open for 11% of the time, Pallas kernels for 0%

commit v1 on v0

v1 whole, which is shorter than its diff:
```python
import math, functools

import jax
import jax.numpy as jnp
import numpy as np
from jax import lax
from jax.experimental import pallas as pl
from jax.experimental.pallas import tpu as pltpu
from jax.sharding import PartitionSpec as P

HEADS=16
LANE=128
BIG=-1e30

def attend_kernel(t0, t1, h0, h1, hd, bundle, *refs):
    first = t0 == 0
    if first:
        x_ref, w_ref, split_ref, o_hbm, kc_out, oc_out, proj, oscr, sem = refs
        kc_in = oc_in = None
    else:
        x_ref, w_ref, split_ref, kc_in, oc_in, o_in, o_hbm, kc_out, oc_out, proj, oscr, sem = refs
    rows = x_ref.shape[0]
    nt = t1 - t0
    base = t0 - 1
    width = (nt + 1) * LANE
    for part in range(3):
        p = jnp.dot(x_ref[...], w_ref[:, part*nt*LANE:(part+1)*nt*LANE], preferred_element_type=jnp.float32)
        proj[part, :, LANE:] = p.astype(jnp.bfloat16)
        if not first:
            proj[part, :, :LANE] = kc_in[:, part*LANE:(part+1)*LANE]
        kc_out[:, part*LANE:(part+1)*LANE] = proj[part, :, nt*LANE:]
    split = split_ref[0]
    c = math.log2(math.e) / math.sqrt(hd)
    partial = None if first else oc_in[...]
    def tags(w, at, values):
        row = lax.broadcasted_iota(jnp.int32, (rows, w), 0)
        lane = lax.broadcasted_iota(jnp.int32, (rows, w), 1)
        late = row >= split
        a, b = values
        one = jnp.where(late, b, a); two = jnp.where(late, a, b)
        return jnp.where(lane == at, one, jnp.where(lane == at + 1, two, 0.0)).astype(jnp.bfloat16)
    made = {}
    def get(w, at, values):
        if (w, at, values) not in made: made[(w, at, values)] = tags(w, at, values)
        return made[(w, at, values)]
    emitted = []
    for h in range(h0, h1):
        lo, hi = h*hd, (h+1)*hd
        s0, s1 = lo // LANE, -(-hi // LANE)
        w = (s1 - s0) * LANE
        a, b = lo - s0*LANE, hi - s0*LANE
        at = 0 if a >= 2 else w - 2
        ones_at = at
        lane = lax.broadcasted_iota(jnp.int32, (rows, w), 1)
        own = (lane >= a) & (lane < b)
        cols = slice((s0-base)*LANE, (s1-base)*LANE)
        q = jnp.where(own, proj[0, :, cols], get(w, at, (1.0, 0.0)))
        k = jnp.where(own, proj[1, :, cols], get(w, at, (0.0, BIG)))
        v = jnp.where(own, proj[2, :, cols], jnp.where(lane == ones_at, 1.0, 0.0).astype(jnp.bfloat16))
        s = lax.dot_general(q, k, (((1,), (1,)), ((), ())), preferred_element_type=jnp.float32)
        m = jnp.max(s, axis=1, keepdims=True) * c
        e = jnp.exp2(s * c - m).astype(jnp.bfloat16)
        o = jnp.dot(e, v, preferred_element_type=jnp.float32)
        o = (o / o[:, ones_at:ones_at+1]).astype(jnp.bfloat16)
        for t in range(s0, s1):
            piece = o[:, (t-s0)*LANE:(t-s0+1)*LANE]
            start = max(lo - t*LANE, 0)
            if start > 0:
                ln = lax.broadcasted_iota(jnp.int32, (rows, LANE), 1)
                piece = jnp.where(ln < start, partial, piece)
            if hi >= (t+1)*LANE:
                emitted.append(t)
                oscr[:, (t-emitted[0])*LANE:(t-emitted[0]+1)*LANE] = piece
                partial = None
            else:
                partial = piece
    n = len(emitted)
    if partial is not None: oc_out[...] = partial
    else: oc_out[...] = jnp.zeros_like(oc_out)
    cp = pltpu.make_async_copy(oscr, o_hbm.at[pl.ds(bundle*rows, rows), pl.ds(emitted[0]*LANE, n*LANE)], sem)
    cp.start(); cp.wait()

def attend(t0, t1, h0, h1, bundle, x, w, split, carry, out):
    rows, d = x.shape
    hd = d // HEADS
    first = t0 == 0
    nt = t1 - t0
    e0 = (h0*hd) // LANE
    e1 = (h1*hd) // LANE
    V = pl.BlockSpec(memory_space=pltpu.VMEM)
    A = pl.BlockSpec(memory_space=pl.ANY)
    S = pl.BlockSpec(memory_space=pltpu.SMEM)
    ins = [x, w, split]; specs=[V, V, S]
    if not first:
        ins += [*carry]; specs += [V, V]
    alias = {}
    if out is not None:
        ins.append(out); specs.append(A); alias={len(ins)-1: 0}
    body = functools.partial(attend_kernel, t0, t1, h0, h1, hd, bundle)
    if first and out is not None:
        inner = body
        body = lambda x, w, s, o_in, *rest: inner(x, w, s, *rest)
    res = pl.pallas_call(body,
        out_shape=[jax.ShapeDtypeStruct((2*rows, d), jnp.bfloat16), jax.ShapeDtypeStruct((rows, 3*LANE), jnp.bfloat16), jax.ShapeDtypeStruct((rows, LANE), jnp.bfloat16)],
        in_specs=specs, out_specs=[A, V, V],
        scratch_shapes=[pltpu.VMEM((3, rows, (nt+1)*LANE), jnp.bfloat16), pltpu.VMEM((rows, (e1-e0)*LANE), jnp.bfloat16), pltpu.SemaphoreType.DMA],
        input_output_aliases=alias,
        compiler_params=pltpu.CompilerParams(vmem_limit_bytes=40*2**20),
        name=f"attend_{t0}_{bundle}",
    )(*ins)
    return res[0], (res[1], res[2])

def ready_heads(bounds, hd):
    out=[]; h=0
    for t0,t1 in bounds:
        e=min(HEADS, t1*LANE//hd)
        out.append((h,e)); h=e
    return out


BOUNDS = ((0, 3), (3, 6), (6, 9), (9, 11))
SWAPS = (2, 2, 2, 4)
PIECES = 4


def relative_order(shard_rows, shards, halves):
    quarter = shard_rows // PIECES
    step, flip, row = [], [], []
    for j in (0, 2, 1, 3):
        for start, size in halves:
            for s in range(1, shards):
                step += [s] * size
                flip += [j] * size
                row += list(range(start, start + size))
    return np.array(step), np.array(flip), np.array(row)


def quarter_of(rank):
    return ((((rank >> 2) ^ (rank >> 1)) & 1) << 1) | (rank & 1)


def source_columns(rank, column, shard_rows, shards, halves):
    step, flip, row = relative_order(shard_rows, shards, halves)
    rest = ((column - step) % shards) * shard_rows + (quarter_of(rank) ^ flip) * (shard_rows // PIECES) + row
    own = column * shard_rows + np.arange(shard_rows)
    return jnp.concatenate([own, rest]).astype(jnp.int32)


def reordered(x, columns):
    place = (jnp.arange(x.shape[1], dtype=jnp.int32)[:, None] == columns[None, :]).astype(jnp.bfloat16)
    return jnp.dot(x, place, preferred_element_type=jnp.float32).astype(jnp.bfloat16)


def shifted(x, axis, by):
    n = lax.axis_size(axis)
    return lax.ppermute(x, axis, [(i, (i + by) % n) for i in range(n)])


def swapped(x, mask):
    n = lax.axis_size("dp")
    return lax.ppermute(x, "dp", [(i, i ^ mask) for i in range(n)])


def after(x, y):
    return lax.optimization_barrier((x, y))[0]


def on_device(tokens, qkv_weight, image_lengths, balance):
    ranks = lax.axis_size("dp")
    shards = lax.axis_size("fsdp")
    rank = lax.axis_index("dp")
    column = lax.axis_index("fsdp")
    rows, width = tokens.shape
    bundle_rows = rows // 2
    shard_rows = qkv_weight.shape[0]
    quarter = shard_rows // PIECES
    first = (quarter // 2 + 7) // 8 * 8
    halves = ((0, first), (first, quarter - first))
    hd = width // HEADS

    routes = balance[:, 0]
    lengths = image_lengths[:, 0]

    def first_end(source, route):
        return lengths[source, routes[source, route], 0]

    near_split = first_end((rank - 1) % ranks, 0)
    far_split = first_end((rank - ranks // 2) % ranks, 1)
    splits = (near_split.reshape(1), far_split.reshape(1))

    own_first = routes[rank, 0] == 0
    low, high = tokens[:bundle_rows], tokens[bundle_rows:]
    near = jnp.where(own_first, low, high)
    far = jnp.where(own_first, high, low)
    near_to = (rank + 1) % ranks
    far_to = (rank + ranks // 2) % ranks
    order = functools.partial(source_columns, column=column, shard_rows=shard_rows, shards=shards, halves=halves)
    near = shifted(reordered(near, order(near_to)), "dp", 1)
    far = shifted(reordered(far, order(far_to)), "dp", ranks // 2)

    mine = lax.dynamic_slice_in_dim(qkv_weight, quarter_of(rank) * quarter, quarter, 0)

    def of_chunk(w, t0, t1):
        return jnp.concatenate([w[:, p * width + t0 * LANE : p * width + t1 * LANE] for p in range(3)], axis=1)

    weights = []
    last = [None, None]
    for (t0, t1), mask in zip(BOUNDS, SWAPS):
        payload = of_chunk(mine, t0, t1)
        got = []
        for i, (start, size) in enumerate(halves):
            part = payload[start : start + size]
            if last[i] is not None:
                part = after(part, last[i])
            for _ in range(1, shards):
                part = shifted(part, "fsdp", 1)
                got.append(part)
            last[i] = part
        straight = jnp.concatenate(got, axis=0)
        across = swapped(straight, mask)
        both = jnp.concatenate([straight, across], axis=0)
        other = swapped(both, 1)
        weights.append(jnp.concatenate([of_chunk(qkv_weight, t0, t1), both, other], axis=0))

    out = None
    carry = [None, None]
    for (t0, t1), (h0, h1), w in zip(BOUNDS, ready_heads(BOUNDS, hd), weights):
        for b, x in enumerate((near, far)):
            out, carry[b] = attend(t0, t1, h0, h1, b, x, w, splits[b], carry[b], out)
    return out


def solution(mesh):
    in_specs = (
        P(("dp", "fsdp"), None),
        P("fsdp", None),
        P(None, "fsdp", None, None),
        P(None, "fsdp", None),
    )
    return jax.shard_map(
        on_device, mesh=mesh, in_specs=in_specs, out_specs=P(("dp", "fsdp"), None), check_vma=False
    )
```

time: 416 us -> 203 us (0.49)
  waiting for transfers between devices: 288 us -> 72.9 us
  Pallas kernels: 0 us -> 56.1 us
  matrix products: 48.6 us -> 8.64 us
  other arithmetic: 39.2 us -> 6.97 us
  local copies, waits for them, and re-layouts: 20.2 us -> 38.1 us
  starting transfers between devices: 1.59 us -> 14.7 us
  between operations: 18 us -> 4.95 us
    all_gather x1 -> x0, waiting for transfers between devices: 209 us -> none  [on_device(): lax.all_gather(qkv_weight, 'fsdp', axis=0, tiled=True)]
    pallas_call x0 -> x8, Pallas kernels: none -> 56.1 us  [attend(): pl.pallas_call(body, out_shape=[jax.ShapeDtypeStruct((2 * rows, d), jnp.b...]
    dot_general x5 -> x2, matrix products: 48.6 us -> 8.64 us  [reordered(): jnp.dot(x, place, preferred_element_type=jnp.float32).astype(jnp.bfloat16)]
    sub x2 -> x0, other arithmetic: 32 us -> none  [attend_bundle(): raised = jnp.where(allowed, jnp.exp(masked - row_max), 0.0)]
    unnamed x6 -> x60, local copies, waits for them, and re-layouts: 0.01 us -> 18.5 us
    ppermute x2 -> x34, starting transfers between devices: 1.59 us -> 14.7 us  [the longest x26 7.39 us: shifted(): return lax.ppermute(x, axis, [(i, (i + by) % n) for i in range(n)])]
    ppermute x2 -> x0, local copies, waits for them, and re-layouts: 12.9 us -> none  [passed_along(): lax.ppermute(x, axis, [(i, (i + by) % length) for i in range(length)])]
    concatenate x0 -> x8, local copies, waits for them, and re-layouts: none -> 12.3 us  [the longest x4 8.21 us: on_device(): jnp.concatenate([of_chunk(qkv_weight, t0, t1), both, other], axis=0)]
  transfers between devices with their start and end apart: 3 -> 34, of which waited for: 3 -> 21; matrix products, arithmetic and copies ran while one was open for 11% -> 24% of each run, Pallas kernels for 0% -> 14%
where the time goes in v1:
time: 203 us; the launch traced here: 202 us
  waiting for transfers between devices  72.9 us (36%)
  Pallas kernels  56.1 us (28%)
  local copies, waits for them, and re-layouts  38.1 us (19%)
  starting transfers between devices  14.7 us (7%)
  matrix products  8.64 us (4%)
  other arithmetic  6.97 us (3%)
  between operations  4.95 us (2%)
    ppermute x26, waiting for transfers between devices, shifted(): return lax.ppermute(x, axis, [(i, (i + by) % n) for i in range(n)])  67.1 us
    pallas_call x8, Pallas kernels, attend(): pl.pallas_call(body, out_shape=[jax.ShapeDtypeStruct((2 * rows, d), jnp.b...  56.1 us
    unnamed x60, local copies, waits for them, and re-layouts  18.5 us
    dot_general x2, matrix products, reordered(): jnp.dot(x, place, preferred_element_type=jnp.float32).astype(jnp.bfloat16)  8.64 us
    concatenate x4, local copies, waits for them, and re-layouts, on_device(): jnp.concatenate([of_chunk(qkv_weight, t0, t1), both, other], axis=0)  8.21 us
    ppermute x26, starting transfers between devices, shifted(): return lax.ppermute(x, axis, [(i, (i + by) % n) for i in range(n)])  7.39 us
    ppermute x8, starting transfers between devices, swapped(): return lax.ppermute(x, 'dp', [(i, i ^ mask) for i in range(n)])  7.29 us
    ppermute x8, waiting for transfers between devices, swapped(): return lax.ppermute(x, 'dp', [(i, i ^ mask) for i in range(n)])  5.77 us
  transfers between devices with their start and end apart: 34, of which 21 were waited for; matrix products, arithmetic and copies ran while one was open for 24% of the time, Pallas kernels for 14%

profile of v1, /device:TPU:0, one launch (start us, length us, event | category | flops | bytes accessed | tf_op | source)
XLA Modules:
  0.0 202.4 jit_solution(17961693021727849056)
XLA Ops:
  0.0 1.9 constant_dynamic-slice_fusion
  2.6 3.0 %collective-permute-start.1 = (bf16[48,1152]{1,0:T(8,128)(2,1)}, bf16[48,1152]{1,0:T(8,128)(2,1)}, u32[]{:S(2)}, u32[]{:S(2)}) collective-permute-start(bf16[48,1152]{1,0:T(8,128)(2,1)} %slice.139), channel_id=1, source_target_pairs={{0,1},{1,2},{2,3},{3,0},{4,5},{5,6},{6,7},{7,4},{8,9},{9,10},{10,1... | collective-permute-start | bytes 331784 | tf_op jit(solution)/shard_map/ppermute | solution.py:156
  6.3 1.6 collective-permute-start.13
  9.3 5.2 %fusion.4 = bf16[448,1408]{1,0:T(8,128)(2,1)} fusion(s32[1408]{0:T(1024)S(1)} %get-tuple-element.165, pred[]{:T(512)} %bitcast, bf16[896,1408]{1,0:T(8,128)(2,1)} %param.12), kind=kOutput, calls=%fused_computation.6 | convolution fusion | flops 1779531776 | bytes 3790337 | tf_op jit(solution)/shard_map/dot_general | solution.py:151
  19.4 2.1 %maximum_dynamic-update-slice_fusion.2 = bf16[1408,1152]{1,0:T(8,128)(2,1)} fusion(bf16[352,384]{1,0:T(8,128)(2,1)S(1)} %get-tuple-element.64, bf16[352,384]{1,0:T(8,128)(2,1)} %get-tuple-element.65, bf16[352,384]{1,0:T(8,128)(2,1)S(1)} %get-tuple-element.57), kind=kLoop, calls=%fused_computation.18 | loop fusion | flops 2433023 | bytes 1622016
  21.5 1.0 maximum_dynamic-update-slice_fusion.1
  24.3 1.6 collective-permute-start.14
  26.0 1.6 constant_dynamic-update-slice_fusion.75
  27.6 3.7 %collective-permute-done.14 = bf16[40,1152]{1,0:T(8,128)(2,1)S(1)} collective-permute-done((bf16[40,1152]{1,0:T(8,128)(2,1)}, bf16[40,1152]{1,0:T(8,128)(2,1)S(1)}, u32[]{:S(2)}, u32[]{:S(2)}) %collective-permute-start.14) | collective-permute-done | bytes 92192 | tf_op jit(solution)/shard_map/ppermute | solution.py:156
  31.3 2.5 %collective-permute-done.2 = bf16[48,1152]{1,0:T(8,128)(2,1)S(1)} collective-permute-done((bf16[48,1152]{1,0:T(8,128)(2,1)}, bf16[48,1152]{1,0:T(8,128)(2,1)S(1)}, u32[]{:S(2)}, u32[]{:S(2)}) %collective-permute-start.2) | collective-permute-done | bytes 110624 | tf_op jit(solution)/shard_map/ppermute | solution.py:156
  34.5 4.0 %collective-permute-done.15 = bf16[40,1152]{1,0:T(8,128)(2,1)S(1)} collective-permute-done((bf16[40,1152]{1,0:T(8,128)(2,1)S(1)}, bf16[40,1152]{1,0:T(8,128)(2,1)S(1)}, u32[]{:S(2)}, u32[]{:S(2)}) %collective-permute-start.15) | collective-permute-done | bytes 92192 | tf_op jit(solution)/shard_map/ppermute | solution.py:156
  38.6 2.5 %collective-permute-done.3 = bf16[48,1152]{1,0:T(8,128)(2,1)S(1)} collective-permute-done((bf16[48,1152]{1,0:T(8,128)(2,1)S(1)}, bf16[48,1152]{1,0:T(8,128)(2,1)S(1)}, u32[]{:S(2)}, u32[]{:S(2)}) %collective-permute-start.3) | collective-permute-done | bytes 110624 | tf_op jit(solution)/shard_map/ppermute | solution.py:156
  41.7 1.6 constant_dynamic-update-slice_fusion.72
  43.9 1.2 collective-permute-done.16
  45.8 1.5 collective-permute-start.31
  48.6 3.9 %collective-permute-done.17 = bf16[40,1152]{1,0:T(8,128)(2,1)S(1)} collective-permute-done((bf16[40,1152]{1,0:T(8,128)(2,1)S(1)}, bf16[40,1152]{1,0:T(8,128)(2,1)S(1)}, u32[]{:S(2)}, u32[]{:S(2)}) %collective-permute-start.17) | collective-permute-done | bytes 92192 | tf_op jit(solution)/shard_map/ppermute | solution.py:156
  53.2 1.2 collective-permute-done.5
  54.3 4.8 %collective-permute-done.18 = bf16[40,1152]{1,0:T(8,128)(2,1)S(1)} collective-permute-done((bf16[40,1152]{1,0:T(8,128)(2,1)S(1)}, bf16[40,1152]{1,0:T(8,128)(2,1)S(1)}, u32[]{:S(2)}, u32[]{:S(2)}) %collective-permute-start.18) | collective-permute-done | bytes 92192 | tf_op jit(solution)/shard_map/ppermute | solution.py:156
  59.8 5.6 %collective-permute-done.19 = bf16[40,1152]{1,0:T(8,128)(2,1)S(1)} collective-permute-done((bf16[40,1152]{1,0:T(8,128)(2,1)S(1)}, bf16[40,1152]{1,0:T(8,128)(2,1)S(1)}, u32[]{:S(2)}, u32[]{:S(2)}) %collective-permute-start.19) | collective-permute-done | bytes 92192 | tf_op jit(solution)/shard_map/ppermute | solution.py:156
  68.3 1.6 collective-permute-start.29
  69.9 2.9 %collective-permute-done.20 = bf16[40,1152]{1,0:T(8,128)(2,1)S(1)} collective-permute-done((bf16[40,1152]{1,0:T(8,128)(2,1)S(1)}, bf16[40,1152]{1,0:T(8,128)(2,1)S(1)}, u32[]{:S(2)}, u32[]{:S(2)}) %collective-permute-start.20) | collective-permute-done | bytes 92192 | tf_op jit(solution)/shard_map/ppermute | solution.py:156
  72.8 2.3 %collective-permute-done.7 = bf16[48,1152]{1,0:T(8,128)(2,1)S(1)} collective-permute-done((bf16[48,1152]{1,0:T(8,128)(2,1)S(1)}, bf16[48,1152]{1,0:T(8,128)(2,1)S(1)}, u32[]{:S(2)}, u32[]{:S(2)}) %collective-permute-start.7) | collective-permute-done | bytes 110624 | tf_op jit(solution)/shard_map/ppermute | solution.py:156
  75.8 3.3 %collective-permute-done.21 = bf16[40,1152]{1,0:T(8,128)(2,1)S(1)} collective-permute-done((bf16[40,1152]{1,0:T(8,128)(2,1)S(1)}, bf16[40,1152]{1,0:T(8,128)(2,1)S(1)}, u32[]{:S(2)}, u32[]{:S(2)}) %collective-permute-start.21) | collective-permute-done | bytes 92192 | tf_op jit(solution)/shard_map/ppermute | solution.py:156
  79.2 2.7 %collective-permute-done.8 = bf16[48,1152]{1,0:T(8,128)(2,1)S(1)} collective-permute-done((bf16[48,1152]{1,0:T(8,128)(2,1)S(1)}, bf16[48,1152]{1,0:T(8,128)(2,1)S(1)}, u32[]{:S(2)}, u32[]{:S(2)}) %collective-permute-start.8) | collective-permute-done | bytes 110624 | tf_op jit(solution)/shard_map/ppermute | solution.py:156
  82.6 2.6 %collective-permute-done.22 = bf16[40,768]{1,0:T(8,128)(2,1)S(1)} collective-permute-done((bf16[40,768]{1,0:T(8,128)(2,1)S(1)}, bf16[40,768]{1,0:T(8,128)(2,1)S(1)}, u32[]{:S(2)}, u32[]{:S(2)}) %collective-permute-start.22) | collective-permute-done | bytes 61472 | tf_op jit(solution)/shard_map/ppermute | solution.py:156
  86.1 5.1 %collective-permute-done.23 = bf16[40,768]{1,0:T(8,128)(2,1)S(1)} collective-permute-done((bf16[40,768]{1,0:T(8,128)(2,1)S(1)}, bf16[40,768]{1,0:T(8,128)(2,1)S(1)}, u32[]{:S(2)}, u32[]{:S(2)}) %collective-permute-start.23) | collective-permute-done | bytes 61472 | tf_op jit(solution)/shard_map/ppermute | solution.py:156
  94.0 4.8 %collective-permute-done.10 = bf16[48,768]{1,0:T(8,128)(2,1)S(1)} collective-permute-done((bf16[48,768]{1,0:T(8,128)(2,1)S(1)}, bf16[48,768]{1,0:T(8,128)(2,1)S(1)}, u32[]{:S(2)}, u32[]{:S(2)}) %collective-permute-start.10) | collective-permute-done | bytes 73760 | tf_op jit(solution)/shard_map/ppermute | solution.py:156
  99.5 5.4 %collective-permute-done.11 = bf16[48,768]{1,0:T(8,128)(2,1)S(1)} collective-permute-done((bf16[48,768]{1,0:T(8,128)(2,1)S(1)}, bf16[48,768]{1,0:T(8,128)(2,1)S(1)}, u32[]{:S(2)}, u32[]{:S(2)}) %collective-permute-start.11) | collective-permute-done | bytes 73760 | tf_op jit(solution)/shard_map/ppermute | solution.py:156
  105.6 5.5 %collective-permute-done.12 = bf16[48,768]{1,0:T(8,128)(2,1)S(1)} collective-permute-done((bf16[48,768]{1,0:T(8,128)(2,1)S(1)}, bf16[48,768]{1,0:T(8,128)(2,1)S(1)}, u32[]{:S(2)}, u32[]{:S(2)}) %collective-permute-start.12) | collective-permute-done | bytes 73760 | tf_op jit(solution)/shard_map/ppermute | solution.py:156
  111.1 1.6 collective-permute-start.27
  115.3 2.2 %collective-permute-start.25 = (bf16[264,768]{1,0:T(8,128)(2,1)S(1)}, bf16[264,768]{1,0:T(8,128)(2,1)S(1)}, u32[]{:S(2)}, u32[]{:S(2)}) collective-permute-start(bf16[264,768]{1,0:T(8,128)(2,1)S(1)} %get-tuple-element.154), channel_id=1, source_target_pairs={{0,16},{4,20},{8,24},{12,28},{16,0},{20,4},{24,8},{28,12},{1,17},{... | collective-permute-start | bytes 1216520 | tf_op jit(solution)/shard_map/ppermute | solution.py:161
  117.5 3.4 %fusion.5 = bf16[448,1408]{1,0:T(8,128)(2,1)} fusion(s32[1408]{0:T(1024)S(1)} %get-tuple-element.166, pred[]{:T(512)} %bitcast, bf16[896,1408]{1,0:T(8,128)(2,1)S(1)} %copy-done.17), kind=kOutput, calls=%fused_computation.7 | convolution fusion | flops 1779531776 | bytes 3790337 | tf_op jit(solution)/shard_map/dot_general | solution.py:151
  120.9 1.1 constant_dynamic-update-slice_fusion.48
  122.0 5.8 %collective-permute-done.25 = bf16[264,768]{1,0:T(8,128)(2,1)S(1)} collective-permute-done((bf16[264,768]{1,0:T(8,128)(2,1)S(1)}, bf16[264,768]{1,0:T(8,128)(2,1)S(1)}, u32[]{:S(2)}, u32[]{:S(2)}) %collective-permute-start.25) | collective-permute-done | bytes 405536 | tf_op jit(solution)/shard_map/ppermute | solution.py:161
  129.3 1.1 constant_dynamic-update-slice_fusion.27
  134.9 2.4 %constant_dynamic-update-slice_fusion.76.refs_1_.w = bf16[1408,1152]{1,0:T(8,128)(2,1)} fusion(bf16[1408,1152]{1,0:T(8,128)(2,1)} %get-tuple-element.82, bf16[528,1152]{1,0:T(8,128)(2,1)} %collective-permute-done.32), kind=kLoop, calls=%fused_computation.99 | loop fusion | bytes 2433024 | tf_op jit(solution)/shard_map/concatenate | solution.py:223
  137.3 6.8 %attend_0_0.1 = (bf16[896,1408]{1,0:T(8,128)(2,1)}, bf16[448,384]{1,0:T(8,128)(2,1)S(1)}, bf16[448,128]{1,0:T(8,128)(2,1)S(1)}) custom-call(bf16[448,1408]{1,0:T(8,128)(2,1)S(1)} %collective-permute-done.33.refs_0_, bf16[1408,1152]{1,0:T(8,128)(2,1)} %constant_dynamic-update-slice_fusion.76.refs_1_.w, s32[1]{0:T(128)} %bitcast.4.refs_2_), custom_call_target="tpu_custom_call" | custom-call | tf_op jit(solution)/shard_map/attend_0_0/pallas_call | solution.py:103
  144.1 2.8 %collective-permute-done.x.refs_0_ = bf16[448,1408]{1,0:T(8,128)(2,1)S(1)} collective-permute-done((bf16[448,1408]{1,0:T(8,128)(2,1)}, bf16[448,1408]{1,0:T(8,128)(2,1)S(1)}, u32[]{:S(2)}, u32[]{:S(2)}) %collective-permute-start) | collective-permute-done | bytes 1261600 | tf_op jit(solution)/shard_map/ppermute | solution.py:156
  147.0 6.9 %attend_0_1.1 = (bf16[896,1408]{1,0:T(8,128)(2,1)}, bf16[448,384]{1,0:T(8,128)(2,1)S(1)}, bf16[448,128]{1,0:T(8,128)(2,1)S(1)}) custom-call(bf16[448,1408]{1,0:T(8,128)(2,1)S(1)} %collective-permute-done.x.refs_0_, bf16[1408,1152]{1,0:T(8,128)(2,1)} %constant_dynamic-update-slice_fusion.76.refs_1_.w, ...), custom_call_target="tpu_custom_call", output_to_operand_aliasing={{0}: (3, {})} | custom-call | tf_op jit(solution)/shard_map/attend_0_1/pallas_call | solution.py:103
  153.9 1.0 constant_dynamic-update-slice_fusion.13.refs_1_
  154.9 2.4 %constant_dynamic-update-slice_fusion.55.refs_1_ = bf16[1408,1152]{1,0:T(8,128)(2,1)} fusion(bf16[1408,1152]{1,0:T(8,128)(2,1)} %get-tuple-element.84, bf16[528,1152]{1,0:T(8,128)(2,1)} %collective-permute-done.30), kind=kLoop, calls=%fused_computation.78 | loop fusion | bytes 2433024 | tf_op jit(solution)/shard_map/concatenate | solution.py:223
  157.3 7.3 %attend_3_0.1 = (bf16[896,1408]{1,0:T(8,128)(2,1)}, bf16[448,384]{1,0:T(8,128)(2,1)S(1)}, bf16[448,128]{1,0:T(8,128)(2,1)S(1)}) custom-call(bf16[448,1408]{1,0:T(8,128)(2,1)S(1)} %collective-permute-done.33.refs_0_, bf16[1408,1152]{1,0:T(8,128)(2,1)} %constant_dynamic-update-slice_fusion.55.refs_1_, ...), custom_call_target="tpu_custom_call", output_to_operand_aliasing={{0}: (5, {})} | custom-call | tf_op jit(solution)/shard_map/attend_3_0/pallas_call | solution.py:103
  164.6 7.2 %attend_3_1.1 = (bf16[896,1408]{1,0:T(8,128)(2,1)}, bf16[448,384]{1,0:T(8,128)(2,1)S(1)}, bf16[448,128]{1,0:T(8,128)(2,1)S(1)}) custom-call(bf16[448,1408]{1,0:T(8,128)(2,1)S(1)} %collective-permute-done.x.refs_0_, bf16[1408,1152]{1,0:T(8,128)(2,1)} %constant_dynamic-update-slice_fusion.55.refs_1_, ...), custom_call_target="tpu_custom_call", output_to_operand_aliasing={{0}: (5, {})} | custom-call | tf_op jit(solution)/shard_map/attend_3_1/pallas_call | solution.py:103
  171.8 2.4 %constant_dynamic-update-slice_fusion.34.refs_1_ = bf16[1408,1152]{1,0:T(8,128)(2,1)} fusion(bf16[1408,1152]{1,0:T(8,128)(2,1)} %get-tuple-element.86, bf16[528,1152]{1,0:T(8,128)(2,1)} %collective-permute-done.28), kind=kLoop, calls=%fused_computation.57 | loop fusion | bytes 2433024 | tf_op jit(solution)/shard_map/concatenate | solution.py:223
  174.2 7.2 %attend_6_0.1 = (bf16[896,1408]{1,0:T(8,128)(2,1)}, bf16[448,384]{1,0:T(8,128)(2,1)S(1)}, bf16[448,128]{1,0:T(8,128)(2,1)S(1)}) custom-call(bf16[448,1408]{1,0:T(8,128)(2,1)S(1)} %collective-permute-done.33.refs_0_, bf16[1408,1152]{1,0:T(8,128)(2,1)} %constant_dynamic-update-slice_fusion.34.refs_1_, ...), custom_call_target="tpu_custom_call", output_to_operand_aliasing={{0}: (5, {})} | custom-call | tf_op jit(solution)/shard_map/attend_6_0/pallas_call | solution.py:103
  181.4 7.3 %attend_6_1.1 = (bf16[896,1408]{1,0:T(8,128)(2,1)}, bf16[448,384]{1,0:T(8,128)(2,1)S(1)}, bf16[448,128]{1,0:T(8,128)(2,1)S(1)}) custom-call(bf16[448,1408]{1,0:T(8,128)(2,1)S(1)} %collective-permute-done.x.refs_0_, bf16[1408,1152]{1,0:T(8,128)(2,1)} %constant_dynamic-update-slice_fusion.34.refs_1_, ...), custom_call_target="tpu_custom_call", output_to_operand_aliasing={{0}: (5, {})} | custom-call | tf_op jit(solution)/shard_map/attend_6_1/pallas_call | solution.py:103
  188.7 6.8 %attend_9_0.1 = (bf16[896,1408]{1,0:T(8,128)(2,1)}, bf16[448,384]{1,0:T(8,128)(2,1)}, bf16[448,128]{1,0:T(8,128)(2,1)}) custom-call(bf16[448,1408]{1,0:T(8,128)(2,1)S(1)} %collective-permute-done.33.refs_0_, bf16[1408,768]{1,0:T(8,128)(2,1)} %constant_dynamic-update-slice_fusion.13.refs_1_, s32[1]{0:T(128)} %bitcast.4.refs_2_, ...), custom_call_target="tpu_custom_call", output_to_operand_aliasing={{0}: (5, {})} | custom-call | tf_op jit(solution)/shard_map/attend_9_0/pallas_call | solution.py:103
  195.5 6.6 %attend_9_1.1 = (bf16[896,1408]{1,0:T(8,128)(2,1)}, bf16[448,384]{1,0:T(8,128)(2,1)}, bf16[448,128]{1,0:T(8,128)(2,1)}) custom-call(bf16[448,1408]{1,0:T(8,128)(2,1)S(1)} %collective-permute-done.x.refs_0_, bf16[1408,768]{1,0:T(8,128)(2,1)} %constant_dynamic-update-slice_fusion.13.refs_1_, s32[1]{0:T(128)} %bitcast.2.s.refs_2_, ...), custom_call_target="tpu_custom_call", output_to_operand_aliasing={{0}: (5, {})} | custom-call | tf_op jit(solution)/shard_map/attend_9_1/pallas_call | solution.py:103
  (123 shorter events, 28.4 us)
Async XLA Ops:
  0.0 9.2 %copy-start.12 = (s32[1056]{0:T(1024)S(1)}, s32[1056]{0:T(1024)}, u32[]{:S(2)}) copy-start(s32[1056]{0:T(1024)} %constant.84.clone) | copy-start | bytes 12676
  0.0 9.2 %copy-start.13 = (s32[1056]{0:T(1024)S(1)}, s32[1056]{0:T(1024)}, u32[]{:S(2)}) copy-start(s32[1056]{0:T(1024)} %constant.85.clone) | copy-start | bytes 12676
  0.0 9.2 %copy-start.14 = (s32[1056]{0:T(1024)S(1)}, s32[1056]{0:T(1024)}, u32[]{:S(2)}) copy-start(s32[1056]{0:T(1024)} %constant.88) | copy-start | bytes 12676
  0.0 7.9 %copy-start.15 = (s32[8,1,2]{0,2,1:T(2,128)S(1)}, s32[8,1,2]{0,2,1:T(2,128)}, u32[]{:S(2)}) copy-start(s32[8,1,2]{0,2,1:T(2,128)} %param.15) | copy-start | bytes 196
  2.6 23.3 %collective-permute-start.1 = (bf16[48,1152]{1,0:T(8,128)(2,1)}, bf16[48,1152]{1,0:T(8,128)(2,1)}, u32[]{:S(2)}, u32[]{:S(2)}) collective-permute-start(bf16[48,1152]{1,0:T(8,128)(2,1)} %slice.139), channel_id=1, source_target_pairs={{0,1},{1,2},{2,3},{3,0},{4,5},{5,6},{6,7},{7,4},{8,9},{9,10},{10,1... | collective-permute-start | bytes 331784 | tf_op jit(solution)/shard_map/ppermute | solution.py:156
  6.3 18.0 %collective-permute-start.13 = (bf16[40,1152]{1,0:T(8,128)(2,1)}, bf16[40,1152]{1,0:T(8,128)(2,1)}, u32[]{:S(2)}, u32[]{:S(2)}) collective-permute-start(bf16[40,1152]{1,0:T(8,128)(2,1)} %pad_maximum_fusion.4), channel_id=1, source_target_pairs={{0,1},{1,2},{2,3},{3,0},{4,5},{5,6},{6,7},{7,4},{8,9},{9,10},{10,1... | collective-permute-start | bytes 276488 | tf_op jit(solution)/shard_map/ppermute | solution.py:156
  9.3 5.3 %copy-start = (bf16[352,4224]{1,0:T(8,128)(2,1)S(1)}, bf16[352,4224]{1,0:T(8,128)(2,1)}, u32[]{:S(2)}) copy-start(bf16[352,4224]{1,0:T(8,128)(2,1)} %param.13) | copy-start | bytes 8921092
  14.6 1.7 copy-start.4
  14.6 122.7 %collective-permute-start.33 = (bf16[448,1408]{1,0:T(8,128)(2,1)}, bf16[448,1408]{1,0:T(8,128)(2,1)S(1)}, u32[]{:S(2)}, u32[]{:S(2)}) collective-permute-start(bf16[448,1408]{1,0:T(8,128)(2,1)} %fusion.4), channel_id=1, source_target_pairs={{0,4},{4,8},{8,12},{12,16},{16,20},{20,24},{24,28},{28,0},{1,5},{5... | collective-permute-start | bytes 3784712 | tf_op jit(solution)/shard_map/ppermute | solution.py:156
  19.3 4.1 %copy-start.1 = (bf16[352,256]{1,0:T(8,128)(2,1)S(1)}, bf16[352,256]{1,0:T(8,128)(2,1)}, u32[]{:S(2)}) copy-start(bf16[352,256]{1,0:T(8,128)(2,1)} %get-tuple-element.78) | copy-start | bytes 540676
  19.4 4.1 %copy-start.2 = (bf16[352,256]{1,0:T(8,128)(2,1)S(1)}, bf16[352,256]{1,0:T(8,128)(2,1)}, u32[]{:S(2)}) copy-start(bf16[352,256]{1,0:T(8,128)(2,1)} %get-tuple-element.79) | copy-start | bytes 540676
  19.4 4.1 %copy-start.3 = (bf16[352,256]{1,0:T(8,128)(2,1)S(1)}, bf16[352,256]{1,0:T(8,128)(2,1)}, u32[]{:S(2)}) copy-start(bf16[352,256]{1,0:T(8,128)(2,1)} %get-tuple-element.80) | copy-start | bytes 540676
  22.4 16.1 %copy-start.11 = (bf16[40,1152]{1,0:T(8,128)(2,1)S(1)}, bf16[40,1152]{1,0:T(8,128)(2,1)}, u32[]{:S(2)}) copy-start(bf16[40,1152]{1,0:T(8,128)(2,1)} %pad_maximum_fusion.5) | copy-start | bytes 276484
  22.4 18.6 %copy-start.9 = (bf16[48,1152]{1,0:T(8,128)(2,1)S(1)}, bf16[48,1152]{1,0:T(8,128)(2,1)}, u32[]{:S(2)}) copy-start(bf16[48,1152]{1,0:T(8,128)(2,1)} %slice.138) | copy-start | bytes 331780
  23.4 35.7 %copy-start.10 = (bf16[40,1152]{1,0:T(8,128)(2,1)S(1)}, bf16[40,1152]{1,0:T(8,128)(2,1)}, u32[]{:S(2)}) copy-start(bf16[40,1152]{1,0:T(8,128)(2,1)} %pad_maximum_fusion.6) | copy-start | bytes 276484
  24.3 7.0 %collective-permute-start.14 = (bf16[40,1152]{1,0:T(8,128)(2,1)}, bf16[40,1152]{1,0:T(8,128)(2,1)S(1)}, u32[]{:S(2)}, u32[]{:S(2)}) collective-permute-start(bf16[40,1152]{1,0:T(8,128)(2,1)} %collective-permute-done.13), channel_id=1, source_target_pairs={{0,1},{1,2},{2,3},{3,0},{4,5},{5,6},{6,7},{7,4},{8,9},{9,10},{10,1... | collective-permute-start | bytes 276488 | tf_op jit(solution)/shard_map/ppermute | solution.py:156
  25.9 7.9 %collective-permute-start.2 = (bf16[48,1152]{1,0:T(8,128)(2,1)}, bf16[48,1152]{1,0:T(8,128)(2,1)S(1)}, u32[]{:S(2)}, u32[]{:S(2)}) collective-permute-start(bf16[48,1152]{1,0:T(8,128)(2,1)} %collective-permute-done.1), channel_id=1, source_target_pairs={{0,1},{1,2},{2,3},{3,0},{4,5},{5,6},{6,7},{7,4},{8,9},{9,10},{10,1... | collective-permute-start | bytes 331784 | tf_op jit(solution)/shard_map/ppermute | solution.py:156
  31.3 7.2 %collective-permute-start.15 = (bf16[40,1152]{1,0:T(8,128)(2,1)S(1)}, bf16[40,1152]{1,0:T(8,128)(2,1)S(1)}, u32[]{:S(2)}, u32[]{:S(2)}) collective-permute-start(bf16[40,1152]{1,0:T(8,128)(2,1)S(1)} %collective-permute-done.14), channel_id=1, source_target_pairs={{0,1},{1,2},{2,3},{3,0},{4,5},{5,6},{6,7},{7,4},{8,9},{9,10},{10,1... | collective-permute-start | bytes 276488 | tf_op jit(solution)/shard_map/ppermute | solution.py:156
  33.8 7.2 %collective-permute-start.3 = (bf16[48,1152]{1,0:T(8,128)(2,1)S(1)}, bf16[48,1152]{1,0:T(8,128)(2,1)S(1)}, u32[]{:S(2)}, u32[]{:S(2)}) collective-permute-start(bf16[48,1152]{1,0:T(8,128)(2,1)S(1)} %collective-permute-done.2), channel_id=1, source_target_pairs={{0,1},{1,2},{2,3},{3,0},{4,5},{5,6},{6,7},{7,4},{8,9},{9,10},{10,1... | collective-permute-start | bytes 331784 | tf_op jit(solution)/shard_map/ppermute | solution.py:156
  38.6 6.6 %collective-permute-start.16 = (bf16[40,1152]{1,0:T(8,128)(2,1)S(1)}, bf16[40,1152]{1,0:T(8,128)(2,1)S(1)}, u32[]{:S(2)}, u32[]{:S(2)}) collective-permute-start(bf16[40,1152]{1,0:T(8,128)(2,1)S(1)} %copy-done.11), channel_id=1, source_target_pairs={{0,1},{1,2},{2,3},{3,0},{4,5},{5,6},{6,7},{7,4},{8,9},{9,10},{10,1... | collective-permute-start | bytes 276488 | tf_op jit(solution)/shard_map/ppermute | solution.py:156
  41.0 6.5 %collective-permute-start.4 = (bf16[48,1152]{1,0:T(8,128)(2,1)S(1)}, bf16[48,1152]{1,0:T(8,128)(2,1)S(1)}, u32[]{:S(2)}, u32[]{:S(2)}) collective-permute-start(bf16[48,1152]{1,0:T(8,128)(2,1)S(1)} %copy-done.9), channel_id=1, source_target_pairs={{0,1},{1,2},{2,3},{3,0},{4,5},{5,6},{6,7},{7,4},{8,9},{9,10},{10,1... | collective-permute-start | bytes 331784 | tf_op jit(solution)/shard_map/ppermute | solution.py:156
  45.2 7.3 %collective-permute-start.17 = (bf16[40,1152]{1,0:T(8,128)(2,1)S(1)}, bf16[40,1152]{1,0:T(8,128)(2,1)S(1)}, u32[]{:S(2)}, u32[]{:S(2)}) collective-permute-start(bf16[40,1152]{1,0:T(8,128)(2,1)S(1)} %collective-permute-done.16), channel_id=1, source_target_pairs={{0,1},{1,2},{2,3},{3,0},{4,5},{5,6},{6,7},{7,4},{8,9},{9,10},{10,1... | collective-permute-start | bytes 276488 | tf_op jit(solution)/shard_map/ppermute | solution.py:156
  45.8 39.4 %collective-permute-start.31 = (bf16[264,1152]{1,0:T(8,128)(2,1)S(1)}, bf16[264,1152]{1,0:T(8,128)(2,1)S(1)}, u32[]{:S(2)}, u32[]{:S(2)}) collective-permute-start(bf16[264,1152]{1,0:T(8,128)(2,1)S(1)} %get-tuple-element.118), channel_id=1, source_target_pairs={{0,8},{4,12},{8,0},{12,4},{16,24},{20,28},{24,16},{28,20},{1,9},{5... | collective-permute-start | bytes 1824776 | tf_op jit(solution)/shard_map/ppermute | solution.py:161
  47.6 6.8 %collective-permute-start.5 = (bf16[48,1152]{1,0:T(8,128)(2,1)S(1)}, bf16[48,1152]{1,0:T(8,128)(2,1)S(1)}, u32[]{:S(2)}, u32[]{:S(2)}) collective-permute-start(bf16[48,1152]{1,0:T(8,128)(2,1)S(1)} %collective-permute-done.4), channel_id=1, source_target_pairs={{0,1},{1,2},{2,3},{3,0},{4,5},{5,6},{6,7},{7,4},{8,9},{9,10},{10,1... | collective-permute-start | bytes 331784 | tf_op jit(solution)/shard_map/ppermute | solution.py:156
  52.4 6.7 %collective-permute-start.18 = (bf16[40,1152]{1,0:T(8,128)(2,1)S(1)}, bf16[40,1152]{1,0:T(8,128)(2,1)S(1)}, u32[]{:S(2)}, u32[]{:S(2)}) collective-permute-start(bf16[40,1152]{1,0:T(8,128)(2,1)S(1)} %collective-permute-done.17), channel_id=1, source_target_pairs={{0,1},{1,2},{2,3},{3,0},{4,5},{5,6},{6,7},{7,4},{8,9},{9,10},{10,1... | collective-permute-start | bytes 276488 | tf_op jit(solution)/shard_map/ppermute | solution.py:156
  54.3 11.1 %collective-permute-start.6 = (bf16[48,1152]{1,0:T(8,128)(2,1)S(1)}, bf16[48,1152]{1,0:T(8,128)(2,1)S(1)}, u32[]{:S(2)}, u32[]{:S(2)}) collective-permute-start(bf16[48,1152]{1,0:T(8,128)(2,1)S(1)} %collective-permute-done.5), channel_id=1, source_target_pairs={{0,1},{1,2},{2,3},{3,0},{4,5},{5,6},{6,7},{7,4},{8,9},{9,10},{10,1... | collective-permute-start | bytes 331784 | tf_op jit(solution)/shard_map/ppermute | solution.py:156
  59.1 6.3 %collective-permute-start.19 = (bf16[40,1152]{1,0:T(8,128)(2,1)S(1)}, bf16[40,1152]{1,0:T(8,128)(2,1)S(1)}, u32[]{:S(2)}, u32[]{:S(2)}) collective-permute-start(bf16[40,1152]{1,0:T(8,128)(2,1)S(1)} %copy-done.10), channel_id=1, source_target_pairs={{0,1},{1,2},{2,3},{3,0},{4,5},{5,6},{6,7},{7,4},{8,9},{9,10},{10,1... | collective-permute-start | bytes 276488 | tf_op jit(solution)/shard_map/ppermute | solution.py:156
  65.5 7.3 %collective-permute-start.20 = (bf16[40,1152]{1,0:T(8,128)(2,1)S(1)}, bf16[40,1152]{1,0:T(8,128)(2,1)S(1)}, u32[]{:S(2)}, u32[]{:S(2)}) collective-permute-start(bf16[40,1152]{1,0:T(8,128)(2,1)S(1)} %collective-permute-done.19), channel_id=1, source_target_pairs={{0,1},{1,2},{2,3},{3,0},{4,5},{5,6},{6,7},{7,4},{8,9},{9,10},{10,1... | collective-permute-start | bytes 276488 | tf_op jit(solution)/shard_map/ppermute | solution.py:156
  65.5 9.6 %collective-permute-start.7 = (bf16[48,1152]{1,0:T(8,128)(2,1)S(1)}, bf16[48,1152]{1,0:T(8,128)(2,1)S(1)}, u32[]{:S(2)}, u32[]{:S(2)}) collective-permute-start(bf16[48,1152]{1,0:T(8,128)(2,1)S(1)} %slice.137), channel_id=1, source_target_pairs={{0,1},{1,2},{2,3},{3,0},{4,5},{5,6},{6,7},{7,4},{8,9},{9,10},{10,1... | collective-permute-start | bytes 331784 | tf_op jit(solution)/shard_map/ppermute | solution.py:156
  68.3 52.6 %collective-permute-start.29 = (bf16[264,1152]{1,0:T(8,128)(2,1)S(1)}, bf16[264,1152]{1,0:T(8,128)(2,1)S(1)}, u32[]{:S(2)}, u32[]{:S(2)}) collective-permute-start(bf16[264,1152]{1,0:T(8,128)(2,1)S(1)} %get-tuple-element.127), channel_id=1, source_target_pairs={{0,8},{4,12},{8,0},{12,4},{16,24},{20,28},{24,16},{28,20},{1,9},{5... | collective-permute-start | bytes 1824776 | tf_op jit(solution)/shard_map/ppermute | solution.py:161
  72.8 6.3 %collective-permute-start.21 = (bf16[40,1152]{1,0:T(8,128)(2,1)S(1)}, bf16[40,1152]{1,0:T(8,128)(2,1)S(1)}, u32[]{:S(2)}, u32[]{:S(2)}) collective-permute-start(bf16[40,1152]{1,0:T(8,128)(2,1)S(1)} %collective-permute-done.20), channel_id=1, source_target_pairs={{0,1},{1,2},{2,3},{3,0},{4,5},{5,6},{6,7},{7,4},{8,9},{9,10},{10,1... | collective-permute-start | bytes 276488 | tf_op jit(solution)/shard_map/ppermute | solution.py:156
  75.1 6.8 %collective-permute-start.8 = (bf16[48,1152]{1,0:T(8,128)(2,1)S(1)}, bf16[48,1152]{1,0:T(8,128)(2,1)S(1)}, u32[]{:S(2)}, u32[]{:S(2)}) collective-permute-start(bf16[48,1152]{1,0:T(8,128)(2,1)S(1)} %collective-permute-done.7), channel_id=1, source_target_pairs={{0,1},{1,2},{2,3},{3,0},{4,5},{5,6},{6,7},{7,4},{8,9},{9,10},{10,1... | collective-permute-start | bytes 331784 | tf_op jit(solution)/shard_map/ppermute | solution.py:156
  79.1 6.0 %collective-permute-start.22 = (bf16[40,768]{1,0:T(8,128)(2,1)S(1)}, bf16[40,768]{1,0:T(8,128)(2,1)S(1)}, u32[]{:S(2)}, u32[]{:S(2)}) collective-permute-start(bf16[40,768]{1,0:T(8,128)(2,1)S(1)} %pad_maximum_fusion.7), channel_id=1, source_target_pairs={{0,1},{1,2},{2,3},{3,0},{4,5},{5,6},{6,7},{7,4},{8,9},{9,10},{10,1... | collective-permute-start | bytes 184328 | tf_op jit(solution)/shard_map/ppermute | solution.py:156
  81.8 9.4 %collective-permute-start.9 = (bf16[48,1152]{1,0:T(8,128)(2,1)S(1)}, bf16[48,1152]{1,0:T(8,128)(2,1)S(1)}, u32[]{:S(2)}, u32[]{:S(2)}) collective-permute-start(bf16[48,1152]{1,0:T(8,128)(2,1)S(1)} %collective-permute-done.8), channel_id=1, source_target_pairs={{0,1},{1,2},{2,3},{3,0},{4,5},{5,6},{6,7},{7,4},{8,9},{9,10},{10,1... | collective-permute-start | bytes 331784 | tf_op jit(solution)/shard_map/ppermute | solution.py:156
  85.2 6.0 %collective-permute-start.23 = (bf16[40,768]{1,0:T(8,128)(2,1)S(1)}, bf16[40,768]{1,0:T(8,128)(2,1)S(1)}, u32[]{:S(2)}, u32[]{:S(2)}) collective-permute-start(bf16[40,768]{1,0:T(8,128)(2,1)S(1)} %collective-permute-done.22), channel_id=1, source_target_pairs={{0,1},{1,2},{2,3},{3,0},{4,5},{5,6},{6,7},{7,4},{8,9},{9,10},{10,1... | collective-permute-start | bytes 184328 | tf_op jit(solution)/shard_map/ppermute | solution.py:156
  85.2 32.3 %copy-start.17 = (bf16[896,1408]{1,0:T(8,128)(2,1)S(1)}, bf16[896,1408]{1,0:T(8,128)(2,1)}, u32[]{:S(2)}) copy-start(bf16[896,1408]{1,0:T(8,128)(2,1)} %param.12) | copy-start | bytes 7569412
  86.1 44.3 %collective-permute-start.32 = (bf16[528,1152]{1,0:T(8,128)(2,1)S(1)}, bf16[528,1152]{1,0:T(8,128)(2,1)}, u32[]{:S(2)}, u32[]{:S(2)}) collective-permute-start(bf16[528,1152]{1,0:T(8,128)(2,1)S(1)} %get-tuple-element.81), channel_id=1, source_target_pairs={{0,4},{4,0},{8,12},{12,8},{16,20},{20,16},{24,28},{28,24},{1,5},{5... | collective-permute-start | bytes 3649544 | tf_op jit(solution)/shard_map/ppermute | solution.py:161
  91.2 23.4 %collective-permute-start.24 = (bf16[40,768]{1,0:T(8,128)(2,1)S(1)}, bf16[40,768]{1,0:T(8,128)(2,1)S(1)}, u32[]{:S(2)}, u32[]{:S(2)}) collective-permute-start(bf16[40,768]{1,0:T(8,128)(2,1)S(1)} %collective-permute-done.23), channel_id=1, source_target_pairs={{0,1},{1,2},{2,3},{3,0},{4,5},{5,6},{6,7},{7,4},{8,9},{9,10},{10,1... | collective-permute-start | bytes 184328 | tf_op jit(solution)/shard_map/ppermute | solution.py:156
  91.2 7.6 %collective-permute-start.10 = (bf16[48,768]{1,0:T(8,128)(2,1)S(1)}, bf16[48,768]{1,0:T(8,128)(2,1)S(1)}, u32[]{:S(2)}, u32[]{:S(2)}) collective-permute-start(bf16[48,768]{1,0:T(8,128)(2,1)S(1)} %slice.136), channel_id=1, source_target_pairs={{0,1},{1,2},{2,3},{3,0},{4,5},{5,6},{6,7},{7,4},{8,9},{9,10},{10,1... | collective-permute-start | bytes 221192 | tf_op jit(solution)/shard_map/ppermute | solution.py:156
  98.8 6.2 %collective-permute-start.11 = (bf16[48,768]{1,0:T(8,128)(2,1)S(1)}, bf16[48,768]{1,0:T(8,128)(2,1)S(1)}, u32[]{:S(2)}, u32[]{:S(2)}) collective-permute-start(bf16[48,768]{1,0:T(8,128)(2,1)S(1)} %collective-permute-done.10), channel_id=1, source_target_pairs={{0,1},{1,2},{2,3},{3,0},{4,5},{5,6},{6,7},{7,4},{8,9},{9,10},{10,1... | collective-permute-start | bytes 221192 | tf_op jit(solution)/shard_map/ppermute | solution.py:156
  104.9 6.2 %collective-permute-start.12 = (bf16[48,768]{1,0:T(8,128)(2,1)S(1)}, bf16[48,768]{1,0:T(8,128)(2,1)S(1)}, u32[]{:S(2)}, u32[]{:S(2)}) collective-permute-start(bf16[48,768]{1,0:T(8,128)(2,1)S(1)} %collective-permute-done.11), channel_id=1, source_target_pairs={{0,1},{1,2},{2,3},{3,0},{4,5},{5,6},{6,7},{7,4},{8,9},{9,10},{10,1... | collective-permute-start | bytes 221192 | tf_op jit(solution)/shard_map/ppermute | solution.py:156
  111.1 17.7 %collective-permute-start.27 = (bf16[264,1152]{1,0:T(8,128)(2,1)S(1)}, bf16[264,1152]{1,0:T(8,128)(2,1)S(1)}, u32[]{:S(2)}, u32[]{:S(2)}) collective-permute-start(bf16[264,1152]{1,0:T(8,128)(2,1)S(1)} %get-tuple-element.136), channel_id=1, source_target_pairs={{0,8},{4,12},{8,0},{12,4},{16,24},{20,28},{24,16},{28,20},{1,9},{5... | collective-permute-start | bytes 1824776 | tf_op jit(solution)/shard_map/ppermute | solution.py:161
  115.3 12.5 %collective-permute-start.25 = (bf16[264,768]{1,0:T(8,128)(2,1)S(1)}, bf16[264,768]{1,0:T(8,128)(2,1)S(1)}, u32[]{:S(2)}, u32[]{:S(2)}) collective-permute-start(bf16[264,768]{1,0:T(8,128)(2,1)S(1)} %get-tuple-element.154), channel_id=1, source_target_pairs={{0,16},{4,20},{8,24},{12,28},{16,0},{20,4},{24,8},{28,12},{1,17},{... | collective-permute-start | bytes 1216520 | tf_op jit(solution)/shard_map/ppermute | solution.py:161
  120.9 26.1 %collective-permute-start = (bf16[448,1408]{1,0:T(8,128)(2,1)}, bf16[448,1408]{1,0:T(8,128)(2,1)S(1)}, u32[]{:S(2)}, u32[]{:S(2)}) collective-permute-start(bf16[448,1408]{1,0:T(8,128)(2,1)} %fusion.5), channel_id=1, source_target_pairs={{0,16},{4,20},{8,24},{12,28},{16,0},{20,4},{24,8},{28,12},{1,17},{... | collective-permute-start | bytes 3784712 | tf_op jit(solution)/shard_map/ppermute | solution.py:156
  120.9 13.3 %copy-start.16 = (s32[8,1,2,2]{0,3,2,1:T(2,128)S(1)}, s32[8,1,2,2]{0,3,2,1:T(2,128)}, u32[]{:S(2)}) copy-start(s32[8,1,2,2]{0,3,2,1:T(2,128)} %param.14) | copy-start | bytes 388
  127.8 27.2 %collective-permute-start.30 = (bf16[528,1152]{1,0:T(8,128)(2,1)}, bf16[528,1152]{1,0:T(8,128)(2,1)}, u32[]{:S(2)}, u32[]{:S(2)}) collective-permute-start(bf16[528,1152]{1,0:T(8,128)(2,1)} %get-tuple-element.83), channel_id=1, source_target_pairs={{0,4},{4,0},{8,12},{12,8},{16,20},{20,16},{24,28},{28,24},{1,5},{5... | collective-permute-start | bytes 3649544 | tf_op jit(solution)/shard_map/ppermute | solution.py:161
  128.7 25.2 %collective-permute-start.26 = (bf16[528,768]{1,0:T(8,128)(2,1)}, bf16[528,768]{1,0:T(8,128)(2,1)S(1)}, u32[]{:S(2)}, u32[]{:S(2)}) collective-permute-start(bf16[528,768]{1,0:T(8,128)(2,1)} %get-tuple-element.87), channel_id=1, source_target_pairs={{0,4},{4,0},{8,12},{12,8},{16,20},{20,16},{24,28},{28,24},{1,5},{5... | collective-permute-start | bytes 2433032 | tf_op jit(solution)/shard_map/ppermute | solution.py:161
  130.4 41.4 %collective-permute-start.28 = (bf16[528,1152]{1,0:T(8,128)(2,1)}, bf16[528,1152]{1,0:T(8,128)(2,1)}, u32[]{:S(2)}, u32[]{:S(2)}) collective-permute-start(bf16[528,1152]{1,0:T(8,128)(2,1)} %get-tuple-element.85), channel_id=1, source_target_pairs={{0,4},{4,0},{8,12},{12,8},{16,20},{20,16},{24,28},{28,24},{1,5},{5... | collective-permute-start | bytes 3649544 | tf_op jit(solution)/shard_map/ppermute | solution.py:161
  (4 other events, 4.9 us)

commit v2 on v0

v2 whole, which is shorter than its diff:
```python
import functools
import math

import jax
import jax.numpy as jnp
import numpy as np
from jax import lax
from jax.experimental import pallas as pl
from jax.experimental.pallas import tpu as pltpu
from jax.sharding import PartitionSpec as P

HEADS = 16
LANE = 128
FAR_BELOW = -1e30
PIECES = 4
BOUNDS = ((0, 3), (3, 6), (6, 9), (9, 11))
SWAPS = (2, 2, 4, 2)


def heads_of(bounds, head_dim):
    found, h = [], 0
    for _, t1 in bounds:
        end = min(HEADS, t1 * LANE // head_dim)
        found.append((h, end))
        h = end
    return found


def pick_kernel(route_ref, rank_ref, tokens, near, far, sems):
    rows = near.shape[0]
    copies = []
    for r, to in enumerate((near, far)):
        start = pl.multiple_of(route_ref[rank_ref[0], 0, r] * rows, rows)
        copies.append(pltpu.make_async_copy(tokens.at[pl.ds(start, rows)], to, sems.at[r]))
    for c in copies:
        c.start()
    for c in copies:
        c.wait()


def picked(balance, rank, tokens):
    rows, width = tokens.shape
    anywhere = pl.BlockSpec(memory_space=pl.ANY)
    scalars = pl.BlockSpec(memory_space=pltpu.SMEM)
    half = jax.ShapeDtypeStruct((rows // 2, width), tokens.dtype)
    return pl.pallas_call(
        pick_kernel,
        out_shape=[half, half],
        in_specs=[scalars, scalars, anywhere],
        out_specs=[pl.BlockSpec(memory_space=pltpu.VMEM)] * 2,
        scratch_shapes=[pltpu.SemaphoreType.DMA((2,))],
        name="pick",
    )(balance, rank, tokens)


def attend_kernel(t0, t1, h0, h1, hd, bundles, has_out, *refs):
    nb = len(bundles)
    refs = list(refs)
    x_refs = [refs.pop(0) for _ in range(nb)]
    w_ref, lengths_ref, route_ref, source_ref = [refs.pop(0) for _ in range(4)]
    later = t0 > 0
    pc_in = [refs.pop(0) for _ in range(nb)] if later else None
    oc_in = [refs.pop(0) for _ in range(nb)] if later else None
    if has_out:
        refs.pop(0)
    out = refs.pop(0)
    pc_out = [refs.pop(0) for _ in range(nb)]
    oc_out = [refs.pop(0) for _ in range(nb)]
    proj, done, sems = refs
    rows = x_refs[0].shape[0]
    nt = t1 - t0
    base = t0 - 1
    first_tile = h0 * hd // LANE
    c = math.log2(math.e) / math.sqrt(hd)
    copies = []
    for i, bundle in enumerate(bundles):
        p = jnp.dot(x_refs[i][...], w_ref[...], preferred_element_type=jnp.float32).astype(jnp.bfloat16)
        for part in range(3):
            proj[i, part, :, LANE:] = p[:, part * nt * LANE : (part + 1) * nt * LANE]
            if later:
                proj[i, part, :, :LANE] = pc_in[i][:, part * LANE : (part + 1) * LANE]
            pc_out[i][:, part * LANE : (part + 1) * LANE] = proj[i, part, :, nt * LANE :]
        source = source_ref[bundle]
        split = lengths_ref[source, 0, route_ref[source, 0, bundle], 0]
        made = {}

        def tags(w, at, a, b):
            if (w, at, a, b) not in made:
                late = lax.broadcasted_iota(jnp.int32, (rows, w), 0) >= split
                lane = lax.broadcasted_iota(jnp.int32, (rows, w), 1)
                one, two = jnp.where(late, b, a), jnp.where(late, a, b)
                both = jnp.where(lane == at, one, jnp.where(lane == at + 1, two, 0.0))
                made[(w, at, a, b)] = both.astype(jnp.bfloat16)
            return made[(w, at, a, b)]

        partial = oc_in[i][...] if later else None
        for h in range(h0, h1):
            lo, hi = h * hd, (h + 1) * hd
            s0, s1 = lo // LANE, -(-hi // LANE)
            w = (s1 - s0) * LANE
            a, b = lo - s0 * LANE, hi - s0 * LANE
            at = 0 if a >= 2 else w - 2
            lane = lax.broadcasted_iota(jnp.int32, (rows, w), 1)
            own = (lane >= a) & (lane < b)
            cols = slice((s0 - base) * LANE, (s1 - base) * LANE)
            q = jnp.where(own, proj[i, 0, :, cols], tags(w, at, 1.0, 0.0))
            k = jnp.where(own, proj[i, 1, :, cols], tags(w, at, 0.0, FAR_BELOW))
            ones = jnp.where(lane == at, 1.0, 0.0).astype(jnp.bfloat16)
            v = jnp.where(own, proj[i, 2, :, cols], ones)
            s = lax.dot_general(q, k, (((1,), (1,)), ((), ())), preferred_element_type=jnp.float32)
            m = jnp.max(s, axis=1, keepdims=True) * c
            e = jnp.exp2(s * c - m).astype(jnp.bfloat16)
            o = jnp.dot(e, v, preferred_element_type=jnp.float32)
            o = (o / o[:, at : at + 1]).astype(jnp.bfloat16)
            for t in range(s0, s1):
                piece = o[:, (t - s0) * LANE : (t - s0 + 1) * LANE]
                start = max(lo - t * LANE, 0)
                if start > 0:
                    lanes = lax.broadcasted_iota(jnp.int32, (rows, LANE), 1)
                    piece = jnp.where(lanes < start, partial, piece)
                if hi >= (t + 1) * LANE:
                    j = t - first_tile
                    done[i, j] = piece
                    copy = pltpu.make_async_copy(
                        done.at[i, j],
                        out.at[pl.ds(bundle * rows, rows), pl.ds(t * LANE, LANE)],
                        sems.at[i, j],
                    )
                    copy.start()
                    copies.append(copy)
                    partial = None
                else:
                    partial = piece
        oc_out[i][...] = jnp.zeros((rows, LANE), jnp.bfloat16) if partial is None else partial
    for copy in copies:
        copy.wait()


def attend(t0, t1, h0, h1, bundles, xs, w, info, carry, out):
    rows, d = xs[0].shape
    hd = d // HEADS
    nb, nt = len(bundles), t1 - t0
    tiles = h1 * hd // LANE - h0 * hd // LANE
    inside = pl.BlockSpec(memory_space=pltpu.VMEM)
    anywhere = pl.BlockSpec(memory_space=pl.ANY)
    scalars = pl.BlockSpec(memory_space=pltpu.SMEM)
    operands = [*xs, w, *info]
    specs = [inside] * (nb + 1) + [scalars] * 3
    if t0 > 0:
        operands += [carry[b][0] for b in bundles] + [carry[b][1] for b in bundles]
        specs += [inside] * (2 * nb)
    alias = {}
    if out is not None:
        alias = {len(operands): 0}
        operands.append(out)
        specs.append(anywhere)
    shape = lambda r, c: jax.ShapeDtypeStruct((r, c), jnp.bfloat16)
    res = pl.pallas_call(
        functools.partial(attend_kernel, t0, t1, h0, h1, hd, bundles, out is not None),
        out_shape=[shape(2 * rows, d)] + [shape(rows, 3 * LANE)] * nb + [shape(rows, LANE)] * nb,
        in_specs=specs,
        out_specs=[anywhere] + [inside] * (2 * nb),
        scratch_shapes=[
            pltpu.VMEM((nb, 3, rows, (nt + 1) * LANE), jnp.bfloat16),
            pltpu.VMEM((nb, tiles, rows, LANE), jnp.bfloat16),
            pltpu.SemaphoreType.DMA((nb, tiles)),
        ],
        input_output_aliases=alias,
        compiler_params=pltpu.CompilerParams(vmem_limit_bytes=16 * 2**20),
        cost_estimate=pl.CostEstimate(
            flops=nb * (2 * rows * w.shape[0] * w.shape[1] + 4 * rows * rows * 256 * (h1 - h0)),
            bytes_accessed=2 * w.size + 2 * nb * rows * d,
            transcendentals=nb * rows * rows * (h1 - h0),
        ),
        name=f"attend_{t0}_{bundles[0]}",
    )(*operands)
    for i, b in enumerate(bundles):
        carry[b] = (res[1 + i], res[1 + nb + i])
    return res[0]


ARRIVAL = ((1, 0), (3, 0), (1, 2), (3, 2), (2, 0), (2, 2))


def quarter_of(rank):
    return ((((rank >> 2) ^ (rank >> 1)) & 1) << 1) | (rank & 1)


def source_columns(rank, column, shard_rows, shards):
    quarter = shard_rows // PIECES
    step = np.array([s for core in (0, 1) for s, _ in ARRIVAL for _ in range(quarter)])
    flip = np.array([core | across for core in (0, 1) for _, across in ARRIVAL for _ in range(quarter)])
    row = np.array(list(range(quarter)) * (2 * len(ARRIVAL)))
    rest = ((column - step) % shards) * shard_rows + (quarter_of(rank) ^ flip) * quarter + row
    own = column * shard_rows + np.arange(shard_rows)
    return jnp.concatenate([own, rest]).astype(jnp.int32)


def reordered(x, place):
    return jnp.dot(x, place, preferred_element_type=jnp.float32).astype(jnp.bfloat16)


def shifted(x, axis, by):
    n = lax.axis_size(axis)
    return lax.ppermute(x, axis, [(i, (i + by) % n) for i in range(n)])


def swapped(x, mask):
    n = lax.axis_size("dp")
    return lax.ppermute(x, "dp", [(i, i ^ mask) for i in range(n)])


def fence(*values):
    return lax.optimization_barrier(values)


def stacked(*xs):
    return jnp.concatenate(xs, axis=0)


def on_device(tokens, qkv_weight, image_lengths, balance):
    ranks = lax.axis_size("dp")
    shards = lax.axis_size("fsdp")
    rank = lax.axis_index("dp")
    column = lax.axis_index("fsdp")
    rows, width = tokens.shape
    shard_rows = qkv_weight.shape[0]
    quarter = shard_rows // PIECES
    hd = width // HEADS
    sources = jnp.stack([(rank - 1) % ranks, (rank - ranks // 2) % ranks]).astype(jnp.int32)
    info = (image_lengths, balance, sources)
    columns = source_columns(rank, column, shard_rows, shards)
    quarter_start = quarter_of(rank) * quarter

    def columns_matrix():
        return (jnp.arange(width, dtype=jnp.int32)[:, None] == columns[None, :]).astype(jnp.bfloat16)

    def of_chunk(w, t0, t1):
        return jnp.concatenate([w[:, p * width + t0 * LANE : p * width + t1 * LANE] for p in range(3)], axis=1)

    def payload(w, c):
        return of_chunk(lax.dynamic_slice_in_dim(w, quarter_start, quarter, 0), *BOUNDS[c])

    def up(x):
        return shifted(x, "fsdp", 1)

    def down(x):
        return shifted(x, "fsdp", shards - 1)

    def across(c, *xs):
        return swapped(stacked(*xs) if len(xs) > 1 else xs[0], SWAPS[c])

    spans = [(*b, *h) for b, h in zip(BOUNDS, heads_of(BOUNDS, hd))]
    carry = [None, None]
    w = qkv_weight

    pa = payload(w, 0)
    ap, am = up(pa), down(pa)
    w, _ = fence(w, pa)
    pb = payload(w, 1)
    bp, bm = up(pb), down(pb)
    tokens, w, _ = fence(tokens, w, pb)
    near, far = picked(balance, rank.reshape(1), tokens)
    near_in, far_in = shifted(near, "dp", 1), shifted(far, "dp", ranks // 2)
    w, _ = fence(w, near)
    pc = payload(w, 2)

    ap, pc, w = fence(ap, pc, w)
    a2, cp = up(ap), up(pc)
    own_a = of_chunk(w, *BOUNDS[0])
    pd = payload(w, 3)

    am, bp, pc, pd, own_a, ap = fence(am, bp, pc, pd, own_a, ap)
    ax = across(0, ap, am)
    b2, cm = up(bp), down(pc)
    place = columns_matrix()

    near, a2, pd, w, place = fence(near_in, a2, pd, w, place)
    ay = across(0, a2)
    dp, dm = up(pd), down(pd)
    near = reordered(near, place)
    own_b = of_chunk(w, *BOUNDS[1])

    bm, cp, bp, near, own_b, w = fence(bm, cp, bp, near, own_b, w)
    c2 = up(cp)
    bx = across(1, bp, bm)
    own_c = of_chunk(w, *BOUNDS[2])

    ax, ay, b2, ap, am, a2, own_c, w = fence(ax, ay, b2, ap, am, a2, own_c, w)
    both_a = stacked(ap, am, ax, a2, ay)
    ac = swapped(both_a, 1)
    by = across(1, b2)
    own_d = of_chunk(w, *BOUNDS[3])

    far, cm, dp, cp, place, own_d = fence(far_in, cm, dp, cp, place, own_d)
    d2 = up(dp)
    cx = across(2, cp, cm)
    far = reordered(far, place)

    ac, both_a, own_a, near, far = fence(ac, both_a, own_a, near, far)
    wa = stacked(own_a, both_a, ac)
    out = attend(*spans[0], (0, 1), (near, far), wa, info, carry, None)

    out, bx, dm, dp, by, bp, bm, b2 = fence(out, bx, dm, dp, by, bp, bm, b2)
    dx = across(3, dp, dm)
    both_b = stacked(bp, bm, bx, b2, by)
    bc = swapped(both_b, 1)

    c2, d2, bc, both_b, own_b = fence(c2, d2, bc, both_b, own_b)
    cy = across(2, c2)
    dy = across(3, d2)
    wb = stacked(own_b, both_b, bc)
    out = attend(*spans[1], (0,), (near,), wb, info, carry, out)

    out, cx, cy, dx, dy, cp, cm, c2, dp, dm, d2 = fence(out, cx, cy, dx, dy, cp, cm, c2, dp, dm, d2)
    both_c = stacked(cp, cm, cx, c2, cy)
    cc = swapped(both_c, 1)
    both_d = stacked(dp, dm, dx, d2, dy)
    dc = swapped(both_d, 1)
    out = attend(*spans[1], (1,), (far,), wb, info, carry, out)

    wc = stacked(own_c, both_c, cc)
    out = attend(*spans[2], (0, 1), (near, far), wc, info, carry, out)
    wd = stacked(own_d, both_d, dc)
    out = attend(*spans[3], (0, 1), (near, far), wd, info, carry, out)
    return out


def solution(mesh):
    in_specs = (
        P(("dp", "fsdp"), None),
        P("fsdp", None),
        P(None, "fsdp", None, None),
        P(None, "fsdp", None),
    )
    return jax.shard_map(
        on_device, mesh=mesh, in_specs=in_specs, out_specs=P(("dp", "fsdp"), None), check_vma=False
    )
```

time: 416 us -> 123 us (0.30)
  waiting for transfers between devices: 288 us -> 36.7 us
  matrix products: 48.6 us -> 5.81 us
  Pallas kernels: 0 us -> 38.9 us
  other arithmetic: 39.2 us -> 7.88 us
  starting transfers between devices: 1.59 us -> 24.2 us
  between operations: 18 us -> 0.78 us
  local copies, waits for them, and re-layouts: 20.2 us -> 8.05 us
    all_gather x1 -> x0, waiting for transfers between devices: 209 us -> none  [on_device(): lax.all_gather(qkv_weight, 'fsdp', axis=0, tiled=True)]
    dot_general x5 -> x2, matrix products: 48.6 us -> 5.81 us  [reordered(): jnp.dot(x, place, preferred_element_type=jnp.float32).astype(jnp.bfloat16)]
    ppermute x2 -> x26, waiting for transfers between devices: 78 us -> 36.7 us  [the longest x14 28 us: shifted(): return lax.ppermute(x, axis, [(i, (i + by) % n) for i in range(n)])]
    pallas_call x0 -> x6, Pallas kernels: none -> 38.9 us  [the longest x5 34.9 us: attend(): pl.pallas_call(functools.partial(attend_kernel, t0, t1, h0, h1, hd, bundl...]
    sub x2 -> x0, other arithmetic: 32 us -> none  [attend_bundle(): raised = jnp.where(allowed, jnp.exp(masked - row_max), 0.0)]
    ppermute x2 -> x26, starting transfers between devices: 1.59 us -> 24.2 us  [the longest x14 15.1 us: shifted(): return lax.ppermute(x, axis, [(i, (i + by) % n) for i in range(n)])]
    ppermute x2 -> x0, local copies, waits for them, and re-layouts: 12.9 us -> none  [passed_along(): lax.ppermute(x, axis, [(i, (i + by) % length) for i in range(length)])]
    unnamed x6 -> x36, local copies, waits for them, and re-layouts: 0.01 us -> 4.58 us
  transfers between devices with their start and end apart: 3 -> 26, of which waited for: 3 -> 8; matrix products, arithmetic and copies ran while one was open for 11% -> 16% of each run, Pallas kernels for 0% -> 18%
where the time goes in v2:
time: 123 us; the launch traced here: 122 us
  Pallas kernels  38.9 us (32%)
  waiting for transfers between devices  36.7 us (30%)
  starting transfers between devices  24.2 us (20%)
  local copies, waits for them, and re-layouts  8.05 us (7%)
  other arithmetic  7.88 us (6%)
  matrix products  5.81 us (5%)
    pallas_call x5, Pallas kernels, attend(): pl.pallas_call(functools.partial(attend_kernel, t0, t1, h0, h1, hd, bundl...  34.9 us
    ppermute x14, waiting for transfers between devices, shifted(): return lax.ppermute(x, axis, [(i, (i + by) % n) for i in range(n)])  28 us
    ppermute x14, starting transfers between devices, shifted(): return lax.ppermute(x, axis, [(i, (i + by) % n) for i in range(n)])  15.1 us
    ppermute x12, starting transfers between devices, swapped(): return lax.ppermute(x, 'dp', [(i, i ^ mask) for i in range(n)])  9.08 us
    ppermute x12, waiting for transfers between devices, swapped(): return lax.ppermute(x, 'dp', [(i, i ^ mask) for i in range(n)])  8.69 us
    dot_general x2, matrix products, reordered(): jnp.dot(x, place, preferred_element_type=jnp.float32).astype(jnp.bfloat16)  5.81 us
    unnamed x36, local copies, waits for them, and re-layouts  4.58 us
    pallas_call x1, Pallas kernels, picked(): pl.pallas_call(pick_kernel, out_shape=[half, half], in_specs=[scalars, sc...  3.92 us
  transfers between devices with their start and end apart: 26, of which 8 were waited for; matrix products, arithmetic and copies ran while one was open for 16% of the time, Pallas kernels for 18%

profile of v2, /device:TPU:0, one launch (start us, length us, event | category | flops | bytes accessed | tf_op | source)
XLA Modules:
  0.0 122.2 jit_solution(16458139574863484177)
XLA Ops:
  0.0 1.0 constant_dynamic-slice_fusion
  1.0 0.7 pad_maximum_fusion.9
  1.7 3.0 %collective-permute-start.2 = (bf16[88,1152]{1,0:T(8,128)(2,1)}, bf16[88,1152]{1,0:T(8,128)(2,1)}, u32[]{:S(2)}, u32[]{:S(2)}) collective-permute-start(bf16[88,1152]{1,0:T(8,128)(2,1)} %pad_maximum_fusion.9), channel_id=1, source_target_pairs={{0,1},{1,2},{2,3},{3,0},{4,5},{5,6},{6,7},{7,4},{8,9},{9,10},{10,1... | collective-permute-start | bytes 608264 | tf_op jit(solution)/shard_map/ppermute | solution.py:205
  4.8 2.0 %collective-permute-start = (bf16[88,1152]{1,0:T(8,128)(2,1)}, bf16[88,1152]{1,0:T(8,128)(2,1)}, u32[]{:S(2)}, u32[]{:S(2)}) collective-permute-start(bf16[88,1152]{1,0:T(8,128)(2,1)} %pad_maximum_fusion.9), channel_id=1, source_target_pairs={{0,3},{1,0},{2,1},{3,2},{4,7},{5,4},{6,5},{7,6},{8,11},{9,8},{10,9... | collective-permute-start | bytes 608264 | tf_op jit(solution)/shard_map/ppermute | solution.py:205
  6.8 1.0 fusion.11
  7.8 0.7 pad_maximum_fusion.10
  8.5 3.8 %collective-permute-start.8 = (bf16[88,1152]{1,0:T(8,128)(2,1)}, bf16[88,1152]{1,0:T(8,128)(2,1)S(1)}, u32[]{:S(2)}, u32[]{:S(2)}) collective-permute-start(bf16[88,1152]{1,0:T(8,128)(2,1)} %pad_maximum_fusion.10), channel_id=1, source_target_pairs={{0,3},{1,0},{2,1},{3,2},{4,7},{5,4},{6,5},{7,6},{8,11},{9,8},{10,9... | collective-permute-start | bytes 608264 | tf_op jit(solution)/shard_map/ppermute | solution.py:205
  12.3 1.3 %copy.13.route_ref.refs_4_.refs_3_ = s32[8,1,2]{2,1,0:T(1,128)} copy(s32[8,1,2]{0,2,1:T(2,128)} %param.11) | data formatting | bytes 128 | tf_op args[3]
  13.6 3.9 %pick.1 = (bf16[448,1408]{1,0:T(8,128)(2,1)}, bf16[448,1408]{1,0:T(8,128)(2,1)}) custom-call(s32[8,1,2]{2,1,0:T(1,128)} %copy.13.route_ref.refs_4_.refs_3_, s32[1]{0:T(128)} %bitcast.rank_ref, bf16[896,1408]{1,0:T(8,128)(2,1)} %tokens), custom_call_target="tpu_custom_call" | custom-call | tf_op jit(solution)/shard_map/pick/pallas_call | solution.py:46
  17.8 3.6 %fusion = bf16[1408,1408]{1,0:T(8,128)(2,1)} fusion(s32[1408]{0:T(1024)S(1)} %pad_add_fusion), kind=kLoop, calls=%fused_computation.1 | loop fusion | flops 3964928 | bytes 3970560 | tf_op jit(solution)/shard_map/convert_element_type | solution.py:236
  21.4 0.7 fusion.10
  22.1 0.9 pad_maximum_fusion.11
  23.0 1.8 %collective-permute-start.11 = (bf16[448,1408]{1,0:T(8,128)(2,1)}, bf16[448,1408]{1,0:T(8,128)(2,1)S(1)}, u32[]{:S(2)}, u32[]{:S(2)}) collective-permute-start(bf16[448,1408]{1,0:T(8,128)(2,1)} %get-tuple-element.115), channel_id=1, source_target_pairs={{0,16},{4,20},{8,24},{12,28},{16,0},{20,4},{24,8},{28,12},{1,17},{... | collective-permute-start | bytes 3784712 | tf_op jit(solution)/shard_map/ppermute | solution.py:205
  25.2 1.2 pad_maximum_fusion.5
  26.4 8.3 %collective-permute-done.5 = bf16[88,1152]{1,0:T(8,128)(2,1)S(1)} collective-permute-done((bf16[88,1152]{1,0:T(8,128)(2,1)}, bf16[88,1152]{1,0:T(8,128)(2,1)S(1)}, u32[]{:S(2)}, u32[]{:S(2)}) %collective-permute-start.5) | collective-permute-done | bytes 202784 | tf_op jit(solution)/shard_map/ppermute | solution.py:205
  34.7 1.8 %collective-permute-start.3 = (bf16[176,1152]{1,0:T(8,128)(2,1)S(1)}, bf16[176,1152]{1,0:T(8,128)(2,1)S(1)}, u32[]{:S(2)}, u32[]{:S(2)}) collective-permute-start(bf16[176,1152]{1,0:T(8,128)(2,1)S(1)} %pad_maximum_fusion.5), channel_id=1, source_target_pairs={{0,8},{4,12},{8,0},{12,4},{16,24},{20,28},{24,16},{28,20},{1,9},{5... | collective-permute-start | bytes 1216520 | tf_op jit(solution)/shard_map/ppermute | solution.py:210
  36.6 3.6 %convolution_convert_fusion.1.refs_0_ = bf16[448,1408]{1,0:T(8,128)(2,1)S(1)} fusion(bf16[448,1408]{1,0:T(8,128)(2,1)} %collective-permute-done.4, bf16[1408,1408]{1,0:T(8,128)(2,1)S(1)} %copy-done.2), kind=kOutput, calls=%fused_computation.4 | convolution fusion | flops 1776918528 | bytes 6488064 | tf_op jit(solution)/shard_map/dot_general | solution.py:200
  40.3 0.3 collective-permute-start.6
  40.7 3.5 %collective-permute-done.7 = bf16[88,1152]{1,0:T(8,128)(2,1)S(1)} collective-permute-done((bf16[88,1152]{1,0:T(8,128)(2,1)S(1)}, bf16[88,1152]{1,0:T(8,128)(2,1)S(1)}, u32[]{:S(2)}, u32[]{:S(2)}) %collective-permute-start.7) | collective-permute-done | bytes 202784 | tf_op jit(solution)/shard_map/ppermute | solution.py:205
  44.2 2.8 %collective-permute-done.3 = bf16[176,1152]{1,0:T(8,128)(2,1)S(1)} collective-permute-done((bf16[176,1152]{1,0:T(8,128)(2,1)S(1)}, bf16[176,1152]{1,0:T(8,128)(2,1)S(1)}, u32[]{:S(2)}, u32[]{:S(2)}) %collective-permute-start.3) | collective-permute-done | bytes 405536 | tf_op jit(solution)/shard_map/ppermute | solution.py:210
  47.0 4.1 %collective-permute-done.6 = bf16[88,1152]{1,0:T(8,128)(2,1)S(1)} collective-permute-done((bf16[88,1152]{1,0:T(8,128)(2,1)S(1)}, bf16[88,1152]{1,0:T(8,128)(2,1)S(1)}, u32[]{:S(2)}, u32[]{:S(2)}) %collective-permute-start.6) | collective-permute-done | bytes 202784 | tf_op jit(solution)/shard_map/ppermute | solution.py:210
  51.1 0.9 constant_dynamic-update-slice_fusion.4
  52.0 1.0 constant_dynamic-update-slice_fusion.3
  53.3 2.0 %collective-permute-start.13 = (bf16[88,768]{1,0:T(8,128)(2,1)S(1)}, bf16[88,768]{1,0:T(8,128)(2,1)S(1)}, u32[]{:S(2)}, u32[]{:S(2)}) collective-permute-start(bf16[88,768]{1,0:T(8,128)(2,1)S(1)} %pad_maximum_fusion.12), channel_id=1, source_target_pairs={{0,1},{1,2},{2,3},{3,0},{4,5},{5,6},{6,7},{7,4},{8,9},{9,10},{10,1... | collective-permute-start | bytes 405512 | tf_op jit(solution)/shard_map/ppermute | solution.py:205
  55.3 1.9 %collective-permute-start.17 = (bf16[88,768]{1,0:T(8,128)(2,1)S(1)}, bf16[88,768]{1,0:T(8,128)(2,1)S(1)}, u32[]{:S(2)}, u32[]{:S(2)}) collective-permute-start(bf16[88,768]{1,0:T(8,128)(2,1)S(1)} %pad_maximum_fusion.12), channel_id=1, source_target_pairs={{0,3},{1,0},{2,1},{3,2},{4,7},{5,4},{6,5},{7,6},{8,11},{9,8},{10,9... | collective-permute-start | bytes 405512 | tf_op jit(solution)/shard_map/ppermute | solution.py:205
  57.3 6.7 %collective-permute-done.12 = bf16[88,1152]{1,0:T(8,128)(2,1)S(1)} collective-permute-done((bf16[88,1152]{1,0:T(8,128)(2,1)S(1)}, bf16[88,1152]{1,0:T(8,128)(2,1)S(1)}, u32[]{:S(2)}, u32[]{:S(2)}) %collective-permute-start.12) | collective-permute-done | bytes 202784 | tf_op jit(solution)/shard_map/ppermute | solution.py:205
  64.0 0.3 collective-permute-start.16
  64.3 1.7 %collective-permute-start.18 = (bf16[88,1152]{1,0:T(8,128)(2,1)S(1)}, bf16[88,1152]{1,0:T(8,128)(2,1)S(1)}, u32[]{:S(2)}, u32[]{:S(2)}) collective-permute-start(bf16[88,1152]{1,0:T(8,128)(2,1)S(1)} %collective-permute-done.7), channel_id=1, source_target_pairs={{0,8},{4,12},{8,0},{12,4},{16,24},{20,28},{24,16},{28,20},{1,9},{5... | collective-permute-start | bytes 608264 | tf_op jit(solution)/shard_map/ppermute | solution.py:210
  66.0 2.3 %convolution_convert_fusion.refs_1_.refs_0_ = bf16[448,1408]{1,0:T(8,128)(2,1)S(1)} fusion(bf16[448,1408]{1,0:T(8,128)(2,1)S(1)} %collective-permute-done.11, bf16[1408,1408]{1,0:T(8,128)(2,1)S(1)} %copy-done.2), kind=kOutput, calls=%fused_computation.3 | convolution fusion | flops 1776918528 | bytes 6488064 | tf_op jit(solution)/shard_map/dot_general | solution.py:200
  68.3 0.3 pad_maximum_fusion.refs_2_
  68.6 0.4 copy-done
  69.0 8.2 %attend_0_0.1 = (bf16[896,1408]{1,0:T(8,128)(2,1)}, bf16[448,384]{1,0:T(8,128)(2,1)S(1)}, bf16[448,384]{1,0:T(8,128)(2,1)S(1)}, bf16[448,128]{1,0:T(8,128)(2,1)S(1)}, bf16[448,128]{1,0:T(8,128)(2,1)S(1)}) custom-call(bf16[448,1408]{1,0:T(8,128)(2,1)S(1)} %convolution_convert_fusion.1.refs_0_, bf16[448,1408]{1,0:T(8,128)(2,1)S(1)} %convolution_convert_fusion.refs_1_.refs_0_, ...), custom_call_target="tpu_custom_call" | custom-call | flops 4550819840 | bytes 5767168 | tf_op jit(solution)/shard_map/attend_0_0/pallas_call | solution.py:158
  77.2 1.8 %collective-permute-done.18 = bf16[88,1152]{1,0:T(8,128)(2,1)S(1)} collective-permute-done((bf16[88,1152]{1,0:T(8,128)(2,1)S(1)}, bf16[88,1152]{1,0:T(8,128)(2,1)S(1)}, u32[]{:S(2)}, u32[]{:S(2)}) %collective-permute-start.18) | collective-permute-done | bytes 202784 | tf_op jit(solution)/shard_map/ppermute | solution.py:210
  79.2 0.3 collective-permute-start.15
  79.6 0.3 collective-permute-start.20
  80.0 1.8 %collective-permute-start.22 = (bf16[176,768]{1,0:T(8,128)(2,1)S(1)}, bf16[176,768]{1,0:T(8,128)(2,1)S(1)}, u32[]{:S(2)}, u32[]{:S(2)}) collective-permute-start(bf16[176,768]{1,0:T(8,128)(2,1)S(1)} %pad_maximum_fusion.8), channel_id=1, source_target_pairs={{0,8},{4,12},{8,0},{12,4},{16,24},{20,28},{24,16},{28,20},{1,9},{5... | collective-permute-start | bytes 811016 | tf_op jit(solution)/shard_map/ppermute | solution.py:210
  81.8 7.0 %collective-permute-done.14 = bf16[88,1152]{1,0:T(8,128)(2,1)S(1)} collective-permute-done((bf16[88,1152]{1,0:T(8,128)(2,1)S(1)}, bf16[88,1152]{1,0:T(8,128)(2,1)S(1)}, u32[]{:S(2)}, u32[]{:S(2)}) %collective-permute-start.14) | collective-permute-done | bytes 202784 | tf_op jit(solution)/shard_map/ppermute | solution.py:205
  88.9 2.4 %collective-permute-done.15 = bf16[88,768]{1,0:T(8,128)(2,1)S(1)} collective-permute-done((bf16[88,768]{1,0:T(8,128)(2,1)S(1)}, bf16[88,768]{1,0:T(8,128)(2,1)S(1)}, u32[]{:S(2)}, u32[]{:S(2)}) %collective-permute-start.15) | collective-permute-done | bytes 135200 | tf_op jit(solution)/shard_map/ppermute | solution.py:205
  91.4 0.3 collective-permute-start.21
  91.7 1.7 %collective-permute-start.23 = (bf16[88,768]{1,0:T(8,128)(2,1)S(1)}, bf16[88,768]{1,0:T(8,128)(2,1)S(1)}, u32[]{:S(2)}, u32[]{:S(2)}) collective-permute-start(bf16[88,768]{1,0:T(8,128)(2,1)S(1)} %collective-permute-done.15), channel_id=1, source_target_pairs={{0,8},{4,12},{8,0},{12,4},{16,24},{20,28},{24,16},{28,20},{1,9},{5... | collective-permute-start | bytes 405512 | tf_op jit(solution)/shard_map/ppermute | solution.py:210
  93.4 0.2 constant_dynamic-update-slice_fusion.11
  93.6 0.2 constant_dynamic-update-slice_fusion.10.refs_1_
  93.8 5.0 %attend_3_0.1 = (bf16[896,1408]{1,0:T(8,128)(2,1)}, bf16[448,384]{1,0:T(8,128)(2,1)S(1)}, bf16[448,128]{1,0:T(8,128)(2,1)S(1)}) custom-call(bf16[448,1408]{1,0:T(8,128)(2,1)S(1)} %convolution_convert_fusion.1.refs_0_, bf16[1408,1152]{1,0:T(8,128)(2,1)S(1)} %constant_dynamic-update-slice_fusion.10.refs_1_, ...), custom_call_target="tpu_custom_call", output_to_operand_aliasing={{0}: (7, {})} | custom-call | flops 2275409920 | bytes 4505600 | tf_op jit(solution)/shard_map/attend_3_0/pallas_call | solution.py:158
  99.4 0.6 collective-permute-start.24
  100.0 5.0 %attend_3_1.1 = (bf16[896,1408]{1,0:T(8,128)(2,1)}, bf16[448,384]{1,0:T(8,128)(2,1)S(1)}, bf16[448,128]{1,0:T(8,128)(2,1)S(1)}) custom-call(bf16[448,1408]{1,0:T(8,128)(2,1)S(1)} %convolution_convert_fusion.refs_1_.refs_0_, bf16[1408,1152]{1,0:T(8,128)(2,1)S(1)} %constant_dynamic-update-slice_fusion.10.refs_1_, ...), custom_call_target="tpu_custom_call", output_to_operand_aliasing={{0}: (7, {})} | custom-call | flops 2275409920 | bytes 4505600 | tf_op jit(solution)/shard_map/attend_3_1/pallas_call | solution.py:158
  105.1 0.2 constant_dynamic-update-slice_fusion.30.refs_2_
  105.3 9.0 %attend_6_0.1 = (bf16[896,1408]{1,0:T(8,128)(2,1)}, bf16[448,384]{1,0:T(8,128)(2,1)S(1)}, bf16[448,384]{1,0:T(8,128)(2,1)S(1)}, bf16[448,128]{1,0:T(8,128)(2,1)S(1)}, bf16[448,128]{1,0:T(8,128)(2,1)S(1)}) custom-call(bf16[448,1408]{1,0:T(8,128)(2,1)S(1)} %convolution_convert_fusion.1.refs_0_, ...), custom_call_target="tpu_custom_call", output_to_operand_aliasing={{0}: (10, {})} | custom-call | flops 4961861632 | bytes 5767168 | tf_op jit(solution)/shard_map/attend_6_0/pallas_call | solution.py:158
  114.3 7.7 %attend_9_0.1 = (bf16[896,1408]{1,0:T(8,128)(2,1)}, bf16[448,384]{1,0:T(8,128)(2,1)}, bf16[448,384]{1,0:T(8,128)(2,1)}, bf16[448,128]{1,0:T(8,128)(2,1)}, bf16[448,128]{1,0:T(8,128)(2,1)}) custom-call(bf16[448,1408]{1,0:T(8,128)(2,1)S(1)} %convolution_convert_fusion.1.refs_0_, ...), custom_call_target="tpu_custom_call", output_to_operand_aliasing={{0}: (10, {})} | custom-call | flops 3170893824 | bytes 4685824 | tf_op jit(solution)/shard_map/attend_9_0/pallas_call | solution.py:158
  (81 shorter events, 2.3 us)
Async XLA Ops:
  0.0 17.6 %copy-start.3 = (s32[1056]{0:T(1024)S(1)}, s32[1056]{0:T(1024)}, u32[]{:S(2)}) copy-start(s32[1056]{0:T(1024)} %constant.64.clone) | copy-start | bytes 12676
  0.0 17.6 %copy-start.4 = (s32[1056]{0:T(1024)S(1)}, s32[1056]{0:T(1024)}, u32[]{:S(2)}) copy-start(s32[1056]{0:T(1024)} %constant.65.clone) | copy-start | bytes 12676
  0.0 17.7 %copy-start.5 = (s32[1056]{0:T(1024)S(1)}, s32[1056]{0:T(1024)}, u32[]{:S(2)}) copy-start(s32[1056]{0:T(1024)} %constant.68) | copy-start | bytes 12676
  1.7 21.3 %collective-permute-start.2 = (bf16[88,1152]{1,0:T(8,128)(2,1)}, bf16[88,1152]{1,0:T(8,128)(2,1)}, u32[]{:S(2)}, u32[]{:S(2)}) collective-permute-start(bf16[88,1152]{1,0:T(8,128)(2,1)} %pad_maximum_fusion.9), channel_id=1, source_target_pairs={{0,1},{1,2},{2,3},{3,0},{4,5},{5,6},{6,7},{7,4},{8,9},{9,10},{10,1... | collective-permute-start | bytes 608264 | tf_op jit(solution)/shard_map/ppermute | solution.py:205
  4.8 20.4 %collective-permute-start = (bf16[88,1152]{1,0:T(8,128)(2,1)}, bf16[88,1152]{1,0:T(8,128)(2,1)}, u32[]{:S(2)}, u32[]{:S(2)}) collective-permute-start(bf16[88,1152]{1,0:T(8,128)(2,1)} %pad_maximum_fusion.9), channel_id=1, source_target_pairs={{0,3},{1,0},{2,1},{3,2},{4,7},{5,4},{6,5},{7,6},{8,11},{9,8},{10,9... | collective-permute-start | bytes 608264 | tf_op jit(solution)/shard_map/ppermute | solution.py:205
  8.5 16.6 %collective-permute-start.1 = (bf16[88,1152]{1,0:T(8,128)(2,1)}, bf16[88,1152]{1,0:T(8,128)(2,1)S(1)}, u32[]{:S(2)}, u32[]{:S(2)}) collective-permute-start(bf16[88,1152]{1,0:T(8,128)(2,1)} %pad_maximum_fusion.10), channel_id=1, source_target_pairs={{0,1},{1,2},{2,3},{3,0},{4,5},{5,6},{6,7},{7,4},{8,9},{9,10},{10,1... | collective-permute-start | bytes 608264 | tf_op jit(solution)/shard_map/ppermute | solution.py:205
  8.5 31.8 %collective-permute-start.8 = (bf16[88,1152]{1,0:T(8,128)(2,1)}, bf16[88,1152]{1,0:T(8,128)(2,1)S(1)}, u32[]{:S(2)}, u32[]{:S(2)}) collective-permute-start(bf16[88,1152]{1,0:T(8,128)(2,1)} %pad_maximum_fusion.10), channel_id=1, source_target_pairs={{0,3},{1,0},{2,1},{3,2},{4,7},{5,4},{6,5},{7,6},{8,11},{9,8},{10,9... | collective-permute-start | bytes 608264 | tf_op jit(solution)/shard_map/ppermute | solution.py:205
  17.5 3.8 %copy-start.1 = (bf16[352,4224]{1,0:T(8,128)(2,1)S(1)}, bf16[352,4224]{1,0:T(8,128)(2,1)}, u32[]{:S(2)}) copy-start(bf16[352,4224]{1,0:T(8,128)(2,1)} %param.9) | copy-start | bytes 8921092
  17.6 19.0 %collective-permute-start.4 = (bf16[448,1408]{1,0:T(8,128)(2,1)}, bf16[448,1408]{1,0:T(8,128)(2,1)}, u32[]{:S(2)}, u32[]{:S(2)}) collective-permute-start(bf16[448,1408]{1,0:T(8,128)(2,1)} %get-tuple-element.94), channel_id=1, source_target_pairs={{0,4},{4,8},{8,12},{12,16},{16,20},{20,24},{24,28},{28,0},{1,5},{5... | collective-permute-start | bytes 3784712 | tf_op jit(solution)/shard_map/ppermute | solution.py:205
  17.8 4.3 %copy-start.6 = (s32[8,1,2,2]{0,3,2,1:T(2,128)S(1)}, s32[8,1,2,2]{0,3,2,1:T(2,128)}, u32[]{:S(2)}) copy-start(s32[8,1,2,2]{0,3,2,1:T(2,128)} %param.10) | copy-start | bytes 388
  23.0 41.2 %collective-permute-start.11 = (bf16[448,1408]{1,0:T(8,128)(2,1)}, bf16[448,1408]{1,0:T(8,128)(2,1)S(1)}, u32[]{:S(2)}, u32[]{:S(2)}) collective-permute-start(bf16[448,1408]{1,0:T(8,128)(2,1)} %get-tuple-element.115), channel_id=1, source_target_pairs={{0,16},{4,20},{8,24},{12,28},{16,0},{20,4},{24,8},{28,12},{1,17},{... | collective-permute-start | bytes 3784712 | tf_op jit(solution)/shard_map/ppermute | solution.py:205
  25.0 11.6 %copy-start.2 = (bf16[1408,1408]{1,0:T(8,128)(2,1)S(1)}, bf16[1408,1408]{1,0:T(8,128)(2,1)}, u32[]{:S(2)}) copy-start(bf16[1408,1408]{1,0:T(8,128)(2,1)} %fusion) | copy-start | bytes 11894788
  25.1 9.7 %collective-permute-start.5 = (bf16[88,1152]{1,0:T(8,128)(2,1)}, bf16[88,1152]{1,0:T(8,128)(2,1)S(1)}, u32[]{:S(2)}, u32[]{:S(2)}) collective-permute-start(bf16[88,1152]{1,0:T(8,128)(2,1)} %collective-permute-done.2), channel_id=1, source_target_pairs={{0,1},{1,2},{2,3},{3,0},{4,5},{5,6},{6,7},{7,4},{8,9},{9,10},{10,1... | collective-permute-start | bytes 608264 | tf_op jit(solution)/shard_map/ppermute | solution.py:205
  25.1 15.1 %collective-permute-start.9 = (bf16[88,1152]{1,0:T(8,128)(2,1)S(1)}, bf16[88,1152]{1,0:T(8,128)(2,1)S(1)}, u32[]{:S(2)}, u32[]{:S(2)}) collective-permute-start(bf16[88,1152]{1,0:T(8,128)(2,1)S(1)} %pad_maximum_fusion.11), channel_id=1, source_target_pairs={{0,1},{1,2},{2,3},{3,0},{4,5},{5,6},{6,7},{7,4},{8,9},{9,10},{10,1... | collective-permute-start | bytes 608264 | tf_op jit(solution)/shard_map/ppermute | solution.py:205
  34.7 12.2 %collective-permute-start.3 = (bf16[176,1152]{1,0:T(8,128)(2,1)S(1)}, bf16[176,1152]{1,0:T(8,128)(2,1)S(1)}, u32[]{:S(2)}, u32[]{:S(2)}) collective-permute-start(bf16[176,1152]{1,0:T(8,128)(2,1)S(1)} %pad_maximum_fusion.5), channel_id=1, source_target_pairs={{0,8},{4,12},{8,0},{12,4},{16,24},{20,28},{24,16},{28,20},{1,9},{5... | collective-permute-start | bytes 1216520 | tf_op jit(solution)/shard_map/ppermute | solution.py:210
  36.5 7.7 %collective-permute-start.7 = (bf16[88,1152]{1,0:T(8,128)(2,1)S(1)}, bf16[88,1152]{1,0:T(8,128)(2,1)S(1)}, u32[]{:S(2)}, u32[]{:S(2)}) collective-permute-start(bf16[88,1152]{1,0:T(8,128)(2,1)S(1)} %collective-permute-done.1), channel_id=1, source_target_pairs={{0,1},{1,2},{2,3},{3,0},{4,5},{5,6},{6,7},{7,4},{8,9},{9,10},{10,1... | collective-permute-start | bytes 608264 | tf_op jit(solution)/shard_map/ppermute | solution.py:205
  40.3 10.8 %collective-permute-start.6 = (bf16[88,1152]{1,0:T(8,128)(2,1)S(1)}, bf16[88,1152]{1,0:T(8,128)(2,1)S(1)}, u32[]{:S(2)}, u32[]{:S(2)}) collective-permute-start(bf16[88,1152]{1,0:T(8,128)(2,1)S(1)} %collective-permute-done.5), channel_id=1, source_target_pairs={{0,8},{4,12},{8,0},{12,4},{16,24},{20,28},{24,16},{28,20},{1,9},{5... | collective-permute-start | bytes 608264 | tf_op jit(solution)/shard_map/ppermute | solution.py:210
  53.1 15.2 %collective-permute-start.10 = (bf16[528,1152]{1,0:T(8,128)(2,1)S(1)}, bf16[528,1152]{1,0:T(8,128)(2,1)S(1)}, u32[]{:S(2)}, u32[]{:S(2)}) collective-permute-start(bf16[528,1152]{1,0:T(8,128)(2,1)S(1)} %constant_dynamic-update-slice_fusion), channel_id=1, source_target_pairs={{0,4},{4,0},{8,12},{12,8},{16,20},{20,16},{24,28},{28,24},{1,5},{5... | collective-permute-start | bytes 3649544 | tf_op jit(solution)/shard_map/ppermute | solution.py:210
  53.3 10.7 %collective-permute-start.12 = (bf16[88,1152]{1,0:T(8,128)(2,1)S(1)}, bf16[88,1152]{1,0:T(8,128)(2,1)S(1)}, u32[]{:S(2)}, u32[]{:S(2)}) collective-permute-start(bf16[88,1152]{1,0:T(8,128)(2,1)S(1)} %pad_maximum_fusion.11), channel_id=1, source_target_pairs={{0,3},{1,0},{2,1},{3,2},{4,7},{5,4},{6,5},{7,6},{8,11},{9,8},{10,9... | collective-permute-start | bytes 608264 | tf_op jit(solution)/shard_map/ppermute | solution.py:205
  53.3 11.0 %collective-permute-start.13 = (bf16[88,768]{1,0:T(8,128)(2,1)S(1)}, bf16[88,768]{1,0:T(8,128)(2,1)S(1)}, u32[]{:S(2)}, u32[]{:S(2)}) collective-permute-start(bf16[88,768]{1,0:T(8,128)(2,1)S(1)} %pad_maximum_fusion.12), channel_id=1, source_target_pairs={{0,1},{1,2},{2,3},{3,0},{4,5},{5,6},{6,7},{7,4},{8,9},{9,10},{10,1... | collective-permute-start | bytes 405512 | tf_op jit(solution)/shard_map/ppermute | solution.py:205
  55.3 21.8 %collective-permute-start.17 = (bf16[88,768]{1,0:T(8,128)(2,1)S(1)}, bf16[88,768]{1,0:T(8,128)(2,1)S(1)}, u32[]{:S(2)}, u32[]{:S(2)}) collective-permute-start(bf16[88,768]{1,0:T(8,128)(2,1)S(1)} %pad_maximum_fusion.12), channel_id=1, source_target_pairs={{0,3},{1,0},{2,1},{3,2},{4,7},{5,4},{6,5},{7,6},{8,11},{9,8},{10,9... | collective-permute-start | bytes 405512 | tf_op jit(solution)/shard_map/ppermute | solution.py:205
  64.0 13.2 %collective-permute-start.16 = (bf16[176,1152]{1,0:T(8,128)(2,1)S(1)}, bf16[176,1152]{1,0:T(8,128)(2,1)S(1)}, u32[]{:S(2)}, u32[]{:S(2)}) collective-permute-start(bf16[176,1152]{1,0:T(8,128)(2,1)S(1)} %pad_maximum_fusion.6), channel_id=1, source_target_pairs={{0,8},{4,12},{8,0},{12,4},{16,24},{20,28},{24,16},{28,20},{1,9},{5... | collective-permute-start | bytes 1216520 | tf_op jit(solution)/shard_map/ppermute | solution.py:210
  64.3 14.7 %collective-permute-start.18 = (bf16[88,1152]{1,0:T(8,128)(2,1)S(1)}, bf16[88,1152]{1,0:T(8,128)(2,1)S(1)}, u32[]{:S(2)}, u32[]{:S(2)}) collective-permute-start(bf16[88,1152]{1,0:T(8,128)(2,1)S(1)} %collective-permute-done.7), channel_id=1, source_target_pairs={{0,8},{4,12},{8,0},{12,4},{16,24},{20,28},{24,16},{28,20},{1,9},{5... | collective-permute-start | bytes 608264 | tf_op jit(solution)/shard_map/ppermute | solution.py:210
  68.3 0.7 copy-start
  79.1 12.2 %collective-permute-start.19 = (bf16[528,1152]{1,0:T(8,128)(2,1)S(1)}, bf16[528,1152]{1,0:T(8,128)(2,1)S(1)}, u32[]{:S(2)}, u32[]{:S(2)}) collective-permute-start(bf16[528,1152]{1,0:T(8,128)(2,1)S(1)} %constant_dynamic-update-slice_fusion.5), channel_id=1, source_target_pairs={{0,4},{4,0},{8,12},{12,8},{16,20},{20,16},{24,28},{28,24},{1,5},{5... | collective-permute-start | bytes 3649544 | tf_op jit(solution)/shard_map/ppermute | solution.py:210
  79.2 9.7 %collective-permute-start.14 = (bf16[88,1152]{1,0:T(8,128)(2,1)S(1)}, bf16[88,1152]{1,0:T(8,128)(2,1)S(1)}, u32[]{:S(2)}, u32[]{:S(2)}) collective-permute-start(bf16[88,1152]{1,0:T(8,128)(2,1)S(1)} %collective-permute-done.9), channel_id=1, source_target_pairs={{0,1},{1,2},{2,3},{3,0},{4,5},{5,6},{6,7},{7,4},{8,9},{9,10},{10,1... | collective-permute-start | bytes 608264 | tf_op jit(solution)/shard_map/ppermute | solution.py:205
  79.2 12.1 %collective-permute-start.15 = (bf16[88,768]{1,0:T(8,128)(2,1)S(1)}, bf16[88,768]{1,0:T(8,128)(2,1)S(1)}, u32[]{:S(2)}, u32[]{:S(2)}) collective-permute-start(bf16[88,768]{1,0:T(8,128)(2,1)S(1)} %collective-permute-done.13), channel_id=1, source_target_pairs={{0,1},{1,2},{2,3},{3,0},{4,5},{5,6},{6,7},{7,4},{8,9},{9,10},{10,1... | collective-permute-start | bytes 405512 | tf_op jit(solution)/shard_map/ppermute | solution.py:205
  79.6 19.3 %collective-permute-start.20 = (bf16[176,1152]{1,0:T(8,128)(2,1)S(1)}, bf16[176,1152]{1,0:T(8,128)(2,1)S(1)}, u32[]{:S(2)}, u32[]{:S(2)}) collective-permute-start(bf16[176,1152]{1,0:T(8,128)(2,1)S(1)} %pad_maximum_fusion.7), channel_id=1, source_target_pairs={{0,16},{4,20},{8,24},{12,28},{16,0},{20,4},{24,8},{28,12},{1,17},{... | collective-permute-start | bytes 1216520 | tf_op jit(solution)/shard_map/ppermute | solution.py:210
  80.0 18.8 %collective-permute-start.22 = (bf16[176,768]{1,0:T(8,128)(2,1)S(1)}, bf16[176,768]{1,0:T(8,128)(2,1)S(1)}, u32[]{:S(2)}, u32[]{:S(2)}) collective-permute-start(bf16[176,768]{1,0:T(8,128)(2,1)S(1)} %pad_maximum_fusion.8), channel_id=1, source_target_pairs={{0,8},{4,12},{8,0},{12,4},{16,24},{20,28},{24,16},{28,20},{1,9},{5... | collective-permute-start | bytes 811016 | tf_op jit(solution)/shard_map/ppermute | solution.py:210
  91.4 7.5 %collective-permute-start.21 = (bf16[88,1152]{1,0:T(8,128)(2,1)S(1)}, bf16[88,1152]{1,0:T(8,128)(2,1)S(1)}, u32[]{:S(2)}, u32[]{:S(2)}) collective-permute-start(bf16[88,1152]{1,0:T(8,128)(2,1)S(1)} %collective-permute-done.14), channel_id=1, source_target_pairs={{0,16},{4,20},{8,24},{12,28},{16,0},{20,4},{24,8},{28,12},{1,17},{... | collective-permute-start | bytes 608264 | tf_op jit(solution)/shard_map/ppermute | solution.py:210
  91.7 7.2 %collective-permute-start.23 = (bf16[88,768]{1,0:T(8,128)(2,1)S(1)}, bf16[88,768]{1,0:T(8,128)(2,1)S(1)}, u32[]{:S(2)}, u32[]{:S(2)}) collective-permute-start(bf16[88,768]{1,0:T(8,128)(2,1)S(1)} %collective-permute-done.15), channel_id=1, source_target_pairs={{0,8},{4,12},{8,0},{12,4},{16,24},{20,28},{24,16},{28,20},{1,9},{5... | collective-permute-start | bytes 405512 | tf_op jit(solution)/shard_map/ppermute | solution.py:210
  99.2 5.9 %collective-permute-start.25 = (bf16[528,1152]{1,0:T(8,128)(2,1)S(1)}, bf16[528,1152]{1,0:T(8,128)(2,1)S(1)}, u32[]{:S(2)}, u32[]{:S(2)}) collective-permute-start(bf16[528,1152]{1,0:T(8,128)(2,1)S(1)} %get-tuple-element.205), channel_id=1, source_target_pairs={{0,4},{4,0},{8,12},{12,8},{16,20},{20,16},{24,28},{28,24},{1,5},{5... | collective-permute-start | bytes 3649544 | tf_op jit(solution)/shard_map/ppermute | solution.py:210
  99.4 5.6 %collective-permute-start.24 = (bf16[528,768]{1,0:T(8,128)(2,1)S(1)}, bf16[528,768]{1,0:T(8,128)(2,1)S(1)}, u32[]{:S(2)}, u32[]{:S(2)}) collective-permute-start(bf16[528,768]{1,0:T(8,128)(2,1)S(1)} %get-tuple-element.213), channel_id=1, source_target_pairs={{0,4},{4,0},{8,12},{12,8},{16,20},{20,16},{24,28},{28,24},{1,5},{5... | collective-permute-start | bytes 2433032 | tf_op jit(solution)/shard_map/ppermute | solution.py:210

commit v3 on v2

v3 whole, which is shorter than its diff:
```python
import functools
import math

import jax
import jax.numpy as jnp
import numpy as np
from jax import lax
from jax.experimental import pallas as pl
from jax.experimental.pallas import tpu as pltpu
from jax.sharding import PartitionSpec as P

HEADS = 16
LANE = 128
FAR_BELOW = -1e30
PIECES = 4
BOUNDS = ((0, 3), (3, 6), (6, 9), (9, 11))
SWAPS = (2, 2, 2, 4)


def heads_of(bounds, head_dim):
    found, h = [], 0
    for _, t1 in bounds:
        end = min(HEADS, t1 * LANE // head_dim)
        found.append((h, end))
        h = end
    return found


def pick_kernel(route_ref, rank_ref, tokens, near, far, sems):
    rows = near.shape[0]
    copies = []
    for r, to in enumerate((near, far)):
        start = pl.multiple_of(route_ref[rank_ref[0], 0, r] * rows, rows)
        copies.append(pltpu.make_async_copy(tokens.at[pl.ds(start, rows)], to, sems.at[r]))
    for c in copies:
        c.start()
    for c in copies:
        c.wait()


def picked(balance, rank, tokens):
    rows, width = tokens.shape
    anywhere = pl.BlockSpec(memory_space=pl.ANY)
    scalars = pl.BlockSpec(memory_space=pltpu.SMEM)
    half = jax.ShapeDtypeStruct((rows // 2, width), tokens.dtype)
    return pl.pallas_call(
        pick_kernel,
        out_shape=[half, half],
        in_specs=[scalars, scalars, anywhere],
        out_specs=[pl.BlockSpec(memory_space=pltpu.VMEM)] * 2,
        scratch_shapes=[pltpu.SemaphoreType.DMA((2,))],
        name="pick",
    )(balance, rank, tokens)


def attend_kernel(t0, t1, h0, h1, hd, bundles, earlier, *refs):
    nb = len(bundles)
    refs = list(refs)
    take = lambda n: [refs.pop(0) for _ in range(n)]
    x_refs = take(nb)
    w_ref, lengths_ref, route_ref, source_ref = take(4)
    later = t0 > 0
    pc_in, oc_in = (take(nb), take(nb)) if later else (None, None)
    last = earlier is not None
    if last:
        before = take(len(earlier))
        out = refs.pop(0)
        proj, done, sems, own_sems = refs
    else:
        done_refs, pc_out, oc_out = take(nb), take(nb), take(nb)
        (proj,) = refs
    rows = x_refs[0].shape[0]
    nt = t1 - t0
    base = t0 - 1
    first_tile = h0 * hd // LANE
    c = math.log2(math.e) / math.sqrt(hd)
    copies = []
    if last:
        for j, (bundle, tile) in enumerate(earlier):
            to = out.at[pl.ds(bundle * rows, rows), pl.ds(tile * LANE, before[j].shape[1])]
            copies.append(pltpu.make_async_copy(before[j], to, sems.at[j]))
            copies[-1].start()
    for i, bundle in enumerate(bundles):
        p = jnp.dot(x_refs[i][...], w_ref[...], preferred_element_type=jnp.float32).astype(jnp.bfloat16)
        for part in range(3):
            proj[i, part, :, LANE:] = p[:, part * nt * LANE : (part + 1) * nt * LANE]
            if later:
                proj[i, part, :, :LANE] = pc_in[i][:, part * LANE : (part + 1) * LANE]
            if not last:
                pc_out[i][:, part * LANE : (part + 1) * LANE] = proj[i, part, :, nt * LANE :]
        source = source_ref[bundle]
        split = lengths_ref[source, 0, route_ref[source, 0, bundle], 0]
        made = {}

        def tags(w, at, a, b):
            if (w, at, a, b) not in made:
                late = lax.broadcasted_iota(jnp.int32, (rows, w), 0) >= split
                lane = lax.broadcasted_iota(jnp.int32, (rows, w), 1)
                one, two = jnp.where(late, b, a), jnp.where(late, a, b)
                both = jnp.where(lane == at, one, jnp.where(lane == at + 1, two, 0.0))
                made[(w, at, a, b)] = both.astype(jnp.bfloat16)
            return made[(w, at, a, b)]

        def place_of(h):
            lo, hi = h * hd, (h + 1) * hd
            s0, s1 = lo // LANE, -(-hi // LANE)
            w = (s1 - s0) * LANE
            a, b = lo - s0 * LANE, hi - s0 * LANE
            at = 0 if a >= 2 else w - 2
            lane = lax.broadcasted_iota(jnp.int32, (rows, w), 1)
            return lo, hi, s0, s1, w, at, lane, (lane >= a) & (lane < b), slice((s0 - base) * LANE, (s1 - base) * LANE)

        def scores(h):
            _, _, _, _, w, at, _, own, cols = place_of(h)
            q = jnp.where(own, proj[i, 0, :, cols], tags(w, at, 1.0, 0.0))
            k = jnp.where(own, proj[i, 1, :, cols], tags(w, at, 0.0, FAR_BELOW))
            return lax.dot_general(q, k, (((1,), (1,)), ((), ())), preferred_element_type=jnp.float32)

        partial = oc_in[i][...] if later else None
        upcoming = scores(h0)
        for h in range(h0, h1):
            lo, hi, s0, s1, w, at, lane, own, cols = place_of(h)
            s = upcoming
            if h + 1 < h1:
                upcoming = scores(h + 1)
            ones = jnp.where(lane == at, 1.0, 0.0).astype(jnp.bfloat16)
            v = jnp.where(own, proj[i, 2, :, cols], ones)
            m = jnp.max(s, axis=1, keepdims=True) * c
            e = jnp.exp2(s * c - m).astype(jnp.bfloat16)
            o = jnp.dot(e, v, preferred_element_type=jnp.float32)
            o = (o / o[:, at : at + 1]).astype(jnp.bfloat16)
            for t in range(s0, s1):
                piece = o[:, (t - s0) * LANE : (t - s0 + 1) * LANE]
                start = max(lo - t * LANE, 0)
                if start > 0:
                    lanes = lax.broadcasted_iota(jnp.int32, (rows, LANE), 1)
                    piece = jnp.where(lanes < start, partial, piece)
                if hi >= (t + 1) * LANE:
                    j = t - first_tile
                    if last:
                        done[i, :, j * LANE : (j + 1) * LANE] = piece
                    else:
                        done_refs[i][:, j * LANE : (j + 1) * LANE] = piece
                    partial = None
                else:
                    partial = piece
        if last:
            to = out.at[pl.ds(bundle * rows, rows), pl.ds(first_tile * LANE, done.shape[2])]
            copies.append(pltpu.make_async_copy(done.at[i], to, own_sems.at[i]))
            copies[-1].start()
        else:
            oc_out[i][...] = jnp.zeros((rows, LANE), jnp.bfloat16) if partial is None else partial
    for copy in copies:
        copy.wait()


def attend(t0, t1, h0, h1, bundles, xs, w, info, carry, finished):
    rows, d = xs[0].shape
    hd = d // HEADS
    nb, nt = len(bundles), t1 - t0
    first_tile = h0 * hd // LANE
    tiles = h1 * hd // LANE - first_tile
    last = t1 * LANE == d
    inside = pl.BlockSpec(memory_space=pltpu.VMEM)
    anywhere = pl.BlockSpec(memory_space=pl.ANY)
    scalars = pl.BlockSpec(memory_space=pltpu.SMEM)
    operands = [*xs, w, *info]
    specs = [inside] * (nb + 1) + [scalars] * 3
    if t0 > 0:
        operands += [carry[b][0] for b in bundles] + [carry[b][1] for b in bundles]
        specs += [inside] * (2 * nb)
    shape = lambda r, c: jax.ShapeDtypeStruct((r, c), jnp.bfloat16)
    scratch = [pltpu.VMEM((nb, 3, rows, (nt + 1) * LANE), jnp.bfloat16)]
    if last:
        earlier = [(b, tile) for b, tile, _ in finished]
        operands += [x for _, _, x in finished]
        specs += [anywhere] * len(finished)
        out_shape, out_specs = shape(2 * rows, d), anywhere
        scratch += [
            pltpu.VMEM((nb, rows, tiles * LANE), jnp.bfloat16),
            pltpu.SemaphoreType.DMA((len(finished),)),
            pltpu.SemaphoreType.DMA((nb,)),
        ]
    else:
        earlier = None
        out_shape = [shape(rows, tiles * LANE)] * nb + [shape(rows, 3 * LANE)] * nb + [shape(rows, LANE)] * nb
        out_specs = [inside] * (3 * nb)
    res = pl.pallas_call(
        functools.partial(attend_kernel, t0, t1, h0, h1, hd, bundles, earlier),
        out_shape=out_shape,
        in_specs=specs,
        out_specs=out_specs,
        scratch_shapes=scratch,
        compiler_params=pltpu.CompilerParams(vmem_limit_bytes=16 * 2**20),
        name=f"attend_{t0}_{bundles[0]}",
    )(*operands)
    if last:
        return res
    for i, b in enumerate(bundles):
        carry[b] = (res[nb + i], res[2 * nb + i])
        finished.append((b, first_tile, res[i]))
    return res[2 * nb]


ARRIVAL = ((1, 0), (3, 0), (1, 2), (3, 2), (2, 0), (2, 2))


def quarter_of(rank):
    return ((((rank >> 2) ^ (rank >> 1)) & 1) << 1) | (rank & 1)


def source_columns(rank, column, shard_rows, shards):
    quarter = shard_rows // PIECES
    step = np.array([s for core in (0, 1) for s, _ in ARRIVAL for _ in range(quarter)])
    flip = np.array([core | across for core in (0, 1) for _, across in ARRIVAL for _ in range(quarter)])
    row = np.array(list(range(quarter)) * (2 * len(ARRIVAL)))
    rest = ((column - step) % shards) * shard_rows + (quarter_of(rank) ^ flip) * quarter + row
    own = column * shard_rows + np.arange(shard_rows)
    return jnp.concatenate([own, rest]).astype(jnp.int32)


def reordered(x, place):
    return jnp.dot(x, place, preferred_element_type=jnp.float32).astype(jnp.bfloat16)


def shifted(x, axis, by):
    n = lax.axis_size(axis)
    return lax.ppermute(x, axis, [(i, (i + by) % n) for i in range(n)])


def swapped(x, mask):
    n = lax.axis_size("dp")
    return lax.ppermute(x, "dp", [(i, i ^ mask) for i in range(n)])


def fence(*values):
    return lax.optimization_barrier(values)


def stacked(*xs):
    return jnp.concatenate(xs, axis=0)


def on_device(tokens, qkv_weight, image_lengths, balance):
    ranks = lax.axis_size("dp")
    shards = lax.axis_size("fsdp")
    rank = lax.axis_index("dp")
    column = lax.axis_index("fsdp")
    rows, width = tokens.shape
    shard_rows = qkv_weight.shape[0]
    quarter = shard_rows // PIECES
    hd = width // HEADS
    sources = jnp.stack([(rank - 1) % ranks, (rank - ranks // 2) % ranks]).astype(jnp.int32)
    info = (image_lengths, balance, sources)
    columns = source_columns(rank, column, shard_rows, shards)
    quarter_start = quarter_of(rank) * quarter

    def columns_matrix():
        return (jnp.arange(width, dtype=jnp.int32)[:, None] == columns[None, :]).astype(jnp.bfloat16)

    def of_chunk(w, t0, t1):
        return jnp.concatenate([w[:, p * width + t0 * LANE : p * width + t1 * LANE] for p in range(3)], axis=1)

    def payload(w, *chunks):
        own = lax.dynamic_slice_in_dim(w, quarter_start, quarter, 0)
        return jnp.concatenate(fence(*[of_chunk(own, *BOUNDS[c]) for c in chunks]), axis=1)

    def up(x):
        return shifted(x, "fsdp", 1)

    def down(x):
        return shifted(x, "fsdp", shards - 1)

    def across(c, *xs):
        return swapped(stacked(*xs) if len(xs) > 1 else xs[0], SWAPS[c])

    spans = [(*b, *h) for b, h in zip(BOUNDS, heads_of(BOUNDS, hd))]
    carry = [None, None]
    finished = []
    w = qkv_weight
    n_a, n_b, n_c, n_d = [3 * (t1 - t0) * LANE for t0, t1 in BOUNDS]

    pab = payload(w, 0, 1)
    abp, abm = up(pab), down(pab)
    tokens, w, _ = fence(tokens, w, pab)
    near_first = balance[rank, 0, 0] == 0
    low, high = tokens[: rows // 2], tokens[rows // 2 :]
    near_out, far_out = jnp.where(near_first, low, high), jnp.where(near_first, high, low)
    cut = (rows // 6 // 16 * 16, rows // 3 // 16 * 16)
    far_1 = shifted(far_out[: cut[0]], "dp", ranks // 2)
    near_in = shifted(near_out, "dp", 1)
    pcd = payload(w, 2, 3)

    abp, pcd, w = fence(abp, pcd, w)
    ab2 = up(abp)
    own_a = of_chunk(w, *BOUNDS[0])
    place = columns_matrix()

    abp, abm, pcd, own_a, place, w, far_out = fence(abp, abm, pcd, own_a, place, w, far_out)
    cdp = up(pcd)
    ax = across(0, abp[:, :n_a], abm[:, :n_a])
    far_2 = shifted(far_out[cut[0] : cut[1]], "dp", ranks // 2)
    own_b = of_chunk(w, *BOUNDS[1])

    near, own_b, place = fence(near_in, own_b, place)
    near = reordered(near, place)

    near, ab2, pcd, w = fence(near, ab2, pcd, w)
    cdm = down(pcd)
    ay = across(0, ab2[:, :n_a])
    own_c = of_chunk(w, *BOUNDS[2])

    ax, abp, abm, ab2, own_c, w, far_1 = fence(ax, abp, abm, ab2, own_c, w, far_1)
    bx = across(1, abp[:, n_a:], abm[:, n_a:], ab2[:, n_a:])
    own_d = of_chunk(w, *BOUNDS[3])

    ay, ax, abp, abm, ab2, own_d, cdp, far_out = fence(ay, ax, abp, abm, ab2, own_d, cdp, far_out)
    far_3 = shifted(far_out[cut[1] :], "dp", ranks // 2)
    cd2 = up(cdp)
    both_a = stacked(abp[:, :n_a], abm[:, :n_a], ax, ab2[:, :n_a], ay)
    ac = swapped(both_a, 1)

    ac, both_a, own_a, near, far_2, cdm = fence(ac, both_a, own_a, near, far_2, cdm)
    wa = stacked(own_a, both_a, ac)
    out = attend(*spans[0], (0,), (near,), wa, info, carry, finished)

    out, cdp, cdm, far_1, far_2, far_3 = fence(out, cdp, cdm, far_1, far_2, far_3)
    dx_1 = across(3, cdp[:, n_c:], cdm[:, n_c:])
    cx_1 = across(2, cdp[:, :n_c], cdm[:, :n_c])
    far = reordered(stacked(far_1, far_2, far_3), place)

    bx, far, cd2 = fence(bx, far, cd2)
    dx_2 = across(3, cd2[:, n_c:])
    cx_2 = across(2, cd2[:, :n_c])
    both_b = stacked(abp[:, n_a:], abm[:, n_a:], bx[: 2 * quarter], ab2[:, n_a:], bx[2 * quarter :])
    bc = swapped(both_b, 1)
    out = attend(*spans[0], (1,), (far,), wa, info, carry, finished)

    out, bc, both_b, own_b, cx_1, dx_1, cdp = fence(out, bc, both_b, own_b, cx_1, dx_1, cdp)
    wb = stacked(own_b, both_b, bc)
    out = attend(*spans[1], (0,), (near,), wb, info, carry, finished)

    out, cx_1, dx_1, cx_2, dx_2, cdp, cdm, cd2 = fence(out, cx_1, dx_1, cx_2, dx_2, cdp, cdm, cd2)
    both_c = stacked(cdp[:, :n_c], cdm[:, :n_c], cx_1, cd2[:, :n_c], cx_2)
    cc = swapped(both_c, 1)
    both_d = stacked(cdp[:, n_c:], cdm[:, n_c:], dx_1, cd2[:, n_c:], dx_2)
    dc = swapped(both_d, 1)
    out = attend(*spans[1], (1,), (far,), wb, info, carry, finished)

    wc = stacked(own_c, both_c, cc)
    out = attend(*spans[2], (0, 1), (near, far), wc, info, carry, finished)
    wd = stacked(own_d, both_d, dc)
    out = attend(*spans[3], (0, 1), (near, far), wd, info, carry, finished)
    return out


def solution(mesh):
    in_specs = (
        P(("dp", "fsdp"), None),
        P("fsdp", None),
        P(None, "fsdp", None, None),
        P(None, "fsdp", None),
    )
    return jax.shard_map(
        on_device, mesh=mesh, in_specs=in_specs, out_specs=P(("dp", "fsdp"), None), check_vma=False
    )
```

time: 123 us -> 111 us (0.902)
  waiting for transfers between devices: 36.7 us -> 22.2 us
  local copies, waits for them, and re-layouts: 8.05 us -> 15.6 us
  Pallas kernels: 38.9 us -> 32.1 us
  other arithmetic: 7.88 us -> 9.24 us
  matrix products: 5.81 us -> 7.07 us
    ppermute x14 -> x10, waiting for transfers between devices: 28 us -> 17.4 us  [shifted(): return lax.ppermute(x, axis, [(i, (i + by) % n) for i in range(n)])]
    slice x0 -> x16, local copies, waits for them, and re-layouts: none -> 4.82 us  [the longest x4 1.99 us: on_device(): bx = across(1, abp[:, n_a:], abm[:, n_a:], ab2[:, n_a:])]
    pallas_call x1 -> x0, Pallas kernels: 3.92 us -> none  [picked(): pl.pallas_call(pick_kernel, out_shape=[half, half], in_specs=[scalars, sc...]
    ppermute x12 -> x11, waiting for transfers between devices: 8.69 us -> 4.79 us  [swapped(): return lax.ppermute(x, 'dp', [(i, i ^ mask) for i in range(n)])]
    select_n x0 -> x1, other arithmetic: none -> 3.61 us  [on_device(): jnp.where(near_first, high, low)]
    pallas_call x5 -> x6, Pallas kernels: 34.9 us -> 32.1 us  [attend(): pl.pallas_call(functools.partial(attend_kernel, t0, t1, h0, h1, hd, bundl...]
    concatenate x7 -> x8, local copies, waits for them, and re-layouts: 0.52 us -> 2.65 us  [stacked(): return jnp.concatenate(xs, axis=0)]
    unnamed x36 -> x65, local copies, waits for them, and re-layouts: 4.58 us -> 6.64 us
  transfers between devices with their start and end apart: 26 -> 21, of which waited for: 8 -> 9; matrix products, arithmetic and copies ran while one was open for 16% -> 23% of each run, Pallas kernels for 18% -> 16%
where the time goes in v3:
time: 111 us; the launch traced here: 110 us
  Pallas kernels  32.1 us (29%)
  starting transfers between devices  23.5 us (21%)
  waiting for transfers between devices  22.2 us (20%)
  local copies, waits for them, and re-layouts  15.6 us (14%)
  other arithmetic  9.24 us (8%)
  matrix products  7.07 us (6%)
    pallas_call x6, Pallas kernels, attend(): pl.pallas_call(functools.partial(attend_kernel, t0, t1, h0, h1, hd, bundl...  32.1 us
    ppermute x10, waiting for transfers between devices, shifted(): return lax.ppermute(x, axis, [(i, (i + by) % n) for i in range(n)])  17.4 us
    ppermute x10, starting transfers between devices, shifted(): return lax.ppermute(x, axis, [(i, (i + by) % n) for i in range(n)])  13.7 us
    ppermute x11, starting transfers between devices, swapped(): return lax.ppermute(x, 'dp', [(i, i ^ mask) for i in range(n)])  9.86 us
    dot_general x2, matrix products, reordered(): jnp.dot(x, place, preferred_element_type=jnp.float32).astype(jnp.bfloat16)  7.07 us
    unnamed x65, local copies, waits for them, and re-layouts  6.64 us
    ppermute x11, waiting for transfers between devices, swapped(): return lax.ppermute(x, 'dp', [(i, i ^ mask) for i in range(n)])  4.79 us
    select_n x1, other arithmetic, on_device(): jnp.where(near_first, high, low)  3.61 us
  transfers between devices with their start and end apart: 21, of which 9 were waited for; matrix products, arithmetic and copies ran while one was open for 23% of the time, Pallas kernels for 16%

profile of v3, /device:TPU:0, one launch (start us, length us, event | category | flops | bytes accessed | tf_op | source)
XLA Modules:
  0.0 110.4 jit_solution(2136824239748697608)
XLA Ops:
  0.0 1.1 fusion.17
  1.2 3.1 %collective-permute-start.1 = (bf16[88,2304]{1,0:T(8,128)(2,1)S(1)}, bf16[88,2304]{1,0:T(8,128)(2,1)}, u32[]{:S(2)}, u32[]{:S(2)}) collective-permute-start(bf16[88,2304]{1,0:T(8,128)(2,1)S(1)} %constant_dynamic-update-slice_fusion), channel_id=1, source_target_pairs={{0,1},{1,2},{2,3},{3,0},{4,5},{5,6},{6,7},{7,4},{8,9},{9,10},{10,1... | collective-permute-start | bytes 1216520 | tf_op jit(solution)/shard_map/ppermute | solution.py:228
  4.3 2.1 %collective-permute-start.2 = (bf16[88,2304]{1,0:T(8,128)(2,1)S(1)}, bf16[88,2304]{1,0:T(8,128)(2,1)S(1)}, u32[]{:S(2)}, u32[]{:S(2)}) collective-permute-start(bf16[88,2304]{1,0:T(8,128)(2,1)S(1)} %constant_dynamic-update-slice_fusion), channel_id=1, source_target_pairs={{0,3},{1,0},{2,1},{3,2},{4,7},{5,4},{6,5},{7,6},{8,11},{9,8},{10,9... | collective-permute-start | bytes 1216520 | tf_op jit(solution)/shard_map/ppermute | solution.py:228
  6.4 0.6 fusion.18
  7.0 3.6 %broadcast_select_fusion = (bf16[448,1408]{1,0:T(8,128)(2,1)S(1)}, bf16[448,1408]{1,0:T(8,128)(2,1)}) fusion(pred[]{:T(512)} %bitcast, bf16[896,1408]{1,0:T(8,128)(2,1)} %param.8), kind=kLoop, calls=%fused_computation.9 | loop fusion | flops 1261568 | bytes 5046273 | tf_op jit(solution)/shard_map/jit(_where)/select_n | solution.py:288
  10.6 0.8 slice.220
  11.5 1.7 %collective-permute-start.6 = (bf16[144,1408]{1,0:T(8,128)(2,1)}, bf16[144,1408]{1,0:T(8,128)(2,1)}, u32[]{:S(2)}, u32[]{:S(2)}) collective-permute-start(bf16[144,1408]{1,0:T(8,128)(2,1)} %slice.220), channel_id=1, source_target_pairs={{0,16},{4,20},{8,24},{12,28},{16,0},{20,4},{24,8},{28,12},{1,17},{... | collective-permute-start | bytes 1216520 | tf_op jit(solution)/shard_map/ppermute | solution.py:228
  13.3 1.7 %fusion = bf16[1408,1408]{1,0:T(8,128)(2,1)S(1)} fusion(s32[1408]{0:T(1024)S(1)} %pad_add_fusion), kind=kLoop, calls=%fused_computation.1 | loop fusion | flops 3964928 | bytes 3970560 | tf_op jit(solution)/shard_map/convert_element_type | solution.py:259
  15.2 1.4 %collective-permute-done.1 = bf16[88,2304]{1,0:T(8,128)(2,1)} collective-permute-done((bf16[88,2304]{1,0:T(8,128)(2,1)S(1)}, bf16[88,2304]{1,0:T(8,128)(2,1)}, u32[]{:S(2)}, u32[]{:S(2)}) %collective-permute-start.1) | collective-permute-done | bytes 405536 | tf_op jit(solution)/shard_map/ppermute | solution.py:228
  16.8 1.0 pad_maximum_fusion
  17.8 6.3 %collective-permute-done.2 = bf16[88,2304]{1,0:T(8,128)(2,1)S(1)} collective-permute-done((bf16[88,2304]{1,0:T(8,128)(2,1)S(1)}, bf16[88,2304]{1,0:T(8,128)(2,1)S(1)}, u32[]{:S(2)}, u32[]{:S(2)}) %collective-permute-start.2) | collective-permute-done | bytes 405536 | tf_op jit(solution)/shard_map/ppermute | solution.py:228
  24.1 1.1 slice.186
  25.2 1.8 %collective-permute-start.5 = (bf16[176,1152]{1,0:T(8,128)(2,1)S(1)}, bf16[176,1152]{1,0:T(8,128)(2,1)S(1)}, u32[]{:S(2)}, u32[]{:S(2)}) collective-permute-start(bf16[176,1152]{1,0:T(8,128)(2,1)S(1)} %pad_maximum_fusion.5), channel_id=1, source_target_pairs={{0,8},{4,12},{8,0},{12,4},{16,24},{20,28},{24,16},{28,20},{1,9},{5... | collective-permute-start | bytes 1216520 | tf_op jit(solution)/shard_map/ppermute | solution.py:233
  27.0 1.7 %collective-permute-start.7 = (bf16[88,1920]{1,0:T(8,128)(2,1)S(1)}, bf16[88,1920]{1,0:T(8,128)(2,1)S(1)}, u32[]{:S(2)}, u32[]{:S(2)}) collective-permute-start(bf16[88,1920]{1,0:T(8,128)(2,1)S(1)} %pad_maximum_fusion.7), channel_id=1, source_target_pairs={{0,1},{1,2},{2,3},{3,0},{4,5},{5,6},{6,7},{7,4},{8,9},{9,10},{10,1... | collective-permute-start | bytes 1013768 | tf_op jit(solution)/shard_map/ppermute | solution.py:228
  28.9 3.6 %convolution_convert_fusion.1.refs_0_ = bf16[448,1408]{1,0:T(8,128)(2,1)S(1)} fusion(bf16[448,1408]{1,0:T(8,128)(2,1)} %collective-permute-done, bf16[1408,1408]{1,0:T(8,128)(2,1)S(1)} %fusion), kind=kOutput, calls=%fused_computation.3 | convolution fusion | flops 1776918528 | bytes 6488064 | tf_op jit(solution)/shard_map/dot_general | solution.py:223
  32.5 3.3 %collective-permute-done.3 = bf16[88,2304]{1,0:T(8,128)(2,1)S(1)} collective-permute-done((bf16[88,2304]{1,0:T(8,128)(2,1)}, bf16[88,2304]{1,0:T(8,128)(2,1)S(1)}, u32[]{:S(2)}, u32[]{:S(2)}) %collective-permute-start.3) | collective-permute-done | bytes 405536 | tf_op jit(solution)/shard_map/ppermute | solution.py:228
  35.8 1.6 %collective-permute-start.4 = (bf16[88,1152]{1,0:T(8,128)(2,1)S(1)}, bf16[88,1152]{1,0:T(8,128)(2,1)S(1)}, u32[]{:S(2)}, u32[]{:S(2)}) collective-permute-start(bf16[88,1152]{1,0:T(8,128)(2,1)S(1)} %slice.185), channel_id=1, source_target_pairs={{0,8},{4,12},{8,0},{12,4},{16,24},{20,28},{24,16},{28,20},{1,9},{5... | collective-permute-start | bytes 608264 | tf_op jit(solution)/shard_map/ppermute | solution.py:233
  37.4 1.0 pad_maximum_fusion.2
  38.5 0.8 pad_maximum_fusion.4
  39.3 1.1 collective-permute-done.7
  40.4 1.2 %collective-permute-done.4 = bf16[88,1152]{1,0:T(8,128)(2,1)S(1)} collective-permute-done((bf16[88,1152]{1,0:T(8,128)(2,1)S(1)}, bf16[88,1152]{1,0:T(8,128)(2,1)S(1)}, u32[]{:S(2)}, u32[]{:S(2)}) %collective-permute-start.4) | collective-permute-done | bytes 202784 | tf_op jit(solution)/shard_map/ppermute | solution.py:233
  41.6 1.7 %slice_dynamic-update-slice_fusion.4 = (bf16[528,1152]{1,0:T(8,128)(2,1)S(1)}, bf16[528,1152]{1,0:T(8,128)(2,1)}) fusion(bf16[88,2304]{1,0:T(8,128)(2,1)} %collective-permute-done.1), kind=kLoop, calls=%fused_computation.27 | loop fusion | bytes 811008
  43.3 0.7 slice_dynamic-update-slice_fusion.3
  44.0 0.8 constant_dynamic-update-slice_fusion.3
  44.9 0.7 slice_dynamic-update-slice_fusion.5
  45.6 0.7 constant_dynamic-update-slice_fusion.2
  46.3 0.8 slice.198
  47.1 1.5 %collective-permute-start.9 = (bf16[144,1408]{1,0:T(8,128)(2,1)}, bf16[144,1408]{1,0:T(8,128)(2,1)}, u32[]{:S(2)}, u32[]{:S(2)}) collective-permute-start(bf16[144,1408]{1,0:T(8,128)(2,1)} %slice.198), channel_id=1, source_target_pairs={{0,16},{4,20},{8,24},{12,28},{16,0},{20,4},{24,8},{28,12},{1,17},{... | collective-permute-start | bytes 1216520 | tf_op jit(solution)/shard_map/ppermute | solution.py:228
  48.8 2.0 %collective-permute-start.10 = (bf16[88,1920]{1,0:T(8,128)(2,1)}, bf16[88,1920]{1,0:T(8,128)(2,1)S(1)}, u32[]{:S(2)}, u32[]{:S(2)}) collective-permute-start(bf16[88,1920]{1,0:T(8,128)(2,1)} %copy-done.14), channel_id=1, source_target_pairs={{0,3},{1,0},{2,1},{3,2},{4,7},{5,4},{6,5},{7,6},{8,11},{9,8},{10,9... | collective-permute-start | bytes 1013768 | tf_op jit(solution)/shard_map/ppermute | solution.py:228
  50.9 1.0 slice.201
  51.9 0.9 slice.199
  52.9 1.6 %collective-permute-start.11 = (bf16[264,1152]{1,0:T(8,128)(2,1)S(1)}, bf16[264,1152]{1,0:T(8,128)(2,1)S(1)}, u32[]{:S(2)}, u32[]{:S(2)}) collective-permute-start(bf16[264,1152]{1,0:T(8,128)(2,1)S(1)} %pad_maximum_fusion.3), channel_id=1, source_target_pairs={{0,8},{4,12},{8,0},{12,4},{16,24},{20,28},{24,16},{28,20},{1,9},{5... | collective-permute-start | bytes 1824776 | tf_op jit(solution)/shard_map/ppermute | solution.py:233
  55.1 4.5 %collective-permute-done.9 = bf16[144,1408]{1,0:T(8,128)(2,1)} collective-permute-done((bf16[144,1408]{1,0:T(8,128)(2,1)}, bf16[144,1408]{1,0:T(8,128)(2,1)}, u32[]{:S(2)}, u32[]{:S(2)}) %collective-permute-start.9) | collective-permute-done | bytes 405536 | tf_op jit(solution)/shard_map/ppermute | solution.py:228
  59.5 1.0 collective-permute-start.13
  60.6 1.5 %constant_dynamic-update-slice_fusion.5 = bf16[1408,1152]{1,0:T(8,128)(2,1)S(1)} fusion(bf16[1408,1152]{1,0:T(8,128)(2,1)S(1)} %constant_dynamic-update-slice_fusion.6, bf16[528,1152]{1,0:T(8,128)(2,1)} %constant_dynamic-update-slice_fusion.2), kind=kLoop, calls=%fused_computation.49 | loop fusion | bytes 2433024
  62.1 1.5 %constant_dynamic-update-slice_fusion.4.refs_1_ = bf16[1408,1152]{1,0:T(8,128)(2,1)S(1)} fusion(bf16[1408,1152]{1,0:T(8,128)(2,1)S(1)} %constant_dynamic-update-slice_fusion.5, bf16[528,1152]{1,0:T(8,128)(2,1)} %collective-permute-done.8), kind=kLoop, calls=%fused_computation.48 | loop fusion | bytes 2433024 | tf_op jit(solution)/shard_map/concatenate | solution.py:241
  63.6 4.2 %attend_0_0.1 = (bf16[448,256]{1,0:T(8,128)(2,1)S(1)}, bf16[448,384]{1,0:T(8,128)(2,1)S(1)}, bf16[448,128]{1,0:T(8,128)(2,1)S(1)}) custom-call(bf16[448,1408]{1,0:T(8,128)(2,1)S(1)} %convolution_convert_fusion.1.refs_0_, bf16[1408,1152]{1,0:T(8,128)(2,1)S(1)} %constant_dynamic-update-slice_fusion.4.refs_1_, s32[8,1,2,2]{3,2,1,0:T(2,128)S(1)} %copy.9.refs_2_.refs_3_, ...), custom_call_target="tpu_custom_call" | custom-call | tf_op jit(solution)/shard_map/attend_0_0/pallas_call | solution.py:188
  67.8 0.9 collective-permute-done.12
  68.7 3.5 %convolution_convert_fusion.refs_0_.refs_1_ = bf16[448,1408]{1,0:T(8,128)(2,1)S(1)} fusion(bf16[1408,1408]{1,0:T(8,128)(2,1)S(1)} %copy-done.2, bf16[160,1408]{1,0:T(8,128)(2,1)S(1)} %collective-permute-done.12, bf16[144,1408]{1,0:T(8,128)(2,1)} %collective-permute-done.9, bf16[144,1408]{1,0:T(8,128)(2,1)} %collective-permute-done.6), kind=kOutput, calls=%fused_computation.2 | convolution fusion | flops 1780703232 | bytes 6488064 | tf_op jit(solution)/shard_map/dot_general | solution.py:223
  72.6 1.6 %collective-permute-start.15 = (bf16[176,1152]{1,0:T(8,128)(2,1)S(1)}, bf16[176,1152]{1,0:T(8,128)(2,1)S(1)}, u32[]{:S(2)}, u32[]{:S(2)}) collective-permute-start(bf16[176,1152]{1,0:T(8,128)(2,1)S(1)} %pad_maximum_fusion.6), channel_id=1, source_target_pairs={{0,8},{4,12},{8,0},{12,4},{16,24},{20,28},{24,16},{28,20},{1,9},{5... | collective-permute-start | bytes 1216520 | tf_op jit(solution)/shard_map/ppermute | solution.py:233
  74.2 1.6 %collective-permute-start.16 = (bf16[176,768]{1,0:T(8,128)(2,1)S(1)}, bf16[176,768]{1,0:T(8,128)(2,1)S(1)}, u32[]{:S(2)}, u32[]{:S(2)}) collective-permute-start(bf16[176,768]{1,0:T(8,128)(2,1)S(1)} %pad_maximum_fusion.8), channel_id=1, source_target_pairs={{0,16},{4,20},{8,24},{12,28},{16,0},{20,4},{24,8},{28,12},{1,17},{... | collective-permute-start | bytes 811016 | tf_op jit(solution)/shard_map/ppermute | solution.py:233
  75.9 4.3 %attend_0_1.1 = (bf16[448,256]{1,0:T(8,128)(2,1)S(1)}, bf16[448,384]{1,0:T(8,128)(2,1)S(1)}, bf16[448,128]{1,0:T(8,128)(2,1)S(1)}) custom-call(bf16[448,1408]{1,0:T(8,128)(2,1)S(1)} %convolution_convert_fusion.refs_0_.refs_1_, bf16[1408,1152]{1,0:T(8,128)(2,1)S(1)} %constant_dynamic-update-slice_fusion.4.refs_1_, s32[8,1,2,2]{3,2,1,0:T(2,128)S(1)} %copy.9.refs_2_.refs_3_, ...), custom_call_target="tpu_custom_call" | custom-call | tf_op jit(solution)/shard_map/attend_0_1/pallas_call | solution.py:188
  81.3 1.5 %collective-permute-done.16 = bf16[176,768]{1,0:T(8,128)(2,1)S(1)} collective-permute-done((bf16[176,768]{1,0:T(8,128)(2,1)S(1)}, bf16[176,768]{1,0:T(8,128)(2,1)S(1)}, u32[]{:S(2)}, u32[]{:S(2)}) %collective-permute-start.16) | collective-permute-done | bytes 270368 | tf_op jit(solution)/shard_map/ppermute | solution.py:233
  82.8 2.0 %collective-permute-done.15 = bf16[176,1152]{1,0:T(8,128)(2,1)S(1)} collective-permute-done((bf16[176,1152]{1,0:T(8,128)(2,1)S(1)}, bf16[176,1152]{1,0:T(8,128)(2,1)S(1)}, u32[]{:S(2)}, u32[]{:S(2)}) %collective-permute-start.15) | collective-permute-done | bytes 405536 | tf_op jit(solution)/shard_map/ppermute | solution.py:233
  85.3 4.5 %attend_3_0.1 = (bf16[448,384]{1,0:T(8,128)(2,1)S(1)}, bf16[448,384]{1,0:T(8,128)(2,1)S(1)}, bf16[448,128]{1,0:T(8,128)(2,1)S(1)}) custom-call(bf16[448,1408]{1,0:T(8,128)(2,1)S(1)} %convolution_convert_fusion.1.refs_0_, bf16[1408,1152]{1,0:T(8,128)(2,1)S(1)} %constant_dynamic-update-slice_fusion.7.refs_1_, s32[8,1,2,2]{3,2,1,0:T(2,128)S(1)} %copy.9.refs_2_.refs_3_, ...), custom_call_target="tpu_custom_call" | custom-call | tf_op jit(solution)/shard_map/attend_3_0/pallas_call | solution.py:188
  90.9 4.3 %attend_3_1.1 = (bf16[448,384]{1,0:T(8,128)(2,1)S(1)}, bf16[448,384]{1,0:T(8,128)(2,1)S(1)}, bf16[448,128]{1,0:T(8,128)(2,1)S(1)}) custom-call(bf16[448,1408]{1,0:T(8,128)(2,1)S(1)} %convolution_convert_fusion.refs_0_.refs_1_, bf16[1408,1152]{1,0:T(8,128)(2,1)S(1)} %constant_dynamic-update-slice_fusion.7.refs_1_, s32[8,1,2,2]{3,2,1,0:T(2,128)S(1)} %copy.9.refs_2_.refs_3_, ...), custom_call_target="tpu_custom_call" | custom-call | tf_op jit(solution)/shard_map/attend_3_1/pallas_call | solution.py:188
  95.5 8.2 %attend_6_0.1 = (bf16[448,384]{1,0:T(8,128)(2,1)S(1)}, bf16[448,384]{1,0:T(8,128)(2,1)S(1)}, bf16[448,384]{1,0:T(8,128)(2,1)S(1)}, bf16[448,384]{1,0:T(8,128)(2,...) custom-call(bf16[448,1408]{1,0:T(8,128)(2,1)S(1)} %convolution_convert_fusion.1.refs_0_, ...), custom_call_target="tpu_custom_call" | custom-call | tf_op jit(solution)/shard_map/attend_6_0/pallas_call | solution.py:188
  103.7 6.5 %attend_9_0.1 = bf16[896,1408]{1,0:T(8,128)(2,1)} custom-call(bf16[448,1408]{1,0:T(8,128)(2,1)S(1)} %convolution_convert_fusion.1.refs_0_, bf16[448,1408]{1,0:T(8,128)(2,1)S(1)} %convolution_convert_fusion.refs_0_.refs_1_, bf16[1408,768]{1,0:T(8,128)(2,1)S(1)} %constant_dynamic-update-slice_fusion.12.refs_2_, s32[8,1,2,2]{3,2,1,0:T(2,128)S(1)} %copy.9.refs_2_.refs_3_, ...), custom_call_target="tpu_custom_call" | custom-call | tf_op jit(solution)/shard_map/attend_9_0/pallas_call | solution.py:188
  (118 shorter events, 5.1 us)
Async XLA Ops:
  0.0 6.4 %copy-start.19 = (s32[8,1,2]{0,2,1:T(2,128)S(1)}, s32[8,1,2]{0,2,1:T(2,128)}, u32[]{:S(2)}) copy-start(s32[8,1,2]{0,2,1:T(2,128)} %param.11) | copy-start | bytes 196
  1.2 15.5 %collective-permute-start.1 = (bf16[88,2304]{1,0:T(8,128)(2,1)S(1)}, bf16[88,2304]{1,0:T(8,128)(2,1)}, u32[]{:S(2)}, u32[]{:S(2)}) collective-permute-start(bf16[88,2304]{1,0:T(8,128)(2,1)S(1)} %constant_dynamic-update-slice_fusion), channel_id=1, source_target_pairs={{0,1},{1,2},{2,3},{3,0},{4,5},{5,6},{6,7},{7,4},{8,9},{9,10},{10,1... | collective-permute-start | bytes 1216520 | tf_op jit(solution)/shard_map/ppermute | solution.py:228
  4.3 19.7 %collective-permute-start.2 = (bf16[88,2304]{1,0:T(8,128)(2,1)S(1)}, bf16[88,2304]{1,0:T(8,128)(2,1)S(1)}, u32[]{:S(2)}, u32[]{:S(2)}) collective-permute-start(bf16[88,2304]{1,0:T(8,128)(2,1)S(1)} %constant_dynamic-update-slice_fusion), channel_id=1, source_target_pairs={{0,3},{1,0},{2,1},{3,2},{4,7},{5,4},{6,5},{7,6},{8,11},{9,8},{10,9... | collective-permute-start | bytes 1216520 | tf_op jit(solution)/shard_map/ppermute | solution.py:228
  7.0 6.1 %copy-start.15 = (s32[1056]{0:T(1024)S(1)}, s32[1056]{0:T(1024)}, u32[]{:S(2)}) copy-start(s32[1056]{0:T(1024)} %constant.67.clone) | copy-start | bytes 12676
  7.0 6.1 %copy-start.16 = (s32[1056]{0:T(1024)S(1)}, s32[1056]{0:T(1024)}, u32[]{:S(2)}) copy-start(s32[1056]{0:T(1024)} %constant.66.clone) | copy-start | bytes 12676
  7.0 6.1 %copy-start.17 = (s32[1056]{0:T(1024)S(1)}, s32[1056]{0:T(1024)}, u32[]{:S(2)}) copy-start(s32[1056]{0:T(1024)} %constant.70) | copy-start | bytes 12676
  10.6 18.2 %collective-permute-start = (bf16[448,1408]{1,0:T(8,128)(2,1)}, bf16[448,1408]{1,0:T(8,128)(2,1)}, u32[]{:S(2)}, u32[]{:S(2)}) collective-permute-start(bf16[448,1408]{1,0:T(8,128)(2,1)} %get-tuple-element.196), channel_id=1, source_target_pairs={{0,4},{4,8},{8,12},{12,16},{16,20},{20,24},{24,28},{28,0},{1,5},{5... | collective-permute-start | bytes 3784712 | tf_op jit(solution)/shard_map/ppermute | solution.py:228
  11.5 27.0 %collective-permute-start.6 = (bf16[144,1408]{1,0:T(8,128)(2,1)}, bf16[144,1408]{1,0:T(8,128)(2,1)}, u32[]{:S(2)}, u32[]{:S(2)}) collective-permute-start(bf16[144,1408]{1,0:T(8,128)(2,1)} %slice.220), channel_id=1, source_target_pairs={{0,16},{4,20},{8,24},{12,28},{16,0},{20,4},{24,8},{28,12},{1,17},{... | collective-permute-start | bytes 1216520 | tf_op jit(solution)/shard_map/ppermute | solution.py:228
  13.2 1.8 %copy-start = (bf16[352,4224]{1,0:T(8,128)(2,1)S(1)}, bf16[352,4224]{1,0:T(8,128)(2,1)}, u32[]{:S(2)}) copy-start(bf16[352,4224]{1,0:T(8,128)(2,1)} %param.9) | copy-start | bytes 8921092
  15.1 13.8 %copy-start.1 = (bf16[1408,1408]{1,0:T(8,128)(2,1)}, bf16[1408,1408]{1,0:T(8,128)(2,1)S(1)}, u32[]{:S(2)}) copy-start(bf16[1408,1408]{1,0:T(8,128)(2,1)S(1)} %fusion) | copy-start | bytes 11894788
  15.2 11.8 %copy-start.14 = (bf16[88,1920]{1,0:T(8,128)(2,1)}, bf16[88,1920]{1,0:T(8,128)(2,1)S(1)}, u32[]{:S(2)}) copy-start(bf16[88,1920]{1,0:T(8,128)(2,1)S(1)} %pad_maximum_fusion.7) | copy-start | bytes 1013764
  16.7 19.1 %collective-permute-start.3 = (bf16[88,2304]{1,0:T(8,128)(2,1)}, bf16[88,2304]{1,0:T(8,128)(2,1)S(1)}, u32[]{:S(2)}, u32[]{:S(2)}) collective-permute-start(bf16[88,2304]{1,0:T(8,128)(2,1)} %collective-permute-done.1), channel_id=1, source_target_pairs={{0,1},{1,2},{2,3},{3,0},{4,5},{5,6},{6,7},{7,4},{8,9},{9,10},{10,1... | collective-permute-start | bytes 1216520 | tf_op jit(solution)/shard_map/ppermute | solution.py:228
  24.0 4.8 %copy-start.8 = (bf16[88,2304]{1,0:T(8,128)(2,1)}, bf16[88,2304]{1,0:T(8,128)(2,1)S(1)}, u32[]{:S(2)}) copy-start(bf16[88,2304]{1,0:T(8,128)(2,1)S(1)} %collective-permute-done.2) | copy-start | bytes 1216516
  25.2 13.2 %collective-permute-start.5 = (bf16[176,1152]{1,0:T(8,128)(2,1)S(1)}, bf16[176,1152]{1,0:T(8,128)(2,1)S(1)}, u32[]{:S(2)}, u32[]{:S(2)}) collective-permute-start(bf16[176,1152]{1,0:T(8,128)(2,1)S(1)} %pad_maximum_fusion.5), channel_id=1, source_target_pairs={{0,8},{4,12},{8,0},{12,4},{16,24},{20,28},{24,16},{28,20},{1,9},{5... | collective-permute-start | bytes 1216520 | tf_op jit(solution)/shard_map/ppermute | solution.py:233
  27.0 13.4 %collective-permute-start.7 = (bf16[88,1920]{1,0:T(8,128)(2,1)S(1)}, bf16[88,1920]{1,0:T(8,128)(2,1)S(1)}, u32[]{:S(2)}, u32[]{:S(2)}) collective-permute-start(bf16[88,1920]{1,0:T(8,128)(2,1)S(1)} %pad_maximum_fusion.7), channel_id=1, source_target_pairs={{0,1},{1,2},{2,3},{3,0},{4,5},{5,6},{6,7},{7,4},{8,9},{9,10},{10,1... | collective-permute-start | bytes 1013768 | tf_op jit(solution)/shard_map/ppermute | solution.py:228
  35.8 9.1 %copy-start.10 = (bf16[88,2304]{1,0:T(8,128)(2,1)}, bf16[88,2304]{1,0:T(8,128)(2,1)S(1)}, u32[]{:S(2)}) copy-start(bf16[88,2304]{1,0:T(8,128)(2,1)S(1)} %collective-permute-done.3) | copy-start | bytes 1216516
  35.8 5.8 %collective-permute-start.4 = (bf16[88,1152]{1,0:T(8,128)(2,1)S(1)}, bf16[88,1152]{1,0:T(8,128)(2,1)S(1)}, u32[]{:S(2)}, u32[]{:S(2)}) collective-permute-start(bf16[88,1152]{1,0:T(8,128)(2,1)S(1)} %slice.185), channel_id=1, source_target_pairs={{0,8},{4,12},{8,0},{12,4},{16,24},{20,28},{24,16},{28,20},{1,9},{5... | collective-permute-start | bytes 608264 | tf_op jit(solution)/shard_map/ppermute | solution.py:233
  38.4 4.9 %copy-start.9 = (bf16[88,2304]{1,0:T(8,128)(2,1)S(1)}, bf16[88,2304]{1,0:T(8,128)(2,1)}, u32[]{:S(2)}) copy-start(bf16[88,2304]{1,0:T(8,128)(2,1)} %copy-done.8) | copy-start | bytes 1216516
  40.4 5.9 %copy-start.12 = (bf16[88,1920]{1,0:T(8,128)(2,1)}, bf16[88,1920]{1,0:T(8,128)(2,1)S(1)}, u32[]{:S(2)}) copy-start(bf16[88,1920]{1,0:T(8,128)(2,1)S(1)} %collective-permute-done.7) | copy-start | bytes 1013764
  43.3 5.2 %copy-start.20 = (s32[8,1,2]{0,2,1:T(2,128)S(1)}, s32[8,1,2]{0,2,1:T(2,128)}, u32[]{:S(2)}) copy-start(s32[8,1,2]{0,2,1:T(2,128)} %param.11) | copy-start | bytes 196
  43.3 5.3 %copy-start.18 = (s32[8,1,2,2]{0,3,2,1:T(2,128)S(1)}, s32[8,1,2,2]{0,3,2,1:T(2,128)}, u32[]{:S(2)}) copy-start(s32[8,1,2,2]{0,3,2,1:T(2,128)} %param.10) | copy-start | bytes 388
  44.0 3.0 %copy-start.6 = (bf16[528,1152]{1,0:T(8,128)(2,1)}, bf16[528,1152]{1,0:T(8,128)(2,1)S(1)}, u32[]{:S(2)}) copy-start(bf16[528,1152]{1,0:T(8,128)(2,1)S(1)} %get-tuple-element.199) | copy-start | bytes 3649540
  44.9 8.0 %slice-start = ((bf16[88,2304]{1,0:T(8,128)(2,1)}), bf16[88,1152]{1,0:T(8,128)(2,1)S(1)}, s32[]{:S(2)}) async-start(bf16[88,2304]{1,0:T(8,128)(2,1)} %copy-done.8), calls=%async_computation | async-start | bytes 405504 | tf_op jit(solution)/shard_map/slice | solution.py:314
  46.3 14.3 %collective-permute-start.8 = (bf16[528,1152]{1,0:T(8,128)(2,1)}, bf16[528,1152]{1,0:T(8,128)(2,1)}, u32[]{:S(2)}, u32[]{:S(2)}) collective-permute-start(bf16[528,1152]{1,0:T(8,128)(2,1)} %constant_dynamic-update-slice_fusion.2), channel_id=1, source_target_pairs={{0,4},{4,0},{8,12},{12,8},{16,20},{20,16},{24,28},{28,24},{1,5},{5... | collective-permute-start | bytes 3649544 | tf_op jit(solution)/shard_map/ppermute | solution.py:233
  47.1 12.5 %collective-permute-start.9 = (bf16[144,1408]{1,0:T(8,128)(2,1)}, bf16[144,1408]{1,0:T(8,128)(2,1)}, u32[]{:S(2)}, u32[]{:S(2)}) collective-permute-start(bf16[144,1408]{1,0:T(8,128)(2,1)} %slice.198), channel_id=1, source_target_pairs={{0,16},{4,20},{8,24},{12,28},{16,0},{20,4},{24,8},{28,12},{1,17},{... | collective-permute-start | bytes 1216520 | tf_op jit(solution)/shard_map/ppermute | solution.py:228
  48.8 11.8 %collective-permute-start.10 = (bf16[88,1920]{1,0:T(8,128)(2,1)}, bf16[88,1920]{1,0:T(8,128)(2,1)S(1)}, u32[]{:S(2)}, u32[]{:S(2)}) collective-permute-start(bf16[88,1920]{1,0:T(8,128)(2,1)} %copy-done.14), channel_id=1, source_target_pairs={{0,3},{1,0},{2,1},{3,2},{4,7},{5,4},{6,5},{7,6},{8,11},{9,8},{10,9... | collective-permute-start | bytes 1013768 | tf_op jit(solution)/shard_map/ppermute | solution.py:228
  50.9 8.7 %copy-start.13 = (bf16[88,1920]{1,0:T(8,128)(2,1)S(1)}, bf16[88,1920]{1,0:T(8,128)(2,1)}, u32[]{:S(2)}) copy-start(bf16[88,1920]{1,0:T(8,128)(2,1)} %copy-done.12) | copy-start | bytes 1013764
  50.9 9.7 %copy-start.4 = (bf16[352,1152]{1,0:T(8,128)(2,1)S(1)}, bf16[352,1152]{1,0:T(8,128)(2,1)}, u32[]{:S(2)}) copy-start(bf16[352,1152]{1,0:T(8,128)(2,1)} %pad_maximum_fusion) | copy-start | bytes 2433028
  52.9 19.3 %collective-permute-start.11 = (bf16[264,1152]{1,0:T(8,128)(2,1)S(1)}, bf16[264,1152]{1,0:T(8,128)(2,1)S(1)}, u32[]{:S(2)}, u32[]{:S(2)}) collective-permute-start(bf16[264,1152]{1,0:T(8,128)(2,1)S(1)} %pad_maximum_fusion.3), channel_id=1, source_target_pairs={{0,8},{4,12},{8,0},{12,4},{16,24},{20,28},{24,16},{28,20},{1,9},{5... | collective-permute-start | bytes 1824776 | tf_op jit(solution)/shard_map/ppermute | solution.py:233
  54.5 14.2 %collective-permute-start.12 = (bf16[160,1408]{1,0:T(8,128)(2,1)S(1)}, bf16[160,1408]{1,0:T(8,128)(2,1)S(1)}, u32[]{:S(2)}, u32[]{:S(2)}) collective-permute-start(bf16[160,1408]{1,0:T(8,128)(2,1)S(1)} %slice.202), channel_id=1, source_target_pairs={{0,16},{4,20},{8,24},{12,28},{16,0},{20,4},{24,8},{28,12},{1,17},{... | collective-permute-start | bytes 1351688 | tf_op jit(solution)/shard_map/ppermute | solution.py:228
  59.5 12.7 %collective-permute-start.13 = (bf16[88,1920]{1,0:T(8,128)(2,1)S(1)}, bf16[88,1920]{1,0:T(8,128)(2,1)S(1)}, u32[]{:S(2)}, u32[]{:S(2)}) collective-permute-start(bf16[88,1920]{1,0:T(8,128)(2,1)S(1)} %copy-done.13), channel_id=1, source_target_pairs={{0,1},{1,2},{2,3},{3,0},{4,5},{5,6},{6,7},{7,4},{8,9},{9,10},{10,1... | collective-permute-start | bytes 1013768 | tf_op jit(solution)/shard_map/ppermute | solution.py:228
  63.6 5.1 %copy-start.2 = (bf16[1408,1408]{1,0:T(8,128)(2,1)S(1)}, bf16[1408,1408]{1,0:T(8,128)(2,1)}, u32[]{:S(2)}) copy-start(bf16[1408,1408]{1,0:T(8,128)(2,1)} %copy-done.1) | copy-start | bytes 11894788
  68.7 3.5 %copy-start.7 = (bf16[528,1152]{1,0:T(8,128)(2,1)S(1)}, bf16[528,1152]{1,0:T(8,128)(2,1)}, u32[]{:S(2)}) copy-start(bf16[528,1152]{1,0:T(8,128)(2,1)} %copy-done.6) | copy-start | bytes 3649540
  68.7 3.6 %copy-start.11 = (bf16[88,2304]{1,0:T(8,128)(2,1)S(1)}, bf16[88,2304]{1,0:T(8,128)(2,1)}, u32[]{:S(2)}) copy-start(bf16[88,2304]{1,0:T(8,128)(2,1)} %copy-done.10) | copy-start | bytes 1216516
  72.3 3.4 %copy-start.3 = (bf16[352,1152]{1,0:T(8,128)(2,1)S(1)}, bf16[352,1152]{1,0:T(8,128)(2,1)}, u32[]{:S(2)}) copy-start(bf16[352,1152]{1,0:T(8,128)(2,1)} %pad_maximum_fusion.2) | copy-start | bytes 2433028
  72.4 12.5 %collective-permute-start.14 = (bf16[528,1152]{1,0:T(8,128)(2,1)S(1)}, bf16[528,1152]{1,0:T(8,128)(2,1)S(1)}, u32[]{:S(2)}, u32[]{:S(2)}) collective-permute-start(bf16[528,1152]{1,0:T(8,128)(2,1)S(1)} %slice_dynamic-update-slice_fusion.1), channel_id=1, source_target_pairs={{0,4},{4,0},{8,12},{12,8},{16,20},{20,16},{24,28},{28,24},{1,5},{5... | collective-permute-start | bytes 3649544 | tf_op jit(solution)/shard_map/ppermute | solution.py:233
  72.5 3.3 %copy-start.5 = (bf16[352,768]{1,0:T(8,128)(2,1)S(1)}, bf16[352,768]{1,0:T(8,128)(2,1)}, u32[]{:S(2)}) copy-start(bf16[352,768]{1,0:T(8,128)(2,1)} %pad_maximum_fusion.4) | copy-start | bytes 1622020
  72.6 12.2 %collective-permute-start.15 = (bf16[176,1152]{1,0:T(8,128)(2,1)S(1)}, bf16[176,1152]{1,0:T(8,128)(2,1)S(1)}, u32[]{:S(2)}, u32[]{:S(2)}) collective-permute-start(bf16[176,1152]{1,0:T(8,128)(2,1)S(1)} %pad_maximum_fusion.6), channel_id=1, source_target_pairs={{0,8},{4,12},{8,0},{12,4},{16,24},{20,28},{24,16},{28,20},{1,9},{5... | collective-permute-start | bytes 1216520 | tf_op jit(solution)/shard_map/ppermute | solution.py:233
  74.2 8.7 %collective-permute-start.16 = (bf16[176,768]{1,0:T(8,128)(2,1)S(1)}, bf16[176,768]{1,0:T(8,128)(2,1)S(1)}, u32[]{:S(2)}, u32[]{:S(2)}) collective-permute-start(bf16[176,768]{1,0:T(8,128)(2,1)S(1)} %pad_maximum_fusion.8), channel_id=1, source_target_pairs={{0,16},{4,20},{8,24},{12,28},{16,0},{20,4},{24,8},{28,12},{1,17},{... | collective-permute-start | bytes 811016 | tf_op jit(solution)/shard_map/ppermute | solution.py:233
  80.2 9.6 %collective-permute-start.17 = (bf16[88,1152]{1,0:T(8,128)(2,1)S(1)}, bf16[88,1152]{1,0:T(8,128)(2,1)S(1)}, u32[]{:S(2)}, u32[]{:S(2)}) collective-permute-start(bf16[88,1152]{1,0:T(8,128)(2,1)S(1)} %slice.212), channel_id=1, source_target_pairs={{0,8},{4,12},{8,0},{12,4},{16,24},{20,28},{24,16},{28,20},{1,9},{5... | collective-permute-start | bytes 608264 | tf_op jit(solution)/shard_map/ppermute | solution.py:233
  80.8 9.0 %collective-permute-start.18 = (bf16[88,768]{1,0:T(8,128)(2,1)S(1)}, bf16[88,768]{1,0:T(8,128)(2,1)S(1)}, u32[]{:S(2)}, u32[]{:S(2)}) collective-permute-start(bf16[88,768]{1,0:T(8,128)(2,1)S(1)} %slice.213), channel_id=1, source_target_pairs={{0,16},{4,20},{8,24},{12,28},{16,0},{20,4},{24,8},{28,12},{1,17},{... | collective-permute-start | bytes 405512 | tf_op jit(solution)/shard_map/ppermute | solution.py:233
  90.2 5.2 %collective-permute-start.20 = (bf16[528,1152]{1,0:T(8,128)(2,1)S(1)}, bf16[528,1152]{1,0:T(8,128)(2,1)S(1)}, u32[]{:S(2)}, u32[]{:S(2)}) collective-permute-start(bf16[528,1152]{1,0:T(8,128)(2,1)S(1)} %get-tuple-element.217), channel_id=1, source_target_pairs={{0,4},{4,0},{8,12},{12,8},{16,20},{20,16},{24,28},{28,24},{1,5},{5... | collective-permute-start | bytes 3649544 | tf_op jit(solution)/shard_map/ppermute | solution.py:233
  90.4 4.9 %collective-permute-start.19 = (bf16[528,768]{1,0:T(8,128)(2,1)S(1)}, bf16[528,768]{1,0:T(8,128)(2,1)S(1)}, u32[]{:S(2)}, u32[]{:S(2)}) collective-permute-start(bf16[528,768]{1,0:T(8,128)(2,1)S(1)} %get-tuple-element.219), channel_id=1, source_target_pairs={{0,4},{4,0},{8,12},{12,8},{16,20},{20,16},{24,28},{28,24},{1,5},{5... | collective-permute-start | bytes 2433032 | tf_op jit(solution)/shard_map/ppermute | solution.py:233

commit v4 on v3

--- a/solution.py
+++ b/solution.py
@@ -53,12 +53,13 @@
     )(balance, rank, tokens)
 
 
-def attend_kernel(t0, t1, h0, h1, hd, bundles, earlier, *refs):
+def attend_kernel(spans, h0, h1, hd, bundles, earlier, *refs):
     nb = len(bundles)
     refs = list(refs)
     take = lambda n: [refs.pop(0) for _ in range(n)]
-    x_refs = take(nb)
-    w_ref, lengths_ref, route_ref, source_ref = take(4)
+    x_refs, w_refs = take(nb), take(len(spans))
+    lengths_ref, route_ref, source_ref = take(3)
+    t0, t1 = spans[0][0], spans[-1][1]
     later = t0 > 0
     pc_in, oc_in = (take(nb), take(nb)) if later else (None, None)
     last = earlier is not None
@@ -81,9 +82,12 @@
             copies.append(pltpu.make_async_copy(before[j], to, sems.at[j]))
             copies[-1].start()
     for i, bundle in enumerate(bundles):
-        p = jnp.dot(x_refs[i][...], w_ref[...], preferred_element_type=jnp.float32).astype(jnp.bfloat16)
+        for w_ref, (u0, u1) in zip(w_refs, spans):
+            p = jnp.dot(x_refs[i][...], w_ref[...], preferred_element_type=jnp.float32).astype(jnp.bfloat16)
+            n = (u1 - u0) * LANE
+            for part in range(3):
+                proj[i, part, :, (u0 - base) * LANE : (u1 - base) * LANE] = p[:, part * n : (part + 1) * n]
         for part in range(3):
-            proj[i, part, :, LANE:] = p[:, part * nt * LANE : (part + 1) * nt * LANE]
             if later:
                 proj[i, part, :, :LANE] = pc_in[i][:, part * LANE : (part + 1) * LANE]
             if not last:
@@ -154,9 +158,10 @@
         copy.wait()
 
 
-def attend(t0, t1, h0, h1, bundles, xs, w, info, carry, finished):
+def attend(spans, h0, h1, bundles, xs, ws, info, carry, finished):
     rows, d = xs[0].shape
     hd = d // HEADS
+    t0, t1 = spans[0][0], spans[-1][1]
     nb, nt = len(bundles), t1 - t0
     first_tile = h0 * hd // LANE
     tiles = h1 * hd // LANE - first_tile
@@ -164,8 +169,8 @@
     inside = pl.BlockSpec(memory_space=pltpu.VMEM)
     anywhere = pl.BlockSpec(memory_space=pl.ANY)
     scalars = pl.BlockSpec(memory_space=pltpu.SMEM)
-    operands = [*xs, w, *info]
-    specs = [inside] * (nb + 1) + [scalars] * 3
+    operands = [*xs, *ws, *info]
+    specs = [inside] * (nb + len(ws)) + [scalars] * 3
     if t0 > 0:
         operands += [carry[b][0] for b in bundles] + [carry[b][1] for b in bundles]
         specs += [inside] * (2 * nb)
@@ -186,7 +191,7 @@
         out_shape = [shape(rows, tiles * LANE)] * nb + [shape(rows, 3 * LANE)] * nb + [shape(rows, LANE)] * nb
         out_specs = [inside] * (3 * nb)
     res = pl.pallas_call(
-        functools.partial(attend_kernel, t0, t1, h0, h1, hd, bundles, earlier),
+        functools.partial(attend_kernel, spans, h0, h1, hd, bundles, earlier),
         out_shape=out_shape,
         in_specs=specs,
         out_specs=out_specs,
@@ -274,7 +279,7 @@
     def across(c, *xs):
         return swapped(stacked(*xs) if len(xs) > 1 else xs[0], SWAPS[c])
 
-    spans = [(*b, *h) for b, h in zip(BOUNDS, heads_of(BOUNDS, hd))]
+    heads = heads_of(BOUNDS, hd)
     carry = [None, None]
     finished = []
     w = qkv_weight
@@ -286,7 +291,7 @@
     near_first = balance[rank, 0, 0] == 0
     low, high = tokens[: rows // 2], tokens[rows // 2 :]
     near_out, far_out = jnp.where(near_first, low, high), jnp.where(near_first, high, low)
-    cut = (rows // 6 // 16 * 16, rows // 3 // 16 * 16)
+    cut = (rows // 5 // 16 * 16, rows * 2 // 7 // 16 * 16)
     far_1 = shifted(far_out[: cut[0]], "dp", ranks // 2)
     near_in = shifted(near_out, "dp", 1)
     pcd = payload(w, 2, 3)
@@ -314,15 +319,15 @@
     bx = across(1, abp[:, n_a:], abm[:, n_a:], ab2[:, n_a:])
     own_d = of_chunk(w, *BOUNDS[3])
 
-    ay, ax, abp, abm, ab2, own_d, cdp, far_out = fence(ay, ax, abp, abm, ab2, own_d, cdp, far_out)
+    ay, ax, abp, abm, ab2, own_d, cdp, far_out, far_2 = fence(ay, ax, abp, abm, ab2, own_d, cdp, far_out, far_2)
     far_3 = shifted(far_out[cut[1] :], "dp", ranks // 2)
     cd2 = up(cdp)
     both_a = stacked(abp[:, :n_a], abm[:, :n_a], ax, ab2[:, :n_a], ay)
     ac = swapped(both_a, 1)
 
-    ac, both_a, own_a, near, far_2, cdm = fence(ac, both_a, own_a, near, far_2, cdm)
+    ac, both_a, own_a, near, cdm = fence(ac, both_a, own_a, near, cdm)
     wa = stacked(own_a, both_a, ac)
-    out = attend(*spans[0], (0,), (near,), wa, info, carry, finished)
+    out = attend(BOUNDS[:1], *heads[0], (0,), (near,), (wa,), info, carry, finished)
 
     out, cdp, cdm, far_1, far_2, far_3 = fence(out, cdp, cdm, far_1, far_2, far_3)
     dx_1 = across(3, cdp[:, n_c:], cdm[:, n_c:])
@@ -334,24 +339,22 @@
     cx_2 = across(2, cd2[:, :n_c])
     both_b = stacked(abp[:, n_a:], abm[:, n_a:], bx[: 2 * quarter], ab2[:, n_a:], bx[2 * quarter :])
     bc = swapped(both_b, 1)
-    out = attend(*spans[0], (1,), (far,), wa, info, carry, finished)
+    out = attend(BOUNDS[:1], *heads[0], (1,), (far,), (wa,), info, carry, finished)
 
     out, bc, both_b, own_b, cx_1, dx_1, cdp = fence(out, bc, both_b, own_b, cx_1, dx_1, cdp)
     wb = stacked(own_b, both_b, bc)
-    out = attend(*spans[1], (0,), (near,), wb, info, carry, finished)
+    out = attend(BOUNDS[1:2], *heads[1], (0,), (near,), (wb,), info, carry, finished)
 
     out, cx_1, dx_1, cx_2, dx_2, cdp, cdm, cd2 = fence(out, cx_1, dx_1, cx_2, dx_2, cdp, cdm, cd2)
     both_c = stacked(cdp[:, :n_c], cdm[:, :n_c], cx_1, cd2[:, :n_c], cx_2)
     cc = swapped(both_c, 1)
     both_d = stacked(cdp[:, n_c:], cdm[:, n_c:], dx_1, cd2[:, n_c:], dx_2)
     dc = swapped(both_d, 1)
-    out = attend(*spans[1], (1,), (far,), wb, info, carry, finished)
+    out = attend(BOUNDS[1:2], *heads[1], (1,), (far,), (wb,), info, carry, finished)
 
     wc = stacked(own_c, both_c, cc)
-    out = attend(*spans[2], (0, 1), (near, far), wc, info, carry, finished)
     wd = stacked(own_d, both_d, dc)
-    out = attend(*spans[3], (0, 1), (near, far), wd, info, carry, finished)
-    return out
+    return attend(BOUNDS[2:], heads[2][0], heads[3][1], (0, 1), (near, far), (wc, wd), info, carry, finished)
 
 
 def solution(mesh):

time: 111 us -> 108 us (0.973)
  Pallas kernels: 32.1 us -> 30.2 us
    pallas_call x6 -> x5, Pallas kernels: 32.1 us -> 30.2 us  [attend(): pl.pallas_call(functools.partial(attend_kernel, spans, h0, h1, hd, bundle...]
    ppermute x10, waiting for transfers between devices: 17.4 us -> 18.9 us  [shifted(): return lax.ppermute(x, axis, [(i, (i + by) % n) for i in range(n)])]
    ppermute x11, waiting for transfers between devices: 4.79 us -> 3.5 us  [swapped(): return lax.ppermute(x, 'dp', [(i, i ^ mask) for i in range(n)])]
    ppermute x11, starting transfers between devices: 9.86 us -> 8.62 us  [swapped(): return lax.ppermute(x, 'dp', [(i, i ^ mask) for i in range(n)])]
    unnamed x65 -> x69, local copies, waits for them, and re-layouts: 6.64 us -> 6.81 us
where the time goes in v4:
time: 108 us; the launch traced here: 107 us
  Pallas kernels  30.2 us (28%)
  starting transfers between devices  22.6 us (21%)
  waiting for transfers between devices  22.4 us (21%)
  local copies, waits for them, and re-layouts  15 us (14%)
  other arithmetic  9.23 us (9%)
  matrix products  6.97 us (6%)
    pallas_call x5, Pallas kernels, attend(): pl.pallas_call(functools.partial(attend_kernel, spans, h0, h1, hd, bundle...  30.2 us
    ppermute x10, waiting for transfers between devices, shifted(): return lax.ppermute(x, axis, [(i, (i + by) % n) for i in range(n)])  18.9 us
    ppermute x10, starting transfers between devices, shifted(): return lax.ppermute(x, axis, [(i, (i + by) % n) for i in range(n)])  13.9 us
    ppermute x11, starting transfers between devices, swapped(): return lax.ppermute(x, 'dp', [(i, i ^ mask) for i in range(n)])  8.62 us
    dot_general x2, matrix products, reordered(): jnp.dot(x, place, preferred_element_type=jnp.float32).astype(jnp.bfloat16)  6.97 us
    unnamed x69, local copies, waits for them, and re-layouts  6.81 us
    select_n x1, other arithmetic, on_device(): jnp.where(near_first, high, low)  3.62 us
    ppermute x11, waiting for transfers between devices, swapped(): return lax.ppermute(x, 'dp', [(i, i ^ mask) for i in range(n)])  3.5 us
  transfers between devices with their start and end apart: 21, of which 9 were waited for; matrix products, arithmetic and copies ran while one was open for 23% of the time, Pallas kernels for 16%

profile of v4, /device:TPU:0, one launch (start us, length us, event | category | flops | bytes accessed | tf_op | source)
XLA Modules:
  0.0 107.2 jit_solution(13458770499005242692)
XLA Ops:
  0.0 1.1 %fusion.17 = (bf16[88,384]{1,0:T(8,128)(2,1)S(1)}, bf16[88,384]{1,0:T(8,128)(2,1)S(1)}, bf16[88,384]{1,0:T(8,128)(2,1)S(1)}, bf16[88,384]{1,0:T(8,128)(2,1)S(1)}...) fusion(bf16[352,4224]{1,0:T(8,128)(2,1)} %param.9, s32[]{:T(128)S(6)} %select_n.38, s32[]{:T(128)S(6)} %add.48, ...), kind=kLoop, calls=%fused_computation.87 | loop fusion | bytes 811032 | tf_op jit(solution)/shard_map/slice | solution.py:267
  1.2 3.1 %collective-permute-start.1 = (bf16[88,2304]{1,0:T(8,128)(2,1)S(1)}, bf16[88,2304]{1,0:T(8,128)(2,1)}, u32[]{:S(2)}, u32[]{:S(2)}) collective-permute-start(bf16[88,2304]{1,0:T(8,128)(2,1)S(1)} %constant_dynamic-update-slice_fusion), channel_id=1, source_target_pairs={{0,1},{1,2},{2,3},{3,0},{4,5},{5,6},{6,7},{7,4},{8,9},{9,10},{10,1... | collective-permute-start | bytes 1216520 | tf_op jit(solution)/shard_map/ppermute | solution.py:233
  4.3 2.1 %collective-permute-start.2 = (bf16[88,2304]{1,0:T(8,128)(2,1)S(1)}, bf16[88,2304]{1,0:T(8,128)(2,1)S(1)}, u32[]{:S(2)}, u32[]{:S(2)}) collective-permute-start(bf16[88,2304]{1,0:T(8,128)(2,1)S(1)} %constant_dynamic-update-slice_fusion), channel_id=1, source_target_pairs={{0,3},{1,0},{2,1},{3,2},{4,7},{5,4},{6,5},{7,6},{8,11},{9,8},{10,9... | collective-permute-start | bytes 1216520 | tf_op jit(solution)/shard_map/ppermute | solution.py:233
  6.4 0.6 fusion.18
  7.0 3.6 %broadcast_select_fusion = (bf16[448,1408]{1,0:T(8,128)(2,1)S(1)}, bf16[448,1408]{1,0:T(8,128)(2,1)}) fusion(pred[]{:T(512)} %bitcast, bf16[896,1408]{1,0:T(8,128)(2,1)} %param.8), kind=kLoop, calls=%fused_computation.9 | loop fusion | flops 1261568 | bytes 5046273 | tf_op jit(solution)/shard_map/jit(_where)/select_n | solution.py:293
  10.6 0.8 slice.220
  11.5 1.7 %collective-permute-start.6 = (bf16[176,1408]{1,0:T(8,128)(2,1)}, bf16[176,1408]{1,0:T(8,128)(2,1)}, u32[]{:S(2)}, u32[]{:S(2)}) collective-permute-start(bf16[176,1408]{1,0:T(8,128)(2,1)} %slice.220), channel_id=1, source_target_pairs={{0,16},{4,20},{8,24},{12,28},{16,0},{20,4},{24,8},{28,12},{1,17},{... | collective-permute-start | bytes 1486856 | tf_op jit(solution)/shard_map/ppermute | solution.py:233
  13.3 1.7 %fusion = bf16[1408,1408]{1,0:T(8,128)(2,1)S(1)} fusion(s32[1408]{0:T(1024)S(1)} %pad_add_fusion), kind=kLoop, calls=%fused_computation.1 | loop fusion | flops 3964928 | bytes 3970560 | tf_op jit(solution)/shard_map/convert_element_type | solution.py:264
  15.3 1.4 %collective-permute-done.1 = bf16[88,2304]{1,0:T(8,128)(2,1)} collective-permute-done((bf16[88,2304]{1,0:T(8,128)(2,1)S(1)}, bf16[88,2304]{1,0:T(8,128)(2,1)}, u32[]{:S(2)}, u32[]{:S(2)}) %collective-permute-start.1) | collective-permute-done | bytes 405536 | tf_op jit(solution)/shard_map/ppermute | solution.py:233
  16.8 1.0 pad_maximum_fusion
  17.8 6.3 %collective-permute-done.2 = bf16[88,2304]{1,0:T(8,128)(2,1)S(1)} collective-permute-done((bf16[88,2304]{1,0:T(8,128)(2,1)S(1)}, bf16[88,2304]{1,0:T(8,128)(2,1)S(1)}, u32[]{:S(2)}, u32[]{:S(2)}) %collective-permute-start.2) | collective-permute-done | bytes 405536 | tf_op jit(solution)/shard_map/ppermute | solution.py:233
  24.1 1.1 %slice.186 = bf16[88,1152]{1,0:T(8,128)(2,1)S(1)} slice(bf16[88,2304]{1,0:T(8,128)(2,1)} %collective-permute-done.1), slice={[0:88], [0:1152]} | slice | bytes 405504 | tf_op jit(solution)/shard_map/slice | solution.py:306
  25.2 1.8 %collective-permute-start.5 = (bf16[176,1152]{1,0:T(8,128)(2,1)S(1)}, bf16[176,1152]{1,0:T(8,128)(2,1)S(1)}, u32[]{:S(2)}, u32[]{:S(2)}) collective-permute-start(bf16[176,1152]{1,0:T(8,128)(2,1)S(1)} %pad_maximum_fusion.5), channel_id=1, source_target_pairs={{0,8},{4,12},{8,0},{12,4},{16,24},{20,28},{24,16},{28,20},{1,9},{5... | collective-permute-start | bytes 1216520 | tf_op jit(solution)/shard_map/ppermute | solution.py:238
  27.0 1.7 %collective-permute-start.7 = (bf16[88,1920]{1,0:T(8,128)(2,1)S(1)}, bf16[88,1920]{1,0:T(8,128)(2,1)S(1)}, u32[]{:S(2)}, u32[]{:S(2)}) collective-permute-start(bf16[88,1920]{1,0:T(8,128)(2,1)S(1)} %pad_maximum_fusion.7), channel_id=1, source_target_pairs={{0,1},{1,2},{2,3},{3,0},{4,5},{5,6},{6,7},{7,4},{8,9},{9,10},{10,1... | collective-permute-start | bytes 1013768 | tf_op jit(solution)/shard_map/ppermute | solution.py:233
  28.9 1.6 %collective-permute-start.8 = (bf16[80,1408]{1,0:T(8,128)(2,1)S(1)}, bf16[80,1408]{1,0:T(8,128)(2,1)S(1)}, u32[]{:S(2)}, u32[]{:S(2)}) collective-permute-start(bf16[80,1408]{1,0:T(8,128)(2,1)S(1)} %slice.195), channel_id=1, source_target_pairs={{0,16},{4,20},{8,24},{12,28},{16,0},{20,4},{24,8},{28,12},{1,17},{... | collective-permute-start | bytes 675848 | tf_op jit(solution)/shard_map/ppermute | solution.py:233
  30.5 3.6 %convolution_convert_fusion.1.refs_0_ = bf16[448,1408]{1,0:T(8,128)(2,1)S(1)} fusion(bf16[448,1408]{1,0:T(8,128)(2,1)} %collective-permute-done, bf16[1408,1408]{1,0:T(8,128)(2,1)S(1)} %fusion), kind=kOutput, calls=%fused_computation.3 | convolution fusion | flops 1776918528 | bytes 6488064 | tf_op jit(solution)/shard_map/dot_general | solution.py:228
  34.1 1.7 %collective-permute-done.3 = bf16[88,2304]{1,0:T(8,128)(2,1)S(1)} collective-permute-done((bf16[88,2304]{1,0:T(8,128)(2,1)}, bf16[88,2304]{1,0:T(8,128)(2,1)S(1)}, u32[]{:S(2)}, u32[]{:S(2)}) %collective-permute-start.3) | collective-permute-done | bytes 405536 | tf_op jit(solution)/shard_map/ppermute | solution.py:233
  35.8 1.6 %collective-permute-start.4 = (bf16[88,1152]{1,0:T(8,128)(2,1)S(1)}, bf16[88,1152]{1,0:T(8,128)(2,1)S(1)}, u32[]{:S(2)}, u32[]{:S(2)}) collective-permute-start(bf16[88,1152]{1,0:T(8,128)(2,1)S(1)} %slice.185), channel_id=1, source_target_pairs={{0,8},{4,12},{8,0},{12,4},{16,24},{20,28},{24,16},{28,20},{1,9},{5... | collective-permute-start | bytes 608264 | tf_op jit(solution)/shard_map/ppermute | solution.py:238
  37.4 1.0 pad_maximum_fusion.2
  38.4 0.5 collective-permute-done.6
  38.9 0.9 pad_maximum_fusion.4
  39.8 3.8 %collective-permute-done.8 = bf16[80,1408]{1,0:T(8,128)(2,1)S(1)} collective-permute-done((bf16[80,1408]{1,0:T(8,128)(2,1)S(1)}, bf16[80,1408]{1,0:T(8,128)(2,1)S(1)}, u32[]{:S(2)}, u32[]{:S(2)}) %collective-permute-start.8) | collective-permute-done | bytes 225312 | tf_op jit(solution)/shard_map/ppermute | solution.py:233
  43.6 1.9 %slice_dynamic-update-slice_fusion.4 = (bf16[528,1152]{1,0:T(8,128)(2,1)S(1)}, bf16[528,1152]{1,0:T(8,128)(2,1)}) fusion(bf16[88,2304]{1,0:T(8,128)(2,1)} %collective-permute-done.1), kind=kLoop, calls=%fused_computation.27 | loop fusion | bytes 811008
  45.6 0.7 slice_dynamic-update-slice_fusion.3
  46.3 0.8 constant_dynamic-update-slice_fusion.3
  47.1 0.7 slice_dynamic-update-slice_fusion.5
  47.8 0.7 constant_dynamic-update-slice_fusion.2
  48.8 2.0 %collective-permute-start.10 = (bf16[88,1920]{1,0:T(8,128)(2,1)}, bf16[88,1920]{1,0:T(8,128)(2,1)S(1)}, u32[]{:S(2)}, u32[]{:S(2)}) collective-permute-start(bf16[88,1920]{1,0:T(8,128)(2,1)} %copy-done.14), channel_id=1, source_target_pairs={{0,3},{1,0},{2,1},{3,2},{4,7},{5,4},{6,5},{7,6},{8,11},{9,8},{10,9... | collective-permute-start | bytes 1013768 | tf_op jit(solution)/shard_map/ppermute | solution.py:233
  50.9 0.9 slice.201
  51.9 1.0 slice.199
  53.1 1.6 %collective-permute-start.12 = (bf16[192,1408]{1,0:T(8,128)(2,1)S(1)}, bf16[192,1408]{1,0:T(8,128)(2,1)S(1)}, u32[]{:S(2)}, u32[]{:S(2)}) collective-permute-start(bf16[192,1408]{1,0:T(8,128)(2,1)S(1)} %slice.202), channel_id=1, source_target_pairs={{0,16},{4,20},{8,24},{12,28},{16,0},{20,4},{24,8},{28,12},{1,17},{... | collective-permute-start | bytes 1622024 | tf_op jit(solution)/shard_map/ppermute | solution.py:233
  54.9 4.5 %collective-permute-done.10 = bf16[88,1920]{1,0:T(8,128)(2,1)S(1)} collective-permute-done((bf16[88,1920]{1,0:T(8,128)(2,1)}, bf16[88,1920]{1,0:T(8,128)(2,1)S(1)}, u32[]{:S(2)}, u32[]{:S(2)}) %collective-permute-start.10) | collective-permute-done | bytes 337952 | tf_op jit(solution)/shard_map/ppermute | solution.py:233
  59.5 1.5 %constant_dynamic-update-slice_fusion.5 = bf16[1408,1152]{1,0:T(8,128)(2,1)S(1)} fusion(bf16[1408,1152]{1,0:T(8,128)(2,1)S(1)} %constant_dynamic-update-slice_fusion.6, bf16[528,1152]{1,0:T(8,128)(2,1)} %constant_dynamic-update-slice_fusion.2), kind=kLoop, calls=%fused_computation.49 | loop fusion | bytes 2433024
  61.0 1.5 %constant_dynamic-update-slice_fusion.4.refs_1_ = bf16[1408,1152]{1,0:T(8,128)(2,1)S(1)} fusion(bf16[1408,1152]{1,0:T(8,128)(2,1)S(1)} %constant_dynamic-update-slice_fusion.5, bf16[528,1152]{1,0:T(8,128)(2,1)} %collective-permute-done.9), kind=kLoop, calls=%fused_computation.48 | loop fusion | bytes 2433024 | tf_op jit(solution)/shard_map/concatenate | solution.py:246
  62.5 4.2 %attend_0_0.1 = (bf16[448,256]{1,0:T(8,128)(2,1)S(1)}, bf16[448,384]{1,0:T(8,128)(2,1)S(1)}, bf16[448,128]{1,0:T(8,128)(2,1)S(1)}) custom-call(bf16[448,1408]{1,0:T(8,128)(2,1)S(1)} %convolution_convert_fusion.1.refs_0_, bf16[1408,1152]{1,0:T(8,128)(2,1)S(1)} %constant_dynamic-update-slice_fusion.4.refs_1_, s32[8,1,2,2]{3,2,1,0:T(2,128)S(1)} %copy.9.refs_2_.refs_4_, ...), custom_call_target="tpu_custom_call" | custom-call | tf_op jit(solution)/shard_map/attend_0_0/pallas_call | solution.py:193
  66.7 0.7 collective-permute-done.12
  67.4 3.4 %convolution_convert_fusion.refs_0_.refs_1_ = bf16[448,1408]{1,0:T(8,128)(2,1)S(1)} fusion(bf16[1408,1408]{1,0:T(8,128)(2,1)S(1)} %copy-done.2, bf16[192,1408]{1,0:T(8,128)(2,1)S(1)} %collective-permute-done.12, bf16[80,1408]{1,0:T(8,128)(2,1)S(1)} %copy-done.22, bf16[176,1408]{1,0:T(8,128)(2,1)} %collective-permute-done.6), kind=kOutput, calls=%fused_computation.2 | convolution fusion | flops 1780703232 | bytes 6488064 | tf_op jit(solution)/shard_map/dot_general | solution.py:228
  71.2 1.8 %collective-permute-start.15 = (bf16[176,1152]{1,0:T(8,128)(2,1)S(1)}, bf16[176,1152]{1,0:T(8,128)(2,1)S(1)}, u32[]{:S(2)}, u32[]{:S(2)}) collective-permute-start(bf16[176,1152]{1,0:T(8,128)(2,1)S(1)} %pad_maximum_fusion.6), channel_id=1, source_target_pairs={{0,8},{4,12},{8,0},{12,4},{16,24},{20,28},{24,16},{28,20},{1,9},{5... | collective-permute-start | bytes 1216520 | tf_op jit(solution)/shard_map/ppermute | solution.py:238
  73.1 1.6 %collective-permute-start.16 = (bf16[176,768]{1,0:T(8,128)(2,1)S(1)}, bf16[176,768]{1,0:T(8,128)(2,1)S(1)}, u32[]{:S(2)}, u32[]{:S(2)}) collective-permute-start(bf16[176,768]{1,0:T(8,128)(2,1)S(1)} %pad_maximum_fusion.8), channel_id=1, source_target_pairs={{0,16},{4,20},{8,24},{12,28},{16,0},{20,4},{24,8},{28,12},{1,17},{... | collective-permute-start | bytes 811016 | tf_op jit(solution)/shard_map/ppermute | solution.py:238
  74.8 4.3 %attend_0_1.1 = (bf16[448,256]{1,0:T(8,128)(2,1)S(1)}, bf16[448,384]{1,0:T(8,128)(2,1)S(1)}, bf16[448,128]{1,0:T(8,128)(2,1)S(1)}) custom-call(bf16[448,1408]{1,0:T(8,128)(2,1)S(1)} %convolution_convert_fusion.refs_0_.refs_1_, bf16[1408,1152]{1,0:T(8,128)(2,1)S(1)} %constant_dynamic-update-slice_fusion.4.refs_1_, s32[8,1,2,2]{3,2,1,0:T(2,128)S(1)} %copy.9.refs_2_.refs_4_, ...), custom_call_target="tpu_custom_call" | custom-call | tf_op jit(solution)/shard_map/attend_0_1/pallas_call | solution.py:193
  79.1 0.4 collective-permute-start.17
  79.4 0.6 collective-permute-start.18
  80.0 1.7 %collective-permute-done.16 = bf16[176,768]{1,0:T(8,128)(2,1)S(1)} collective-permute-done((bf16[176,768]{1,0:T(8,128)(2,1)S(1)}, bf16[176,768]{1,0:T(8,128)(2,1)S(1)}, u32[]{:S(2)}, u32[]{:S(2)}) %collective-permute-start.16) | collective-permute-done | bytes 270368 | tf_op jit(solution)/shard_map/ppermute | solution.py:238
  81.7 1.8 %collective-permute-done.15 = bf16[176,1152]{1,0:T(8,128)(2,1)S(1)} collective-permute-done((bf16[176,1152]{1,0:T(8,128)(2,1)S(1)}, bf16[176,1152]{1,0:T(8,128)(2,1)S(1)}, u32[]{:S(2)}, u32[]{:S(2)}) %collective-permute-start.15) | collective-permute-done | bytes 405536 | tf_op jit(solution)/shard_map/ppermute | solution.py:238
  83.9 4.5 %attend_3_0.1 = (bf16[448,384]{1,0:T(8,128)(2,1)S(1)}, bf16[448,384]{1,0:T(8,128)(2,1)S(1)}, bf16[448,128]{1,0:T(8,128)(2,1)S(1)}) custom-call(bf16[448,1408]{1,0:T(8,128)(2,1)S(1)} %convolution_convert_fusion.1.refs_0_, bf16[1408,1152]{1,0:T(8,128)(2,1)S(1)} %constant_dynamic-update-slice_fusion.7.refs_1_, s32[8,1,2,2]{3,2,1,0:T(2,128)S(1)} %copy.9.refs_2_.refs_4_, ...), custom_call_target="tpu_custom_call" | custom-call | tf_op jit(solution)/shard_map/attend_3_0/pallas_call | solution.py:193
  89.0 0.6 collective-permute-start.20
  89.6 4.3 %attend_3_1.1 = (bf16[448,384]{1,0:T(8,128)(2,1)S(1)}, bf16[448,384]{1,0:T(8,128)(2,1)S(1)}, bf16[448,128]{1,0:T(8,128)(2,1)S(1)}) custom-call(bf16[448,1408]{1,0:T(8,128)(2,1)S(1)} %convolution_convert_fusion.refs_0_.refs_1_, bf16[1408,1152]{1,0:T(8,128)(2,1)S(1)} %constant_dynamic-update-slice_fusion.7.refs_1_, s32[8,1,2,2]{3,2,1,0:T(2,128)S(1)} %copy.9.refs_2_.refs_4_, ...), custom_call_target="tpu_custom_call" | custom-call | tf_op jit(solution)/shard_map/attend_3_1/pallas_call | solution.py:193
  94.2 12.9 %attend_6_0.1 = bf16[896,1408]{1,0:T(8,128)(2,1)} custom-call(bf16[448,1408]{1,0:T(8,128)(2,1)S(1)} %convolution_convert_fusion.1.refs_0_, bf16[448,1408]{1,0:T(8,128)(2,1)S(1)} %convolution_convert_fusion.refs_0_.refs_1_, bf16[1408,1152]{1,0:T(8,128)(2,1)S(1)} %constant_dynamic-update-slice_fusion.12.refs_2_, ...), custom_call_target="tpu_custom_call" | custom-call | tf_op jit(solution)/shard_map/attend_6_0/pallas_call | solution.py:193
  (121 shorter events, 3.4 us)
Async XLA Ops:
  0.0 6.4 %copy-start.19 = (s32[8,1,2]{0,2,1:T(2,128)S(1)}, s32[8,1,2]{0,2,1:T(2,128)}, u32[]{:S(2)}) copy-start(s32[8,1,2]{0,2,1:T(2,128)} %param.11) | copy-start | bytes 196
  1.2 15.5 %collective-permute-start.1 = (bf16[88,2304]{1,0:T(8,128)(2,1)S(1)}, bf16[88,2304]{1,0:T(8,128)(2,1)}, u32[]{:S(2)}, u32[]{:S(2)}) collective-permute-start(bf16[88,2304]{1,0:T(8,128)(2,1)S(1)} %constant_dynamic-update-slice_fusion), channel_id=1, source_target_pairs={{0,1},{1,2},{2,3},{3,0},{4,5},{5,6},{6,7},{7,4},{8,9},{9,10},{10,1... | collective-permute-start | bytes 1216520 | tf_op jit(solution)/shard_map/ppermute | solution.py:233
  4.3 19.7 %collective-permute-start.2 = (bf16[88,2304]{1,0:T(8,128)(2,1)S(1)}, bf16[88,2304]{1,0:T(8,128)(2,1)S(1)}, u32[]{:S(2)}, u32[]{:S(2)}) collective-permute-start(bf16[88,2304]{1,0:T(8,128)(2,1)S(1)} %constant_dynamic-update-slice_fusion), channel_id=1, source_target_pairs={{0,3},{1,0},{2,1},{3,2},{4,7},{5,4},{6,5},{7,6},{8,11},{9,8},{10,9... | collective-permute-start | bytes 1216520 | tf_op jit(solution)/shard_map/ppermute | solution.py:233
  7.0 6.2 %copy-start.15 = (s32[1056]{0:T(1024)S(1)}, s32[1056]{0:T(1024)}, u32[]{:S(2)}) copy-start(s32[1056]{0:T(1024)} %constant.67.clone) | copy-start | bytes 12676
  7.0 6.2 %copy-start.16 = (s32[1056]{0:T(1024)S(1)}, s32[1056]{0:T(1024)}, u32[]{:S(2)}) copy-start(s32[1056]{0:T(1024)} %constant.66.clone) | copy-start | bytes 12676
  7.0 6.2 %copy-start.17 = (s32[1056]{0:T(1024)S(1)}, s32[1056]{0:T(1024)}, u32[]{:S(2)}) copy-start(s32[1056]{0:T(1024)} %constant.70) | copy-start | bytes 12676
  10.6 18.3 %collective-permute-start = (bf16[448,1408]{1,0:T(8,128)(2,1)}, bf16[448,1408]{1,0:T(8,128)(2,1)}, u32[]{:S(2)}, u32[]{:S(2)}) collective-permute-start(bf16[448,1408]{1,0:T(8,128)(2,1)} %get-tuple-element.184), channel_id=1, source_target_pairs={{0,4},{4,8},{8,12},{12,16},{16,20},{20,24},{24,28},{28,0},{1,5},{5... | collective-permute-start | bytes 3784712 | tf_op jit(solution)/shard_map/ppermute | solution.py:233
  11.5 27.4 %collective-permute-start.6 = (bf16[176,1408]{1,0:T(8,128)(2,1)}, bf16[176,1408]{1,0:T(8,128)(2,1)}, u32[]{:S(2)}, u32[]{:S(2)}) collective-permute-start(bf16[176,1408]{1,0:T(8,128)(2,1)} %slice.220), channel_id=1, source_target_pairs={{0,16},{4,20},{8,24},{12,28},{16,0},{20,4},{24,8},{28,12},{1,17},{... | collective-permute-start | bytes 1486856 | tf_op jit(solution)/shard_map/ppermute | solution.py:233
  13.3 1.8 %copy-start = (bf16[352,4224]{1,0:T(8,128)(2,1)S(1)}, bf16[352,4224]{1,0:T(8,128)(2,1)}, u32[]{:S(2)}) copy-start(bf16[352,4224]{1,0:T(8,128)(2,1)} %param.9) | copy-start | bytes 8921092
  15.1 15.4 %copy-start.1 = (bf16[1408,1408]{1,0:T(8,128)(2,1)}, bf16[1408,1408]{1,0:T(8,128)(2,1)S(1)}, u32[]{:S(2)}) copy-start(bf16[1408,1408]{1,0:T(8,128)(2,1)S(1)} %fusion) | copy-start | bytes 11894788
  15.2 11.7 %copy-start.14 = (bf16[88,1920]{1,0:T(8,128)(2,1)}, bf16[88,1920]{1,0:T(8,128)(2,1)S(1)}, u32[]{:S(2)}) copy-start(bf16[88,1920]{1,0:T(8,128)(2,1)S(1)} %pad_maximum_fusion.7) | copy-start | bytes 1013764
  16.7 19.1 %collective-permute-start.3 = (bf16[88,2304]{1,0:T(8,128)(2,1)}, bf16[88,2304]{1,0:T(8,128)(2,1)S(1)}, u32[]{:S(2)}, u32[]{:S(2)}) collective-permute-start(bf16[88,2304]{1,0:T(8,128)(2,1)} %collective-permute-done.1), channel_id=1, source_target_pairs={{0,1},{1,2},{2,3},{3,0},{4,5},{5,6},{6,7},{7,4},{8,9},{9,10},{10,1... | collective-permute-start | bytes 1216520 | tf_op jit(solution)/shard_map/ppermute | solution.py:233
  24.0 4.8 %copy-start.8 = (bf16[88,2304]{1,0:T(8,128)(2,1)}, bf16[88,2304]{1,0:T(8,128)(2,1)S(1)}, u32[]{:S(2)}) copy-start(bf16[88,2304]{1,0:T(8,128)(2,1)S(1)} %collective-permute-done.2) | copy-start | bytes 1216516
  25.2 13.7 %collective-permute-start.5 = (bf16[176,1152]{1,0:T(8,128)(2,1)S(1)}, bf16[176,1152]{1,0:T(8,128)(2,1)S(1)}, u32[]{:S(2)}, u32[]{:S(2)}) collective-permute-start(bf16[176,1152]{1,0:T(8,128)(2,1)S(1)} %pad_maximum_fusion.5), channel_id=1, source_target_pairs={{0,8},{4,12},{8,0},{12,4},{16,24},{20,28},{24,16},{28,20},{1,9},{5... | collective-permute-start | bytes 1216520 | tf_op jit(solution)/shard_map/ppermute | solution.py:238
  27.0 16.6 %collective-permute-start.7 = (bf16[88,1920]{1,0:T(8,128)(2,1)S(1)}, bf16[88,1920]{1,0:T(8,128)(2,1)S(1)}, u32[]{:S(2)}, u32[]{:S(2)}) collective-permute-start(bf16[88,1920]{1,0:T(8,128)(2,1)S(1)} %pad_maximum_fusion.7), channel_id=1, source_target_pairs={{0,1},{1,2},{2,3},{3,0},{4,5},{5,6},{6,7},{7,4},{8,9},{9,10},{10,1... | collective-permute-start | bytes 1013768 | tf_op jit(solution)/shard_map/ppermute | solution.py:233
  28.9 14.7 %collective-permute-start.8 = (bf16[80,1408]{1,0:T(8,128)(2,1)S(1)}, bf16[80,1408]{1,0:T(8,128)(2,1)S(1)}, u32[]{:S(2)}, u32[]{:S(2)}) collective-permute-start(bf16[80,1408]{1,0:T(8,128)(2,1)S(1)} %slice.195), channel_id=1, source_target_pairs={{0,16},{4,20},{8,24},{12,28},{16,0},{20,4},{24,8},{28,12},{1,17},{... | collective-permute-start | bytes 675848 | tf_op jit(solution)/shard_map/ppermute | solution.py:233
  35.8 11.3 %copy-start.10 = (bf16[88,2304]{1,0:T(8,128)(2,1)}, bf16[88,2304]{1,0:T(8,128)(2,1)S(1)}, u32[]{:S(2)}) copy-start(bf16[88,2304]{1,0:T(8,128)(2,1)S(1)} %collective-permute-done.3) | copy-start | bytes 1216516
  35.8 7.8 %collective-permute-start.4 = (bf16[88,1152]{1,0:T(8,128)(2,1)S(1)}, bf16[88,1152]{1,0:T(8,128)(2,1)S(1)}, u32[]{:S(2)}, u32[]{:S(2)}) collective-permute-start(bf16[88,1152]{1,0:T(8,128)(2,1)S(1)} %slice.185), channel_id=1, source_target_pairs={{0,8},{4,12},{8,0},{12,4},{16,24},{20,28},{24,16},{28,20},{1,9},{5... | collective-permute-start | bytes 608264 | tf_op jit(solution)/shard_map/ppermute | solution.py:238
  38.4 7.2 %copy-start.9 = (bf16[88,2304]{1,0:T(8,128)(2,1)S(1)}, bf16[88,2304]{1,0:T(8,128)(2,1)}, u32[]{:S(2)}) copy-start(bf16[88,2304]{1,0:T(8,128)(2,1)} %copy-done.8) | copy-start | bytes 1216516
  39.8 8.9 %copy-start.20 = (s32[8,1,2]{0,2,1:T(2,128)S(1)}, s32[8,1,2]{0,2,1:T(2,128)}, u32[]{:S(2)}) copy-start(s32[8,1,2]{0,2,1:T(2,128)} %param.11) | copy-start | bytes 196
  39.8 8.9 %copy-start.18 = (s32[8,1,2,2]{0,3,2,1:T(2,128)S(1)}, s32[8,1,2,2]{0,3,2,1:T(2,128)}, u32[]{:S(2)}) copy-start(s32[8,1,2,2]{0,3,2,1:T(2,128)} %param.10) | copy-start | bytes 388
  43.6 4.9 %copy-start.21 = (bf16[80,1408]{1,0:T(8,128)(2,1)}, bf16[80,1408]{1,0:T(8,128)(2,1)S(1)}, u32[]{:S(2)}) copy-start(bf16[80,1408]{1,0:T(8,128)(2,1)S(1)} %collective-permute-done.8) | copy-start | bytes 675844
  43.6 4.8 %copy-start.12 = (bf16[88,1920]{1,0:T(8,128)(2,1)}, bf16[88,1920]{1,0:T(8,128)(2,1)S(1)}, u32[]{:S(2)}) copy-start(bf16[88,1920]{1,0:T(8,128)(2,1)S(1)} %collective-permute-done.7) | copy-start | bytes 1013764
  46.3 2.2 %copy-start.6 = (bf16[528,1152]{1,0:T(8,128)(2,1)}, bf16[528,1152]{1,0:T(8,128)(2,1)S(1)}, u32[]{:S(2)}) copy-start(bf16[528,1152]{1,0:T(8,128)(2,1)S(1)} %get-tuple-element.187) | copy-start | bytes 3649540
  46.3 6.6 %slice-start = ((bf16[88,2304]{1,0:T(8,128)(2,1)}), bf16[88,1152]{1,0:T(8,128)(2,1)S(1)}, s32[]{:S(2)}) async-start(bf16[88,2304]{1,0:T(8,128)(2,1)} %copy-done.8), calls=%async_computation | async-start | bytes 405504 | tf_op jit(solution)/shard_map/slice | solution.py:319
  48.5 11.0 %collective-permute-start.9 = (bf16[528,1152]{1,0:T(8,128)(2,1)}, bf16[528,1152]{1,0:T(8,128)(2,1)}, u32[]{:S(2)}, u32[]{:S(2)}) collective-permute-start(bf16[528,1152]{1,0:T(8,128)(2,1)} %constant_dynamic-update-slice_fusion.2), channel_id=1, source_target_pairs={{0,4},{4,0},{8,12},{12,8},{16,20},{20,16},{24,28},{28,24},{1,5},{5... | collective-permute-start | bytes 3649544 | tf_op jit(solution)/shard_map/ppermute | solution.py:238
  48.8 10.6 %collective-permute-start.10 = (bf16[88,1920]{1,0:T(8,128)(2,1)}, bf16[88,1920]{1,0:T(8,128)(2,1)S(1)}, u32[]{:S(2)}, u32[]{:S(2)}) collective-permute-start(bf16[88,1920]{1,0:T(8,128)(2,1)} %copy-done.14), channel_id=1, source_target_pairs={{0,3},{1,0},{2,1},{3,2},{4,7},{5,4},{6,5},{7,6},{8,11},{9,8},{10,9... | collective-permute-start | bytes 1013768 | tf_op jit(solution)/shard_map/ppermute | solution.py:233
  51.9 2.8 %copy-start.13 = (bf16[88,1920]{1,0:T(8,128)(2,1)S(1)}, bf16[88,1920]{1,0:T(8,128)(2,1)}, u32[]{:S(2)}) copy-start(bf16[88,1920]{1,0:T(8,128)(2,1)} %copy-done.12) | copy-start | bytes 1013764
  51.9 7.6 %copy-start.4 = (bf16[352,1152]{1,0:T(8,128)(2,1)S(1)}, bf16[352,1152]{1,0:T(8,128)(2,1)}, u32[]{:S(2)}) copy-start(bf16[352,1152]{1,0:T(8,128)(2,1)} %pad_maximum_fusion) | copy-start | bytes 2433028
  53.0 17.9 %collective-permute-start.11 = (bf16[264,1152]{1,0:T(8,128)(2,1)S(1)}, bf16[264,1152]{1,0:T(8,128)(2,1)S(1)}, u32[]{:S(2)}, u32[]{:S(2)}) collective-permute-start(bf16[264,1152]{1,0:T(8,128)(2,1)S(1)} %pad_maximum_fusion.3), channel_id=1, source_target_pairs={{0,8},{4,12},{8,0},{12,4},{16,24},{20,28},{24,16},{28,20},{1,9},{5... | collective-permute-start | bytes 1824776 | tf_op jit(solution)/shard_map/ppermute | solution.py:238
  53.1 14.3 %collective-permute-start.12 = (bf16[192,1408]{1,0:T(8,128)(2,1)S(1)}, bf16[192,1408]{1,0:T(8,128)(2,1)S(1)}, u32[]{:S(2)}, u32[]{:S(2)}) collective-permute-start(bf16[192,1408]{1,0:T(8,128)(2,1)S(1)} %slice.202), channel_id=1, source_target_pairs={{0,16},{4,20},{8,24},{12,28},{16,0},{20,4},{24,8},{28,12},{1,17},{... | collective-permute-start | bytes 1622024 | tf_op jit(solution)/shard_map/ppermute | solution.py:233
  54.7 16.2 %collective-permute-start.13 = (bf16[88,1920]{1,0:T(8,128)(2,1)S(1)}, bf16[88,1920]{1,0:T(8,128)(2,1)S(1)}, u32[]{:S(2)}, u32[]{:S(2)}) collective-permute-start(bf16[88,1920]{1,0:T(8,128)(2,1)S(1)} %copy-done.13), channel_id=1, source_target_pairs={{0,1},{1,2},{2,3},{3,0},{4,5},{5,6},{6,7},{7,4},{8,9},{9,10},{10,1... | collective-permute-start | bytes 1013768 | tf_op jit(solution)/shard_map/ppermute | solution.py:233
  62.5 5.0 %copy-start.2 = (bf16[1408,1408]{1,0:T(8,128)(2,1)S(1)}, bf16[1408,1408]{1,0:T(8,128)(2,1)}, u32[]{:S(2)}) copy-start(bf16[1408,1408]{1,0:T(8,128)(2,1)} %copy-done.1) | copy-start | bytes 11894788
  62.5 5.0 %copy-start.22 = (bf16[80,1408]{1,0:T(8,128)(2,1)S(1)}, bf16[80,1408]{1,0:T(8,128)(2,1)}, u32[]{:S(2)}) copy-start(bf16[80,1408]{1,0:T(8,128)(2,1)} %copy-done.21) | copy-start | bytes 675844
  67.4 3.4 %copy-start.7 = (bf16[528,1152]{1,0:T(8,128)(2,1)S(1)}, bf16[528,1152]{1,0:T(8,128)(2,1)}, u32[]{:S(2)}) copy-start(bf16[528,1152]{1,0:T(8,128)(2,1)} %copy-done.6) | copy-start | bytes 3649540
  67.4 3.5 %copy-start.11 = (bf16[88,2304]{1,0:T(8,128)(2,1)S(1)}, bf16[88,2304]{1,0:T(8,128)(2,1)}, u32[]{:S(2)}) copy-start(bf16[88,2304]{1,0:T(8,128)(2,1)} %copy-done.10) | copy-start | bytes 1216516
  71.0 3.7 %copy-start.3 = (bf16[352,1152]{1,0:T(8,128)(2,1)S(1)}, bf16[352,1152]{1,0:T(8,128)(2,1)}, u32[]{:S(2)}) copy-start(bf16[352,1152]{1,0:T(8,128)(2,1)} %pad_maximum_fusion.2) | copy-start | bytes 2433028
  71.0 12.5 %collective-permute-start.14 = (bf16[528,1152]{1,0:T(8,128)(2,1)S(1)}, bf16[528,1152]{1,0:T(8,128)(2,1)S(1)}, u32[]{:S(2)}, u32[]{:S(2)}) collective-permute-start(bf16[528,1152]{1,0:T(8,128)(2,1)S(1)} %slice_dynamic-update-slice_fusion.1), channel_id=1, source_target_pairs={{0,4},{4,0},{8,12},{12,8},{16,20},{20,16},{24,28},{28,24},{1,5},{5... | collective-permute-start | bytes 3649544 | tf_op jit(solution)/shard_map/ppermute | solution.py:238
  71.2 3.5 %copy-start.5 = (bf16[352,768]{1,0:T(8,128)(2,1)S(1)}, bf16[352,768]{1,0:T(8,128)(2,1)}, u32[]{:S(2)}) copy-start(bf16[352,768]{1,0:T(8,128)(2,1)} %pad_maximum_fusion.4) | copy-start | bytes 1622020
  71.2 12.2 %collective-permute-start.15 = (bf16[176,1152]{1,0:T(8,128)(2,1)S(1)}, bf16[176,1152]{1,0:T(8,128)(2,1)S(1)}, u32[]{:S(2)}, u32[]{:S(2)}) collective-permute-start(bf16[176,1152]{1,0:T(8,128)(2,1)S(1)} %pad_maximum_fusion.6), channel_id=1, source_target_pairs={{0,8},{4,12},{8,0},{12,4},{16,24},{20,28},{24,16},{28,20},{1,9},{5... | collective-permute-start | bytes 1216520 | tf_op jit(solution)/shard_map/ppermute | solution.py:238
  73.1 8.7 %collective-permute-start.16 = (bf16[176,768]{1,0:T(8,128)(2,1)S(1)}, bf16[176,768]{1,0:T(8,128)(2,1)S(1)}, u32[]{:S(2)}, u32[]{:S(2)}) collective-permute-start(bf16[176,768]{1,0:T(8,128)(2,1)S(1)} %pad_maximum_fusion.8), channel_id=1, source_target_pairs={{0,16},{4,20},{8,24},{12,28},{16,0},{20,4},{24,8},{28,12},{1,17},{... | collective-permute-start | bytes 811016 | tf_op jit(solution)/shard_map/ppermute | solution.py:238
  79.1 9.4 %collective-permute-start.17 = (bf16[88,1152]{1,0:T(8,128)(2,1)S(1)}, bf16[88,1152]{1,0:T(8,128)(2,1)S(1)}, u32[]{:S(2)}, u32[]{:S(2)}) collective-permute-start(bf16[88,1152]{1,0:T(8,128)(2,1)S(1)} %slice.212), channel_id=1, source_target_pairs={{0,8},{4,12},{8,0},{12,4},{16,24},{20,28},{24,16},{28,20},{1,9},{5... | collective-permute-start | bytes 608264 | tf_op jit(solution)/shard_map/ppermute | solution.py:238
  79.4 9.0 %collective-permute-start.18 = (bf16[88,768]{1,0:T(8,128)(2,1)S(1)}, bf16[88,768]{1,0:T(8,128)(2,1)S(1)}, u32[]{:S(2)}, u32[]{:S(2)}) collective-permute-start(bf16[88,768]{1,0:T(8,128)(2,1)S(1)} %slice.213), channel_id=1, source_target_pairs={{0,16},{4,20},{8,24},{12,28},{16,0},{20,4},{24,8},{28,12},{1,17},{... | collective-permute-start | bytes 405512 | tf_op jit(solution)/shard_map/ppermute | solution.py:238
  88.8 5.2 %collective-permute-start.19 = (bf16[528,1152]{1,0:T(8,128)(2,1)S(1)}, bf16[528,1152]{1,0:T(8,128)(2,1)S(1)}, u32[]{:S(2)}, u32[]{:S(2)}) collective-permute-start(bf16[528,1152]{1,0:T(8,128)(2,1)S(1)} %get-tuple-element.205), channel_id=1, source_target_pairs={{0,4},{4,0},{8,12},{12,8},{16,20},{20,16},{24,28},{28,24},{1,5},{5... | collective-permute-start | bytes 3649544 | tf_op jit(solution)/shard_map/ppermute | solution.py:238
  89.0 4.9 %collective-permute-start.20 = (bf16[528,768]{1,0:T(8,128)(2,1)S(1)}, bf16[528,768]{1,0:T(8,128)(2,1)S(1)}, u32[]{:S(2)}, u32[]{:S(2)}) collective-permute-start(bf16[528,768]{1,0:T(8,128)(2,1)S(1)} %get-tuple-element.207), channel_id=1, source_target_pairs={{0,4},{4,0},{8,12},{12,8},{16,20},{20,16},{24,28},{28,24},{1,5},{5... | collective-permute-start | bytes 2433032 | tf_op jit(solution)/shard_map/ppermute | solution.py:238

commit v5 on v4

--- a/solution.py
+++ b/solution.py
@@ -291,7 +291,7 @@
     near_first = balance[rank, 0, 0] == 0
     low, high = tokens[: rows // 2], tokens[rows // 2 :]
     near_out, far_out = jnp.where(near_first, low, high), jnp.where(near_first, high, low)
-    cut = (rows // 5 // 16 * 16, rows * 2 // 7 // 16 * 16)
+    cut = (rows // 5 // 16 * 16, rows * 2 // 7 // 16 * 16, rows * 7 // 20 // 16 * 16)
     far_1 = shifted(far_out[: cut[0]], "dp", ranks // 2)
     near_in = shifted(near_out, "dp", 1)
     pcd = payload(w, 2, 3)
@@ -320,19 +320,20 @@
     own_d = of_chunk(w, *BOUNDS[3])
 
     ay, ax, abp, abm, ab2, own_d, cdp, far_out, far_2 = fence(ay, ax, abp, abm, ab2, own_d, cdp, far_out, far_2)
-    far_3 = shifted(far_out[cut[1] :], "dp", ranks // 2)
+    far_3 = shifted(far_out[cut[1] : cut[2]], "dp", ranks // 2)
     cd2 = up(cdp)
     both_a = stacked(abp[:, :n_a], abm[:, :n_a], ax, ab2[:, :n_a], ay)
     ac = swapped(both_a, 1)
 
-    ac, both_a, own_a, near, cdm = fence(ac, both_a, own_a, near, cdm)
+    ac, both_a, own_a, near, far_3, far_out = fence(ac, both_a, own_a, near, far_3, far_out)
+    far_4 = shifted(far_out[cut[2] :], "dp", ranks // 2)
     wa = stacked(own_a, both_a, ac)
     out = attend(BOUNDS[:1], *heads[0], (0,), (near,), (wa,), info, carry, finished)
 
-    out, cdp, cdm, far_1, far_2, far_3 = fence(out, cdp, cdm, far_1, far_2, far_3)
+    out, cdp, cdm, far_1, far_2, far_3, far_4 = fence(out, cdp, cdm, far_1, far_2, far_3, far_4)
     dx_1 = across(3, cdp[:, n_c:], cdm[:, n_c:])
     cx_1 = across(2, cdp[:, :n_c], cdm[:, :n_c])
-    far = reordered(stacked(far_1, far_2, far_3), place)
+    far = reordered(stacked(far_1, far_2, far_3, far_4), place)
 
     bx, far, cd2 = fence(bx, far, cd2)
     dx_2 = across(3, cd2[:, n_c:])

time: 108 us -> 107 us (level)
  starting transfers between devices: 22.6 us -> 24.3 us
  waiting for transfers between devices: 22.4 us -> 21.1 us
    ppermute x10 -> x11, starting transfers between devices: 13.9 us -> 15.8 us  [shifted(): return lax.ppermute(x, axis, [(i, (i + by) % n) for i in range(n)])]
    ppermute x10 -> x11, waiting for transfers between devices: 18.9 us -> 17.6 us  [shifted(): return lax.ppermute(x, axis, [(i, (i + by) % n) for i in range(n)])]
    unnamed x69 -> x71, local copies, waits for them, and re-layouts: 6.81 us -> 6.81 us
  transfers between devices with their start and end apart: 21 -> 22, of which waited for: 9 -> 9; matrix products, arithmetic and copies ran while one was open for 23% -> 22% of each run, Pallas kernels for 16% -> 16%
where the time goes in v5:
time: 107 us
  Pallas kernels  30.2 us (28%)
  starting transfers between devices  24.3 us (23%)
  waiting for transfers between devices  21.1 us (20%)
  local copies, waits for them, and re-layouts  14.1 us (13%)
  other arithmetic  9.24 us (9%)
  matrix products  6.99 us (7%)
    pallas_call x5, Pallas kernels, attend(): pl.pallas_call(functools.partial(attend_kernel, spans, h0, h1, hd, bundle...  30.2 us
    ppermute x11, waiting for transfers between devices, shifted(): return lax.ppermute(x, axis, [(i, (i + by) % n) for i in range(n)])  17.6 us
    ppermute x11, starting transfers between devices, shifted(): return lax.ppermute(x, axis, [(i, (i + by) % n) for i in range(n)])  15.8 us
    ppermute x11, starting transfers between devices, swapped(): return lax.ppermute(x, 'dp', [(i, i ^ mask) for i in range(n)])  8.55 us
    dot_general x2, matrix products, reordered(): jnp.dot(x, place, preferred_element_type=jnp.float32).astype(jnp.bfloat16)  6.99 us
    unnamed x71, local copies, waits for them, and re-layouts  6.81 us
    select_n x1, other arithmetic, on_device(): jnp.where(near_first, high, low)  3.62 us
    ppermute x11, waiting for transfers between devices, swapped(): return lax.ppermute(x, 'dp', [(i, i ^ mask) for i in range(n)])  3.56 us
  transfers between devices with their start and end apart: 22, of which 9 were waited for; matrix products, arithmetic and copies ran while one was open for 22% of the time, Pallas kernels for 16%

profile of v5, /device:TPU:0, one launch (start us, length us, event | category | flops | bytes accessed | tf_op | source)
XLA Modules:
  0.0 106.8 jit_solution(9918590557777565024)
XLA Ops:
  0.0 1.1 %fusion.19 = (bf16[88,384]{1,0:T(8,128)(2,1)S(1)}, bf16[88,384]{1,0:T(8,128)(2,1)S(1)}, bf16[88,384]{1,0:T(8,128)(2,1)S(1)}, bf16[88,384]{1,0:T(8,128)(2,1)S(1)}...) fusion(bf16[352,4224]{1,0:T(8,128)(2,1)} %param.9, s32[]{:T(128)S(6)} %select_n.38, s32[]{:T(128)S(6)} %add.48, ...), kind=kLoop, calls=%fused_computation.89 | loop fusion | bytes 811032 | tf_op jit(solution)/shard_map/slice | solution.py:267
  1.2 3.1 %collective-permute-start.1 = (bf16[88,2304]{1,0:T(8,128)(2,1)S(1)}, bf16[88,2304]{1,0:T(8,128)(2,1)}, u32[]{:S(2)}, u32[]{:S(2)}) collective-permute-start(bf16[88,2304]{1,0:T(8,128)(2,1)S(1)} %constant_dynamic-update-slice_fusion), channel_id=1, source_target_pairs={{0,1},{1,2},{2,3},{3,0},{4,5},{5,6},{6,7},{7,4},{8,9},{9,10},{10,1... | collective-permute-start | bytes 1216520 | tf_op jit(solution)/shard_map/ppermute | solution.py:233
  4.3 2.1 %collective-permute-start.2 = (bf16[88,2304]{1,0:T(8,128)(2,1)S(1)}, bf16[88,2304]{1,0:T(8,128)(2,1)S(1)}, u32[]{:S(2)}, u32[]{:S(2)}) collective-permute-start(bf16[88,2304]{1,0:T(8,128)(2,1)S(1)} %constant_dynamic-update-slice_fusion), channel_id=1, source_target_pairs={{0,3},{1,0},{2,1},{3,2},{4,7},{5,4},{6,5},{7,6},{8,11},{9,8},{10,9... | collective-permute-start | bytes 1216520 | tf_op jit(solution)/shard_map/ppermute | solution.py:233
  6.4 0.6 fusion.20
  7.0 3.6 %broadcast_select_fusion = (bf16[448,1408]{1,0:T(8,128)(2,1)S(1)}, bf16[448,1408]{1,0:T(8,128)(2,1)}) fusion(pred[]{:T(512)} %bitcast, bf16[896,1408]{1,0:T(8,128)(2,1)} %param.8), kind=kLoop, calls=%fused_computation.11 | loop fusion | flops 1261568 | bytes 5046273 | tf_op jit(solution)/shard_map/jit(_where)/select_n | solution.py:293
  10.6 0.8 slice.224
  11.5 1.7 %collective-permute-start.6 = (bf16[176,1408]{1,0:T(8,128)(2,1)}, bf16[176,1408]{1,0:T(8,128)(2,1)}, u32[]{:S(2)}, u32[]{:S(2)}) collective-permute-start(bf16[176,1408]{1,0:T(8,128)(2,1)} %slice.224), channel_id=1, source_target_pairs={{0,16},{4,20},{8,24},{12,28},{16,0},{20,4},{24,8},{28,12},{1,17},{... | collective-permute-start | bytes 1486856 | tf_op jit(solution)/shard_map/ppermute | solution.py:233
  13.3 1.7 %fusion = bf16[1408,1408]{1,0:T(8,128)(2,1)S(1)} fusion(s32[1408]{0:T(1024)S(1)} %pad_add_fusion), kind=kLoop, calls=%fused_computation.1 | loop fusion | flops 3964928 | bytes 3970560 | tf_op jit(solution)/shard_map/convert_element_type | solution.py:264
  15.2 1.4 %collective-permute-done.1 = bf16[88,2304]{1,0:T(8,128)(2,1)} collective-permute-done((bf16[88,2304]{1,0:T(8,128)(2,1)S(1)}, bf16[88,2304]{1,0:T(8,128)(2,1)}, u32[]{:S(2)}, u32[]{:S(2)}) %collective-permute-start.1) | collective-permute-done | bytes 405536 | tf_op jit(solution)/shard_map/ppermute | solution.py:233
  16.8 1.0 pad_maximum_fusion
  17.8 6.2 %collective-permute-done.2 = bf16[88,2304]{1,0:T(8,128)(2,1)S(1)} collective-permute-done((bf16[88,2304]{1,0:T(8,128)(2,1)S(1)}, bf16[88,2304]{1,0:T(8,128)(2,1)S(1)}, u32[]{:S(2)}, u32[]{:S(2)}) %collective-permute-start.2) | collective-permute-done | bytes 405536 | tf_op jit(solution)/shard_map/ppermute | solution.py:233
  24.1 1.1 %slice.189 = bf16[88,1152]{1,0:T(8,128)(2,1)S(1)} slice(bf16[88,2304]{1,0:T(8,128)(2,1)} %collective-permute-done.1), slice={[0:88], [0:1152]} | slice | bytes 405504 | tf_op jit(solution)/shard_map/slice | solution.py:306
  25.2 1.8 %collective-permute-start.5 = (bf16[176,1152]{1,0:T(8,128)(2,1)S(1)}, bf16[176,1152]{1,0:T(8,128)(2,1)S(1)}, u32[]{:S(2)}, u32[]{:S(2)}) collective-permute-start(bf16[176,1152]{1,0:T(8,128)(2,1)S(1)} %pad_maximum_fusion.5), channel_id=1, source_target_pairs={{0,8},{4,12},{8,0},{12,4},{16,24},{20,28},{24,16},{28,20},{1,9},{5... | collective-permute-start | bytes 1216520 | tf_op jit(solution)/shard_map/ppermute | solution.py:238
  27.0 1.7 %collective-permute-start.7 = (bf16[88,1920]{1,0:T(8,128)(2,1)S(1)}, bf16[88,1920]{1,0:T(8,128)(2,1)S(1)}, u32[]{:S(2)}, u32[]{:S(2)}) collective-permute-start(bf16[88,1920]{1,0:T(8,128)(2,1)S(1)} %pad_maximum_fusion.7), channel_id=1, source_target_pairs={{0,1},{1,2},{2,3},{3,0},{4,5},{5,6},{6,7},{7,4},{8,9},{9,10},{10,1... | collective-permute-start | bytes 1013768 | tf_op jit(solution)/shard_map/ppermute | solution.py:233
  28.9 1.6 %collective-permute-start.8 = (bf16[80,1408]{1,0:T(8,128)(2,1)S(1)}, bf16[80,1408]{1,0:T(8,128)(2,1)S(1)}, u32[]{:S(2)}, u32[]{:S(2)}) collective-permute-start(bf16[80,1408]{1,0:T(8,128)(2,1)S(1)} %slice.198), channel_id=1, source_target_pairs={{0,16},{4,20},{8,24},{12,28},{16,0},{20,4},{24,8},{28,12},{1,17},{... | collective-permute-start | bytes 675848 | tf_op jit(solution)/shard_map/ppermute | solution.py:233
  30.5 3.6 %convolution_convert_fusion.1.refs_0_ = bf16[448,1408]{1,0:T(8,128)(2,1)S(1)} fusion(bf16[448,1408]{1,0:T(8,128)(2,1)} %collective-permute-done, bf16[1408,1408]{1,0:T(8,128)(2,1)S(1)} %fusion), kind=kOutput, calls=%fused_computation.3 | convolution fusion | flops 1776918528 | bytes 6488064 | tf_op jit(solution)/shard_map/dot_general | solution.py:228
  34.1 1.7 %collective-permute-done.3 = bf16[88,2304]{1,0:T(8,128)(2,1)S(1)} collective-permute-done((bf16[88,2304]{1,0:T(8,128)(2,1)}, bf16[88,2304]{1,0:T(8,128)(2,1)S(1)}, u32[]{:S(2)}, u32[]{:S(2)}) %collective-permute-start.3) | collective-permute-done | bytes 405536 | tf_op jit(solution)/shard_map/ppermute | solution.py:233
  35.8 1.6 %collective-permute-start.4 = (bf16[88,1152]{1,0:T(8,128)(2,1)S(1)}, bf16[88,1152]{1,0:T(8,128)(2,1)S(1)}, u32[]{:S(2)}, u32[]{:S(2)}) collective-permute-start(bf16[88,1152]{1,0:T(8,128)(2,1)S(1)} %slice.188), channel_id=1, source_target_pairs={{0,8},{4,12},{8,0},{12,4},{16,24},{20,28},{24,16},{28,20},{1,9},{5... | collective-permute-start | bytes 608264 | tf_op jit(solution)/shard_map/ppermute | solution.py:238
  37.4 1.0 pad_maximum_fusion.2
  38.4 0.5 collective-permute-done.6
  38.9 0.8 pad_maximum_fusion.4
  39.8 3.8 %collective-permute-done.8 = bf16[80,1408]{1,0:T(8,128)(2,1)S(1)} collective-permute-done((bf16[80,1408]{1,0:T(8,128)(2,1)S(1)}, bf16[80,1408]{1,0:T(8,128)(2,1)S(1)}, u32[]{:S(2)}, u32[]{:S(2)}) %collective-permute-start.8) | collective-permute-done | bytes 225312 | tf_op jit(solution)/shard_map/ppermute | solution.py:233
  43.6 1.9 %slice_dynamic-update-slice_fusion.4 = (bf16[528,1152]{1,0:T(8,128)(2,1)S(1)}, bf16[528,1152]{1,0:T(8,128)(2,1)}) fusion(bf16[88,2304]{1,0:T(8,128)(2,1)} %collective-permute-done.1), kind=kLoop, calls=%fused_computation.29 | loop fusion | bytes 811008
  45.6 0.7 slice_dynamic-update-slice_fusion.3
  46.3 0.8 constant_dynamic-update-slice_fusion.3
  47.1 0.7 slice_dynamic-update-slice_fusion.5
  47.8 0.7 constant_dynamic-update-slice_fusion.2
  48.9 1.1 slice.203
  50.0 1.8 %collective-permute-start.10 = (bf16[48,1408]{1,0:T(8,128)(2,1)S(1)}, bf16[48,1408]{1,0:T(8,128)(2,1)S(1)}, u32[]{:S(2)}, u32[]{:S(2)}) collective-permute-start(bf16[48,1408]{1,0:T(8,128)(2,1)S(1)} %slice.202), channel_id=1, source_target_pairs={{0,16},{4,20},{8,24},{12,28},{16,0},{20,4},{24,8},{28,12},{1,17},{... | collective-permute-start | bytes 405512 | tf_op jit(solution)/shard_map/ppermute | solution.py:233
  51.9 1.9 %collective-permute-start.12 = (bf16[88,1920]{1,0:T(8,128)(2,1)S(1)}, bf16[88,1920]{1,0:T(8,128)(2,1)S(1)}, u32[]{:S(2)}, u32[]{:S(2)}) collective-permute-start(bf16[88,1920]{1,0:T(8,128)(2,1)S(1)} %copy-done.15), channel_id=1, source_target_pairs={{0,3},{1,0},{2,1},{3,2},{4,7},{5,4},{6,5},{7,6},{8,11},{9,8},{10,9... | collective-permute-start | bytes 1013768 | tf_op jit(solution)/shard_map/ppermute | solution.py:233
  54.0 1.9 %collective-permute-done.10 = bf16[48,1408]{1,0:T(8,128)(2,1)S(1)} collective-permute-done((bf16[48,1408]{1,0:T(8,128)(2,1)S(1)}, bf16[48,1408]{1,0:T(8,128)(2,1)S(1)}, u32[]{:S(2)}, u32[]{:S(2)}) %collective-permute-start.10) | collective-permute-done | bytes 135200 | tf_op jit(solution)/shard_map/ppermute | solution.py:233
  56.1 1.8 %collective-permute-start.13 = (bf16[144,1408]{1,0:T(8,128)(2,1)S(1)}, bf16[144,1408]{1,0:T(8,128)(2,1)S(1)}, u32[]{:S(2)}, u32[]{:S(2)}) collective-permute-start(bf16[144,1408]{1,0:T(8,128)(2,1)S(1)} %slice.206), channel_id=1, source_target_pairs={{0,16},{4,20},{8,24},{12,28},{16,0},{20,4},{24,8},{28,12},{1,17},{... | collective-permute-start | bytes 1216520 | tf_op jit(solution)/shard_map/ppermute | solution.py:233
  57.8 1.5 %constant_dynamic-update-slice_fusion.5 = bf16[1408,1152]{1,0:T(8,128)(2,1)S(1)} fusion(bf16[1408,1152]{1,0:T(8,128)(2,1)S(1)} %constant_dynamic-update-slice_fusion.6, bf16[528,1152]{1,0:T(8,128)(2,1)} %constant_dynamic-update-slice_fusion.2), kind=kLoop, calls=%fused_computation.51 | loop fusion | bytes 2433024
  59.3 1.5 %constant_dynamic-update-slice_fusion.4.refs_1_ = bf16[1408,1152]{1,0:T(8,128)(2,1)S(1)} fusion(bf16[1408,1152]{1,0:T(8,128)(2,1)S(1)} %constant_dynamic-update-slice_fusion.5, bf16[528,1152]{1,0:T(8,128)(2,1)} %collective-permute-done.9), kind=kLoop, calls=%fused_computation.50 | loop fusion | bytes 2433024 | tf_op jit(solution)/shard_map/concatenate | solution.py:246
  60.8 4.2 %attend_0_0.1 = (bf16[448,256]{1,0:T(8,128)(2,1)S(1)}, bf16[448,384]{1,0:T(8,128)(2,1)S(1)}, bf16[448,128]{1,0:T(8,128)(2,1)S(1)}) custom-call(bf16[448,1408]{1,0:T(8,128)(2,1)S(1)} %convolution_convert_fusion.1.refs_0_, bf16[1408,1152]{1,0:T(8,128)(2,1)S(1)} %constant_dynamic-update-slice_fusion.4.refs_1_, s32[8,1,2,2]{3,2,1,0:T(2,128)S(1)} %copy.9.refs_2_.refs_4_, ...), custom_call_target="tpu_custom_call" | custom-call | tf_op jit(solution)/shard_map/attend_0_0/pallas_call | solution.py:193
  65.0 2.0 %collective-permute-done.13 = bf16[144,1408]{1,0:T(8,128)(2,1)S(1)} collective-permute-done((bf16[144,1408]{1,0:T(8,128)(2,1)S(1)}, bf16[144,1408]{1,0:T(8,128)(2,1)S(1)}, u32[]{:S(2)}, u32[]{:S(2)}) %collective-permute-start.13) | collective-permute-done | bytes 405536 | tf_op jit(solution)/shard_map/ppermute | solution.py:233
  67.0 3.4 %convolution_convert_fusion.refs_0_.refs_1_ = bf16[448,1408]{1,0:T(8,128)(2,1)S(1)} fusion(bf16[1408,1408]{1,0:T(8,128)(2,1)S(1)} %copy-done.2, bf16[144,1408]{1,0:T(8,128)(2,1)S(1)} %collective-permute-done.13, bf16[48,1408]{1,0:T(8,128)(2,1)S(1)} %collective-permute-done.10, bf16[80,1408]{1,0:T(8,128)(2,1)S(1)} %copy-done.23, ...), kind=kOutput, calls=%fused_computation.2 | convolution fusion | flops 1781964800 | bytes 6488064 | tf_op jit(solution)/shard_map/dot_general | solution.py:228
  70.8 0.7 collective-permute-start.16
  71.5 1.2 %collective-permute-start.17 = (bf16[176,768]{1,0:T(8,128)(2,1)S(1)}, bf16[176,768]{1,0:T(8,128)(2,1)S(1)}, u32[]{:S(2)}, u32[]{:S(2)}) collective-permute-start(bf16[176,768]{1,0:T(8,128)(2,1)S(1)} %pad_maximum_fusion.8), channel_id=1, source_target_pairs={{0,16},{4,20},{8,24},{12,28},{16,0},{20,4},{24,8},{28,12},{1,17},{... | collective-permute-start | bytes 811016 | tf_op jit(solution)/shard_map/ppermute | solution.py:238
  72.8 4.3 %attend_0_1.1 = (bf16[448,256]{1,0:T(8,128)(2,1)S(1)}, bf16[448,384]{1,0:T(8,128)(2,1)S(1)}, bf16[448,128]{1,0:T(8,128)(2,1)S(1)}) custom-call(bf16[448,1408]{1,0:T(8,128)(2,1)S(1)} %convolution_convert_fusion.refs_0_.refs_1_, bf16[1408,1152]{1,0:T(8,128)(2,1)S(1)} %constant_dynamic-update-slice_fusion.4.refs_1_, s32[8,1,2,2]{3,2,1,0:T(2,128)S(1)} %copy.9.refs_2_.refs_4_, ...), custom_call_target="tpu_custom_call" | custom-call | tf_op jit(solution)/shard_map/attend_0_1/pallas_call | solution.py:193
  77.1 2.1 %collective-permute-start.18 = (bf16[88,1152]{1,0:T(8,128)(2,1)S(1)}, bf16[88,1152]{1,0:T(8,128)(2,1)S(1)}, u32[]{:S(2)}, u32[]{:S(2)}) collective-permute-start(bf16[88,1152]{1,0:T(8,128)(2,1)S(1)} %slice.216), channel_id=1, source_target_pairs={{0,8},{4,12},{8,0},{12,4},{16,24},{20,28},{24,16},{28,20},{1,9},{5... | collective-permute-start | bytes 608264 | tf_op jit(solution)/shard_map/ppermute | solution.py:238
  79.1 0.3 collective-permute-start.19
  79.5 0.7 collective-permute-done.17
  80.1 2.9 %collective-permute-done.16 = bf16[176,1152]{1,0:T(8,128)(2,1)S(1)} collective-permute-done((bf16[176,1152]{1,0:T(8,128)(2,1)S(1)}, bf16[176,1152]{1,0:T(8,128)(2,1)S(1)}, u32[]{:S(2)}, u32[]{:S(2)}) %collective-permute-start.16) | collective-permute-done | bytes 405536 | tf_op jit(solution)/shard_map/ppermute | solution.py:238
  83.5 4.5 %attend_3_0.1 = (bf16[448,384]{1,0:T(8,128)(2,1)S(1)}, bf16[448,384]{1,0:T(8,128)(2,1)S(1)}, bf16[448,128]{1,0:T(8,128)(2,1)S(1)}) custom-call(bf16[448,1408]{1,0:T(8,128)(2,1)S(1)} %convolution_convert_fusion.1.refs_0_, bf16[1408,1152]{1,0:T(8,128)(2,1)S(1)} %constant_dynamic-update-slice_fusion.7.refs_1_, s32[8,1,2,2]{3,2,1,0:T(2,128)S(1)} %copy.9.refs_2_.refs_4_, ...), custom_call_target="tpu_custom_call" | custom-call | tf_op jit(solution)/shard_map/attend_3_0/pallas_call | solution.py:193
  88.5 0.6 collective-permute-start.21
  89.1 4.3 %attend_3_1.1 = (bf16[448,384]{1,0:T(8,128)(2,1)S(1)}, bf16[448,384]{1,0:T(8,128)(2,1)S(1)}, bf16[448,128]{1,0:T(8,128)(2,1)S(1)}) custom-call(bf16[448,1408]{1,0:T(8,128)(2,1)S(1)} %convolution_convert_fusion.refs_0_.refs_1_, bf16[1408,1152]{1,0:T(8,128)(2,1)S(1)} %constant_dynamic-update-slice_fusion.7.refs_1_, s32[8,1,2,2]{3,2,1,0:T(2,128)S(1)} %copy.9.refs_2_.refs_4_, ...), custom_call_target="tpu_custom_call" | custom-call | tf_op jit(solution)/shard_map/attend_3_1/pallas_call | solution.py:193
  93.7 12.9 %attend_6_0.1 = bf16[896,1408]{1,0:T(8,128)(2,1)} custom-call(bf16[448,1408]{1,0:T(8,128)(2,1)S(1)} %convolution_convert_fusion.1.refs_0_, bf16[448,1408]{1,0:T(8,128)(2,1)S(1)} %convolution_convert_fusion.refs_0_.refs_1_, bf16[1408,1152]{1,0:T(8,128)(2,1)S(1)} %constant_dynamic-update-slice_fusion.12.refs_2_, ...), custom_call_target="tpu_custom_call" | custom-call | tf_op jit(solution)/shard_map/attend_6_0/pallas_call | solution.py:193
  (127 shorter events, 3.4 us)
Async XLA Ops:
  0.0 6.4 %copy-start.20 = (s32[8,1,2]{0,2,1:T(2,128)S(1)}, s32[8,1,2]{0,2,1:T(2,128)}, u32[]{:S(2)}) copy-start(s32[8,1,2]{0,2,1:T(2,128)} %param.11) | copy-start | bytes 196
  1.2 15.5 %collective-permute-start.1 = (bf16[88,2304]{1,0:T(8,128)(2,1)S(1)}, bf16[88,2304]{1,0:T(8,128)(2,1)}, u32[]{:S(2)}, u32[]{:S(2)}) collective-permute-start(bf16[88,2304]{1,0:T(8,128)(2,1)S(1)} %constant_dynamic-update-slice_fusion), channel_id=1, source_target_pairs={{0,1},{1,2},{2,3},{3,0},{4,5},{5,6},{6,7},{7,4},{8,9},{9,10},{10,1... | collective-permute-start | bytes 1216520 | tf_op jit(solution)/shard_map/ppermute | solution.py:233
  4.3 19.7 %collective-permute-start.2 = (bf16[88,2304]{1,0:T(8,128)(2,1)S(1)}, bf16[88,2304]{1,0:T(8,128)(2,1)S(1)}, u32[]{:S(2)}, u32[]{:S(2)}) collective-permute-start(bf16[88,2304]{1,0:T(8,128)(2,1)S(1)} %constant_dynamic-update-slice_fusion), channel_id=1, source_target_pairs={{0,3},{1,0},{2,1},{3,2},{4,7},{5,4},{6,5},{7,6},{8,11},{9,8},{10,9... | collective-permute-start | bytes 1216520 | tf_op jit(solution)/shard_map/ppermute | solution.py:233
  7.0 6.1 %copy-start.16 = (s32[1056]{0:T(1024)S(1)}, s32[1056]{0:T(1024)}, u32[]{:S(2)}) copy-start(s32[1056]{0:T(1024)} %constant.67.clone) | copy-start | bytes 12676
  7.0 6.1 %copy-start.17 = (s32[1056]{0:T(1024)S(1)}, s32[1056]{0:T(1024)}, u32[]{:S(2)}) copy-start(s32[1056]{0:T(1024)} %constant.66.clone) | copy-start | bytes 12676
  7.0 6.1 %copy-start.18 = (s32[1056]{0:T(1024)S(1)}, s32[1056]{0:T(1024)}, u32[]{:S(2)}) copy-start(s32[1056]{0:T(1024)} %constant.70) | copy-start | bytes 12676
  10.6 18.3 %collective-permute-start = (bf16[448,1408]{1,0:T(8,128)(2,1)}, bf16[448,1408]{1,0:T(8,128)(2,1)}, u32[]{:S(2)}, u32[]{:S(2)}) collective-permute-start(bf16[448,1408]{1,0:T(8,128)(2,1)} %get-tuple-element.188), channel_id=1, source_target_pairs={{0,4},{4,8},{8,12},{12,16},{16,20},{20,24},{24,28},{28,0},{1,5},{5... | collective-permute-start | bytes 3784712 | tf_op jit(solution)/shard_map/ppermute | solution.py:233
  11.5 27.4 %collective-permute-start.6 = (bf16[176,1408]{1,0:T(8,128)(2,1)}, bf16[176,1408]{1,0:T(8,128)(2,1)}, u32[]{:S(2)}, u32[]{:S(2)}) collective-permute-start(bf16[176,1408]{1,0:T(8,128)(2,1)} %slice.224), channel_id=1, source_target_pairs={{0,16},{4,20},{8,24},{12,28},{16,0},{20,4},{24,8},{28,12},{1,17},{... | collective-permute-start | bytes 1486856 | tf_op jit(solution)/shard_map/ppermute | solution.py:233
  13.3 1.8 %copy-start = (bf16[352,4224]{1,0:T(8,128)(2,1)S(1)}, bf16[352,4224]{1,0:T(8,128)(2,1)}, u32[]{:S(2)}) copy-start(bf16[352,4224]{1,0:T(8,128)(2,1)} %param.9) | copy-start | bytes 8921092
  15.1 15.4 %copy-start.1 = (bf16[1408,1408]{1,0:T(8,128)(2,1)}, bf16[1408,1408]{1,0:T(8,128)(2,1)S(1)}, u32[]{:S(2)}) copy-start(bf16[1408,1408]{1,0:T(8,128)(2,1)S(1)} %fusion) | copy-start | bytes 11894788
  15.2 11.8 %copy-start.14 = (bf16[88,1920]{1,0:T(8,128)(2,1)}, bf16[88,1920]{1,0:T(8,128)(2,1)S(1)}, u32[]{:S(2)}) copy-start(bf16[88,1920]{1,0:T(8,128)(2,1)S(1)} %pad_maximum_fusion.7) | copy-start | bytes 1013764
  16.7 19.1 %collective-permute-start.3 = (bf16[88,2304]{1,0:T(8,128)(2,1)}, bf16[88,2304]{1,0:T(8,128)(2,1)S(1)}, u32[]{:S(2)}, u32[]{:S(2)}) collective-permute-start(bf16[88,2304]{1,0:T(8,128)(2,1)} %collective-permute-done.1), channel_id=1, source_target_pairs={{0,1},{1,2},{2,3},{3,0},{4,5},{5,6},{6,7},{7,4},{8,9},{9,10},{10,1... | collective-permute-start | bytes 1216520 | tf_op jit(solution)/shard_map/ppermute | solution.py:233
  24.0 4.8 %copy-start.8 = (bf16[88,2304]{1,0:T(8,128)(2,1)}, bf16[88,2304]{1,0:T(8,128)(2,1)S(1)}, u32[]{:S(2)}) copy-start(bf16[88,2304]{1,0:T(8,128)(2,1)S(1)} %collective-permute-done.2) | copy-start | bytes 1216516
  25.2 13.7 %collective-permute-start.5 = (bf16[176,1152]{1,0:T(8,128)(2,1)S(1)}, bf16[176,1152]{1,0:T(8,128)(2,1)S(1)}, u32[]{:S(2)}, u32[]{:S(2)}) collective-permute-start(bf16[176,1152]{1,0:T(8,128)(2,1)S(1)} %pad_maximum_fusion.5), channel_id=1, source_target_pairs={{0,8},{4,12},{8,0},{12,4},{16,24},{20,28},{24,16},{28,20},{1,9},{5... | collective-permute-start | bytes 1216520 | tf_op jit(solution)/shard_map/ppermute | solution.py:238
  27.0 16.6 %collective-permute-start.7 = (bf16[88,1920]{1,0:T(8,128)(2,1)S(1)}, bf16[88,1920]{1,0:T(8,128)(2,1)S(1)}, u32[]{:S(2)}, u32[]{:S(2)}) collective-permute-start(bf16[88,1920]{1,0:T(8,128)(2,1)S(1)} %pad_maximum_fusion.7), channel_id=1, source_target_pairs={{0,1},{1,2},{2,3},{3,0},{4,5},{5,6},{6,7},{7,4},{8,9},{9,10},{10,1... | collective-permute-start | bytes 1013768 | tf_op jit(solution)/shard_map/ppermute | solution.py:233
  28.9 14.7 %collective-permute-start.8 = (bf16[80,1408]{1,0:T(8,128)(2,1)S(1)}, bf16[80,1408]{1,0:T(8,128)(2,1)S(1)}, u32[]{:S(2)}, u32[]{:S(2)}) collective-permute-start(bf16[80,1408]{1,0:T(8,128)(2,1)S(1)} %slice.198), channel_id=1, source_target_pairs={{0,16},{4,20},{8,24},{12,28},{16,0},{20,4},{24,8},{28,12},{1,17},{... | collective-permute-start | bytes 675848 | tf_op jit(solution)/shard_map/ppermute | solution.py:233
  35.8 11.3 %copy-start.10 = (bf16[88,2304]{1,0:T(8,128)(2,1)}, bf16[88,2304]{1,0:T(8,128)(2,1)S(1)}, u32[]{:S(2)}) copy-start(bf16[88,2304]{1,0:T(8,128)(2,1)S(1)} %collective-permute-done.3) | copy-start | bytes 1216516
  35.8 7.8 %collective-permute-start.4 = (bf16[88,1152]{1,0:T(8,128)(2,1)S(1)}, bf16[88,1152]{1,0:T(8,128)(2,1)S(1)}, u32[]{:S(2)}, u32[]{:S(2)}) collective-permute-start(bf16[88,1152]{1,0:T(8,128)(2,1)S(1)} %slice.188), channel_id=1, source_target_pairs={{0,8},{4,12},{8,0},{12,4},{16,24},{20,28},{24,16},{28,20},{1,9},{5... | collective-permute-start | bytes 608264 | tf_op jit(solution)/shard_map/ppermute | solution.py:238
  38.4 7.1 %copy-start.9 = (bf16[88,2304]{1,0:T(8,128)(2,1)S(1)}, bf16[88,2304]{1,0:T(8,128)(2,1)}, u32[]{:S(2)}) copy-start(bf16[88,2304]{1,0:T(8,128)(2,1)} %copy-done.8) | copy-start | bytes 1216516
  39.8 8.9 %copy-start.21 = (s32[8,1,2]{0,2,1:T(2,128)S(1)}, s32[8,1,2]{0,2,1:T(2,128)}, u32[]{:S(2)}) copy-start(s32[8,1,2]{0,2,1:T(2,128)} %param.11) | copy-start | bytes 196
  39.8 9.0 %copy-start.19 = (s32[8,1,2,2]{0,3,2,1:T(2,128)S(1)}, s32[8,1,2,2]{0,3,2,1:T(2,128)}, u32[]{:S(2)}) copy-start(s32[8,1,2,2]{0,3,2,1:T(2,128)} %param.10) | copy-start | bytes 388
  43.6 4.9 %copy-start.22 = (bf16[80,1408]{1,0:T(8,128)(2,1)}, bf16[80,1408]{1,0:T(8,128)(2,1)S(1)}, u32[]{:S(2)}) copy-start(bf16[80,1408]{1,0:T(8,128)(2,1)S(1)} %collective-permute-done.8) | copy-start | bytes 675844
  43.6 4.8 %copy-start.12 = (bf16[88,1920]{1,0:T(8,128)(2,1)}, bf16[88,1920]{1,0:T(8,128)(2,1)S(1)}, u32[]{:S(2)}) copy-start(bf16[88,1920]{1,0:T(8,128)(2,1)S(1)} %collective-permute-done.7) | copy-start | bytes 1013764
  46.3 2.2 %copy-start.6 = (bf16[528,1152]{1,0:T(8,128)(2,1)}, bf16[528,1152]{1,0:T(8,128)(2,1)S(1)}, u32[]{:S(2)}) copy-start(bf16[528,1152]{1,0:T(8,128)(2,1)S(1)} %get-tuple-element.191) | copy-start | bytes 3649540
  46.3 5.5 %slice-start = ((bf16[88,2304]{1,0:T(8,128)(2,1)}), bf16[88,1152]{1,0:T(8,128)(2,1)S(1)}, s32[]{:S(2)}) async-start(bf16[88,2304]{1,0:T(8,128)(2,1)} %copy-done.8), calls=%async_computation | async-start | bytes 405504 | tf_op jit(solution)/shard_map/slice | solution.py:319
  48.5 7.5 %collective-permute-start.9 = (bf16[528,1152]{1,0:T(8,128)(2,1)}, bf16[528,1152]{1,0:T(8,128)(2,1)}, u32[]{:S(2)}, u32[]{:S(2)}) collective-permute-start(bf16[528,1152]{1,0:T(8,128)(2,1)} %constant_dynamic-update-slice_fusion.2), channel_id=1, source_target_pairs={{0,4},{4,0},{8,12},{12,8},{16,20},{20,16},{24,28},{28,24},{1,5},{5... | collective-permute-start | bytes 3649544 | tf_op jit(solution)/shard_map/ppermute | solution.py:238
  48.8 3.0 %slice-start.1 = ((bf16[88,2304]{1,0:T(8,128)(2,1)}), bf16[88,1152]{1,0:T(8,128)(2,1)S(1)}, s32[]{:S(2)}) async-start(bf16[88,2304]{1,0:T(8,128)(2,1)} %copy-done.10), calls=%async_computation.1 | async-start | bytes 405504 | tf_op jit(solution)/shard_map/slice | solution.py:319
  48.8 3.1 %copy-start.15 = (bf16[88,1920]{1,0:T(8,128)(2,1)S(1)}, bf16[88,1920]{1,0:T(8,128)(2,1)}, u32[]{:S(2)}) copy-start(bf16[88,1920]{1,0:T(8,128)(2,1)} %copy-done.14) | copy-start | bytes 1013764
  48.8 5.0 %copy-start.13 = (bf16[88,1920]{1,0:T(8,128)(2,1)S(1)}, bf16[88,1920]{1,0:T(8,128)(2,1)}, u32[]{:S(2)}) copy-start(bf16[88,1920]{1,0:T(8,128)(2,1)} %copy-done.12) | copy-start | bytes 1013764
  48.8 7.1 %copy-start.4 = (bf16[352,1152]{1,0:T(8,128)(2,1)S(1)}, bf16[352,1152]{1,0:T(8,128)(2,1)}, u32[]{:S(2)}) copy-start(bf16[352,1152]{1,0:T(8,128)(2,1)} %pad_maximum_fusion) | copy-start | bytes 2433028
  50.0 6.0 %collective-permute-start.10 = (bf16[48,1408]{1,0:T(8,128)(2,1)S(1)}, bf16[48,1408]{1,0:T(8,128)(2,1)S(1)}, u32[]{:S(2)}, u32[]{:S(2)}) collective-permute-start(bf16[48,1408]{1,0:T(8,128)(2,1)S(1)} %slice.202), channel_id=1, source_target_pairs={{0,16},{4,20},{8,24},{12,28},{16,0},{20,4},{24,8},{28,12},{1,17},{... | collective-permute-start | bytes 405512 | tf_op jit(solution)/shard_map/ppermute | solution.py:233
  51.8 18.6 %collective-permute-start.11 = (bf16[264,1152]{1,0:T(8,128)(2,1)S(1)}, bf16[264,1152]{1,0:T(8,128)(2,1)S(1)}, u32[]{:S(2)}, u32[]{:S(2)}) collective-permute-start(bf16[264,1152]{1,0:T(8,128)(2,1)S(1)} %pad_maximum_fusion.3), channel_id=1, source_target_pairs={{0,8},{4,12},{8,0},{12,4},{16,24},{20,28},{24,16},{28,20},{1,9},{5... | collective-permute-start | bytes 1824776 | tf_op jit(solution)/shard_map/ppermute | solution.py:238
  51.9 13.1 %collective-permute-start.12 = (bf16[88,1920]{1,0:T(8,128)(2,1)S(1)}, bf16[88,1920]{1,0:T(8,128)(2,1)S(1)}, u32[]{:S(2)}, u32[]{:S(2)}) collective-permute-start(bf16[88,1920]{1,0:T(8,128)(2,1)S(1)} %copy-done.15), channel_id=1, source_target_pairs={{0,3},{1,0},{2,1},{3,2},{4,7},{5,4},{6,5},{7,6},{8,11},{9,8},{10,9... | collective-permute-start | bytes 1013768 | tf_op jit(solution)/shard_map/ppermute | solution.py:233
  53.8 16.6 %collective-permute-start.14 = (bf16[88,1920]{1,0:T(8,128)(2,1)S(1)}, bf16[88,1920]{1,0:T(8,128)(2,1)S(1)}, u32[]{:S(2)}, u32[]{:S(2)}) collective-permute-start(bf16[88,1920]{1,0:T(8,128)(2,1)S(1)} %copy-done.13), channel_id=1, source_target_pairs={{0,1},{1,2},{2,3},{3,0},{4,5},{5,6},{6,7},{7,4},{8,9},{9,10},{10,1... | collective-permute-start | bytes 1013768 | tf_op jit(solution)/shard_map/ppermute | solution.py:233
  56.1 10.9 %collective-permute-start.13 = (bf16[144,1408]{1,0:T(8,128)(2,1)S(1)}, bf16[144,1408]{1,0:T(8,128)(2,1)S(1)}, u32[]{:S(2)}, u32[]{:S(2)}) collective-permute-start(bf16[144,1408]{1,0:T(8,128)(2,1)S(1)} %slice.206), channel_id=1, source_target_pairs={{0,16},{4,20},{8,24},{12,28},{16,0},{20,4},{24,8},{28,12},{1,17},{... | collective-permute-start | bytes 1216520 | tf_op jit(solution)/shard_map/ppermute | solution.py:233
  60.7 6.2 %copy-start.2 = (bf16[1408,1408]{1,0:T(8,128)(2,1)S(1)}, bf16[1408,1408]{1,0:T(8,128)(2,1)}, u32[]{:S(2)}) copy-start(bf16[1408,1408]{1,0:T(8,128)(2,1)} %copy-done.1) | copy-start | bytes 11894788
  60.7 6.2 %copy-start.23 = (bf16[80,1408]{1,0:T(8,128)(2,1)S(1)}, bf16[80,1408]{1,0:T(8,128)(2,1)}, u32[]{:S(2)}) copy-start(bf16[80,1408]{1,0:T(8,128)(2,1)} %copy-done.22) | copy-start | bytes 675844
  67.0 3.5 %copy-start.7 = (bf16[528,1152]{1,0:T(8,128)(2,1)S(1)}, bf16[528,1152]{1,0:T(8,128)(2,1)}, u32[]{:S(2)}) copy-start(bf16[528,1152]{1,0:T(8,128)(2,1)} %copy-done.6) | copy-start | bytes 3649540
  67.0 3.5 %copy-start.11 = (bf16[88,2304]{1,0:T(8,128)(2,1)S(1)}, bf16[88,2304]{1,0:T(8,128)(2,1)}, u32[]{:S(2)}) copy-start(bf16[88,2304]{1,0:T(8,128)(2,1)} %copy-done.10) | copy-start | bytes 1216516
  70.5 2.1 %copy-start.3 = (bf16[352,1152]{1,0:T(8,128)(2,1)S(1)}, bf16[352,1152]{1,0:T(8,128)(2,1)}, u32[]{:S(2)}) copy-start(bf16[352,1152]{1,0:T(8,128)(2,1)} %pad_maximum_fusion.2) | copy-start | bytes 2433028
  70.6 12.5 %collective-permute-start.15 = (bf16[528,1152]{1,0:T(8,128)(2,1)S(1)}, bf16[528,1152]{1,0:T(8,128)(2,1)S(1)}, u32[]{:S(2)}, u32[]{:S(2)}) collective-permute-start(bf16[528,1152]{1,0:T(8,128)(2,1)S(1)} %slice_dynamic-update-slice_fusion.1), channel_id=1, source_target_pairs={{0,4},{4,0},{8,12},{12,8},{16,20},{20,16},{24,28},{28,24},{1,5},{5... | collective-permute-start | bytes 3649544 | tf_op jit(solution)/shard_map/ppermute | solution.py:238
  70.7 2.0 %copy-start.5 = (bf16[352,768]{1,0:T(8,128)(2,1)S(1)}, bf16[352,768]{1,0:T(8,128)(2,1)}, u32[]{:S(2)}) copy-start(bf16[352,768]{1,0:T(8,128)(2,1)} %pad_maximum_fusion.4) | copy-start | bytes 1622020
  70.8 12.2 %collective-permute-start.16 = (bf16[176,1152]{1,0:T(8,128)(2,1)S(1)}, bf16[176,1152]{1,0:T(8,128)(2,1)S(1)}, u32[]{:S(2)}, u32[]{:S(2)}) collective-permute-start(bf16[176,1152]{1,0:T(8,128)(2,1)S(1)} %pad_maximum_fusion.6), channel_id=1, source_target_pairs={{0,8},{4,12},{8,0},{12,4},{16,24},{20,28},{24,16},{28,20},{1,9},{5... | collective-permute-start | bytes 1216520 | tf_op jit(solution)/shard_map/ppermute | solution.py:238
  71.5 8.7 %collective-permute-start.17 = (bf16[176,768]{1,0:T(8,128)(2,1)S(1)}, bf16[176,768]{1,0:T(8,128)(2,1)S(1)}, u32[]{:S(2)}, u32[]{:S(2)}) collective-permute-start(bf16[176,768]{1,0:T(8,128)(2,1)S(1)} %pad_maximum_fusion.8), channel_id=1, source_target_pairs={{0,16},{4,20},{8,24},{12,28},{16,0},{20,4},{24,8},{28,12},{1,17},{... | collective-permute-start | bytes 811016 | tf_op jit(solution)/shard_map/ppermute | solution.py:238
  77.1 10.9 %collective-permute-start.18 = (bf16[88,1152]{1,0:T(8,128)(2,1)S(1)}, bf16[88,1152]{1,0:T(8,128)(2,1)S(1)}, u32[]{:S(2)}, u32[]{:S(2)}) collective-permute-start(bf16[88,1152]{1,0:T(8,128)(2,1)S(1)} %slice.216), channel_id=1, source_target_pairs={{0,8},{4,12},{8,0},{12,4},{16,24},{20,28},{24,16},{28,20},{1,9},{5... | collective-permute-start | bytes 608264 | tf_op jit(solution)/shard_map/ppermute | solution.py:238
  79.1 8.9 %collective-permute-start.19 = (bf16[88,768]{1,0:T(8,128)(2,1)S(1)}, bf16[88,768]{1,0:T(8,128)(2,1)S(1)}, u32[]{:S(2)}, u32[]{:S(2)}) collective-permute-start(bf16[88,768]{1,0:T(8,128)(2,1)S(1)} %slice.217), channel_id=1, source_target_pairs={{0,16},{4,20},{8,24},{12,28},{16,0},{20,4},{24,8},{28,12},{1,17},{... | collective-permute-start | bytes 405512 | tf_op jit(solution)/shard_map/ppermute | solution.py:238
  88.3 5.2 %collective-permute-start.20 = (bf16[528,1152]{1,0:T(8,128)(2,1)S(1)}, bf16[528,1152]{1,0:T(8,128)(2,1)S(1)}, u32[]{:S(2)}, u32[]{:S(2)}) collective-permute-start(bf16[528,1152]{1,0:T(8,128)(2,1)S(1)} %get-tuple-element.209), channel_id=1, source_target_pairs={{0,4},{4,0},{8,12},{12,8},{16,20},{20,16},{24,28},{28,24},{1,5},{5... | collective-permute-start | bytes 3649544 | tf_op jit(solution)/shard_map/ppermute | solution.py:238
  88.5 4.9 %collective-permute-start.21 = (bf16[528,768]{1,0:T(8,128)(2,1)S(1)}, bf16[528,768]{1,0:T(8,128)(2,1)S(1)}, u32[]{:S(2)}, u32[]{:S(2)}) collective-permute-start(bf16[528,768]{1,0:T(8,128)(2,1)S(1)} %get-tuple-element.211), channel_id=1, source_target_pairs={{0,4},{4,0},{8,12},{12,8},{16,20},{20,16},{24,28},{28,24},{1,5},{5... | collective-permute-start | bytes 2433032 | tf_op jit(solution)/shard_map/ppermute | solution.py:238
